TPU v7x, 32 devices: a whole 2x2x4 slice. The times are simulated.
32 devices in a mesh: tm: 8 (over z, x), head: 4 (over y, core).
Axes of the slice: x: 2, y: 2, z: 4, core: 2. Of those that a mesh axis runs over, the one named last changes fastest.
Arguments:
- query_in: bfloat16 [6272, 5120], P('tm', 'head'), may hold values from -6 to 6
- key_in: bfloat16 [6272, 5120], P('tm', 'head'), may hold values from -6 to 6
- value_in: bfloat16 [6272, 5120], P('tm', 'head'), may hold values from -6 to 6
- layer_grad: bfloat16 [6272, 5120], P('tm', 'head'), may hold values from -6 to 6
- out_weight: bfloat16 [5120, 5120], P('head'), may hold values from -0.078125 to 0.078125
- group_mask: int32 [8, 8], replicated, may hold values from 0 to 1, as said below
- first_group: int32 [1], replicated, may hold values from 0 to 7
Outputs:
- query_grad: bfloat16 [6272, 5120], P('tm', 'head')
- key_grad: bfloat16 [6272, 5120], P('tm', 'head')
- value_grad: bfloat16 [6272, 5120], P('tm', 'head')
Inputs may be any that keep to these rules, and one draw needn't show every extreme that they name: `group_mask`: 1 on the diagonal; each entry just below the diagonal is 1 or 0; every other entry is 0.
All inputs are finite; a program needn't handle non-finite values.
Results may differ from a plain program's by a relative error of at most 0.015.
Values may be sent and summed in bfloat16 or wider, within the bound.
No kernel may reach another device: no remote copies, remote signals or barrier semaphores. Data moves between devices by JAX's collectives and lax.ppermute only.
A program may use at most 256 MiB of HBM per device.

v0:
```python
import jax
import jax.numpy as jnp
from jax import lax
from jax.sharding import PartitionSpec as P

D_HEAD = 128


lowest_start = -1e30


def from_root(shard, axis, root):
    mine = lax.axis_index(axis) == root
    return lax.psum(jnp.where(mine, shard, jnp.zeros_like(shard)), axis)


def passed_along(block, axis, distance):
    devices = range(lax.axis_size(axis))
    route = [(i - distance, i) for i in devices if i - distance in devices]
    return lax.ppermute(block, axis, route)


def split_heads(block, head_dim):
    return block.reshape(block.shape[0], block.shape[1] // head_dim, head_dim)


def empty_stats(heads, rows):
    return (
        jnp.full((heads, rows), lowest_start, jnp.float32),
        jnp.zeros((heads, rows), jnp.float32),
        jnp.zeros((heads, rows), jnp.float32),
    )


def pair_stats(query_blk, grad_blk, key_blk, value_blk, scale):
    scores = scale * jnp.einsum(
        "qhd,khd->hqk", query_blk, key_blk, preferred_element_type=jnp.float32
    )
    peak = jnp.max(scores, axis=2)
    weights = jnp.exp(scores - peak[:, :, None])
    dprobs = jnp.einsum("qhd,khd->hqk", grad_blk, value_blk, preferred_element_type=jnp.float32)
    return (peak, jnp.sum(weights, axis=2), jnp.sum(weights * dprobs, axis=2))


def merge_stats(left, right):
    top = jnp.maximum(left[0], right[0])
    left_f = jnp.exp(left[0] - top)
    right_f = jnp.exp(right[0] - top)
    return (top, left[1] * left_f + right[1] * right_f, left[2] * left_f + right[2] * right_f)


def pair_grads(query_blk, grad_blk, log_sums, deltas, key_blk, value_blk, scale):
    scores = scale * jnp.einsum(
        "qhd,khd->hqk", query_blk, key_blk, preferred_element_type=jnp.float32
    )
    probs = jnp.exp(scores - log_sums[:, :, None])
    probs_low = probs.astype(jnp.bfloat16)
    value_term = jnp.einsum("hqk,qhd->khd", probs_low, grad_blk, preferred_element_type=jnp.float32)
    dprobs = jnp.einsum("qhd,khd->hqk", grad_blk, value_blk, preferred_element_type=jnp.float32)
    dscores = (probs * (dprobs - deltas[:, :, None])).astype(jnp.bfloat16)
    query_term = scale * jnp.einsum(
        "hqk,khd->qhd", dscores, key_blk, preferred_element_type=jnp.float32
    )
    key_term = scale * jnp.einsum(
        "hqk,qhd->khd", dscores, query_blk, preferred_element_type=jnp.float32
    )
    return (query_term, key_term, value_term)


def local(query_in, key_in, value_in, layer_grad, out_weight, group_mask, first_group):
    rows_loc, width_loc = query_in.shape
    head_dim = D_HEAD
    heads_loc = width_loc // head_dim
    scale = head_dim ** (-0.5)
    my_dev = lax.axis_index("tm")
    first = first_group[0]
    attn_grad = lax.dot_general(
        lax.all_gather(layer_grad, "head", axis=1, tiled=True),
        out_weight,
        (((1,), (1,)), ((), ())),
        preferred_element_type=jnp.float32,
    ).astype(jnp.bfloat16)
    query_three = split_heads(query_in, head_dim)
    grad_three = split_heads(attn_grad, head_dim)
    key_three = split_heads(key_in, head_dim)
    value_three = split_heads(value_in, head_dim)
    has_first = first != my_dev
    prev_index = jnp.maximum(my_dev - 1, 0)
    prev_used = (my_dev > 0) & (group_mask[my_dev, prev_index] == 1) & (first != my_dev - 1)
    shared = from_root(jnp.stack([key_in, value_in]), "tm", first)
    first_keys = split_heads(shared[0], head_dim)
    first_values = split_heads(shared[1], head_dim)
    blank = empty_stats(heads_loc, rows_loc)
    zero_three = jnp.zeros((rows_loc, heads_loc, head_dim), jnp.float32)
    zero_grads = (zero_three, zero_three, zero_three)
    diag_stats = pair_stats(query_three, grad_three, key_three, value_three, scale)
    first_stats = lax.cond(
        has_first,
        lambda: pair_stats(query_three, grad_three, first_keys, first_values, scale),
        lambda: blank,
    )
    running = merge_stats(diag_stats, first_stats)
    prev_pair = passed_along(jnp.stack([key_in, value_in]), "tm", 1)
    prev_keys = split_heads(prev_pair[0], head_dim)
    prev_values = split_heads(prev_pair[1], head_dim)
    prev_stats = lax.cond(
        prev_used,
        lambda: pair_stats(query_three, grad_three, prev_keys, prev_values, scale),
        lambda: blank,
    )
    row_max, row_sum, row_dot = merge_stats(running, prev_stats)
    log_sums = row_max + jnp.log(row_sum)
    deltas = row_dot / row_sum
    query_acc, key_acc, value_acc = pair_grads(
        query_three, grad_three, log_sums, deltas, key_three, value_three, scale
    )
    first_query, first_key, first_value = lax.cond(
        has_first,
        lambda: pair_grads(
            query_three, grad_three, log_sums, deltas, first_keys, first_values, scale
        ),
        lambda: zero_grads,
    )
    query_acc = query_acc + first_query
    prev_query_term, prev_key_term, prev_value_term = lax.cond(
        prev_used,
        lambda: pair_grads(
            query_three, grad_three, log_sums, deltas, prev_keys, prev_values, scale
        ),
        lambda: zero_grads,
    )
    query_acc = query_acc + prev_query_term
    returned = passed_along(
        jnp.stack([prev_key_term, prev_value_term]).astype(jnp.bfloat16), "tm", -1
    ).astype(jnp.float32)
    key_acc = key_acc + returned[0]
    value_acc = value_acc + returned[1]
    key_total, value_total = (
        lax.psum(first_key.astype(jnp.bfloat16), "tm").astype(jnp.float32),
        lax.psum(first_value.astype(jnp.bfloat16), "tm").astype(jnp.float32),
    )
    is_owner = my_dev == first
    key_acc = key_acc + jnp.where(is_owner, key_total, 0.0)
    value_acc = value_acc + jnp.where(is_owner, value_total, 0.0)
    query_out = query_acc.reshape(rows_loc, width_loc).astype(jnp.bfloat16)
    key_out = key_acc.reshape(rows_loc, width_loc).astype(jnp.bfloat16)
    value_out = value_acc.reshape(rows_loc, width_loc).astype(jnp.bfloat16)
    return (query_out, key_out, value_out)


def solution(mesh):
    placed = (
        P("tm", "head"),
        P("tm", "head"),
        P("tm", "head"),
        P("tm", "head"),
        P("head", None),
        P(),
        P(),
    )
    return jax.shard_map(
        local,
        mesh=mesh,
        in_specs=placed,
        out_specs=(P("tm", "head"), P("tm", "head"), P("tm", "head")),
        check_vma=False,
    )
```

profile of v0, /device:TPU:0, one launch (start us, length us, event | category | flops | bytes accessed | tf_op | source)
XLA Modules:
  0.0 716.6 jit_solution(11534320662256547631)
XLA Ops:
  8.7 4.9 broadcast_select_fusion
  14.3 6.8 collective-permute-start
  24.1 4.4 copy.45
  33.8 15.2 %multiply_reduce_fusion.5 = (f32[10,784]{1,0:T(8,128)S(1)}, f32[10,784,784]{1,2,0:T(8,128)}) fusion(bf16[784,10,128]{0,2,1:T(8,128)(2,1)S(1)} %bitcast.97, bf16[784,10,128]{0,2,1:T(8,128)(2,1)} %bitcast.113), kind=kOutput, calls=%fused_computation.35 | convolution fusion | flops 1585804672 | bytes 28631680 | tf_op jit(solution)/shard_map/qhd,khd->hqk/dot_general | solution.py:53
  49.1 175.1 %all-reduce.4.cloned.1.call-done = bf16[2,784,1280]{2,1,0:T(8,128)(2,1)} async-done(((bf16[2,784,1280]{2,1,0:T(8,128)(2,1)}), bf16[2,784,1280]{2,1,0:T(8,128)(2,1)}) %all-reduce.4.cloned.1.call-update) | async-done | bytes 4014096 | tf_op jit(solution)/shard_map/psum | solution.py:14
  224.2 4.4 fusion.37
  228.6 4.1 copy.34
  236.8 4.4 fusion.38
  241.2 4.1 copy.40
  249.5 16.3 %convolution_convert_fusion = bf16[784,1280]{1,0:T(8,128)(2,1)} fusion(bf16[784,5120]{1,0:T(8,128)(2,1)} %all-gather.2.cloned.1.call-done, bf16[1280,5120]{1,0:T(8,128)(2,1)} %param.19), kind=kOutput, calls=%fused_computation.53 | convolution fusion | flops 10277048320 | bytes 23142400 | tf_op jit(solution)/shard_map/dot_general | solution.py:77
  265.8 4.2 copy.33
  270.0 41.4 %conditional.4 = (f32[10,784]{1,0:T(8,128)}, f32[10,784]{1,0:T(8,128)S(1)}, f32[10,784]{1,0:T(8,128)S(1)}) conditional(s32[]{:T(128)} %convert_element_type.63, () %tuple.44, (bf16[784,10,128]{0,2,1:T(8,128)(2,1)S(1)}, bf16[784,10,128]{0,2,1:T(8,128)(2,1)}, bf16[784,10,128]{0,2,1:T(8,128)(2,1)}, bf16[784,10,128]{0,2,1:T(8,128)(2,1)}) %tuple.102), branch_computations={%region_2.3_spmd, %region_3.7_spmd} | conditional | flops 3202334208 | bytes 81943704 | solution.py:97
  270.1 15.4 %multiply_reduce_fusion.1 = (f32[10,784]{1,0:T(8,128)}, f32[10,784,784]{1,2,0:T(8,128)}) fusion(bf16[784,10,128]{0,2,1:T(8,128)(2,1)S(1)} %get-tuple-element.111, bf16[784,10,128]{0,2,1:T(8,128)(2,1)} %get-tuple-element.112), kind=kOutput, calls=%fused_computation.2 | convolution fusion | flops 1585804672 | bytes 28631680 | tf_op jit(solution)/shard_map/cond/branch_1_fun/qhd,khd->hqk/dot_general | solution.py:36
  285.5 13.7 %multiply_reduce_fusion = f32[10,784]{1,0:T(8,128)S(1)} fusion(f32[10,784,784]{1,2,0:T(8,128)} %get-tuple-element.139, f32[10,784]{1,0:T(8,128)} %get-tuple-element.162, bf16[784,10,128]{0,2,1:T(8,128)(2,1)} %get-tuple-element.113, bf16[784,10,128]{0,2,1:T(8,128)(2,1)} %get-tuple-element.114), kind=kOutput, calls=%fused_computation | convolution fusion | flops 1598097792 | bytes 28663040 | tf_op jit(solution)/shard_map/cond/branch_1_fun/qhd,khd->hqk/dot_general | solution.py:41
  299.2 12.2 %fusion = f32[10,784]{1,0:T(8,128)S(1)} fusion(f32[10,784,784]{1,2,0:T(8,128)} %get-tuple-element.139, f32[10,784]{1,0:T(8,128)} %get-tuple-element.162), kind=kLoop, calls=%fused_computation.3 | loop fusion | flops 18431840 | bytes 24648960 | tf_op jit(solution)/shard_map/cond/branch_1_fun/reduce_sum | solution.py:42
  312.3 24.3 %multiply_reduce_fusion.4 = (f32[10,784]{1,0:T(8,128)S(1)}, f32[10,784]{1,0:T(8,128)S(1)}, f32[10,784,784]{1,2,0:T(8,128)}) fusion(f32[10,784,784]{1,2,0:T(8,128)} %get-tuple-element.151, f32[10,784]{1,0:T(8,128)S(1)} %get-tuple-element.150, bf16[784,10,128]{0,2,1:T(8,128)(2,1)} %bitcast.105, bf16[784,10,128]{0,2,1:T(8,128)(2,1)} %bitcast.115), kind=kOutput, calls=%fused_computation.30 | convolution fusion | flops 1604236544 | bytes 53280640 | tf_op jit(solution)/shard_map/qhd,khd->hqk/dot_general | solution.py:59
  337.5 15.1 %conditional.7 = (f32[784,10,128]{2,0,1:T(8,128)}, bf16[1,784,10,128]{3,1,2,0:T(8,128)(2,1)}, bf16[1,784,10,128]{3,1,2,0:T(8,128)(2,1)}) conditional(s32[]{:T(128)} %convert_element_type.65, () %tuple.50, (bf16[784,10,128]{0,2,1:T(8,128)(2,1)S(1)}, bf16[784,10,128]{0,2,1:T(8,128)(2,1)S(1)}, f32[10,784]{1,0:T(8,128)S(1)}, ...), branch_computations={%region_16.17_spmd, %region_17.18_spmd} | conditional | flops 7920783360 | bytes 140837824 | solution.py:125
  352.6 4.6 pad_maximum_fusion.1
  358.5 55.2 %conditional.6 = (f32[784,10,128]{2,0,1:T(8,128)}, f32[784,10,128]{2,0,1:T(8,128)}, f32[784,10,128]{2,0,1:T(8,128)}) conditional(s32[]{:T(128)} %convert_element_type.63, () %tuple.48, (bf16[784,10,128]{0,2,1:T(8,128)(2,1)S(1)}, bf16[784,10,128]{0,2,1:T(8,128)(2,1)S(1)}, f32[10,784]{1,0:T(8,128)S(1)}, bf16[784,10,128]{0,2,1:T(8,128)(2,1)}, ...), branch_computations={%region_14.15_spmd, %region_15.16_spmd} | conditional | flops 7918776320 | bytes 144851904 | solution.py:117
  359.9 11.2 %fusion.39 = f32[10,784,784]{2,1,0:T(8,128)} fusion(bf16[784,10,128]{0,2,1:T(8,128)(2,1)S(1)} %get-tuple-element.119, bf16[784,10,128]{0,2,1:T(8,128)(2,1)S(1)} %get-tuple-element.120), kind=kOutput, calls=%fused_computation.64 | convolution fusion | flops 1573519360 | bytes 28600320 | tf_op jit(solution)/shard_map/cond/branch_1_fun/qhd,khd->hqk/dot_general | solution.py:53
  371.1 14.8 %fusion.7 = f32[784,10,128]{2,0,1:T(8,128)} fusion(bf16[784,10,128]{0,2,1:T(8,128)(2,1)} %get-tuple-element.122, f32[10,784,784]{2,1,0:T(8,128)} %fusion.39, f32[10,784]{1,0:T(8,128)S(1)} %get-tuple-element.52), kind=kOutput, calls=%fused_computation.16 | convolution fusion | flops 1591959040 | bytes 30638720 | tf_op jit(solution)/shard_map/cond/branch_1_fun/hqk,qhd->khd/dot_general | solution.py:58
  385.9 13.7 %multiply_convert_fusion = bf16[10,784,784]{2,1,0:T(8,128)(2,1)S(1)} fusion(f32[10,784,784]{2,1,0:T(8,128)} %fusion.39, f32[10,784]{1,0:T(8,128)S(1)} %get-tuple-element.55, f32[10,784]{1,0:T(8,128)S(1)} %get-tuple-element.52, bf16[784,10,128]{0,2,1:T(8,128)(2,1)} %get-tuple-element.122, bf16[784,10,128]{0,2,1:T(8,128)(2,1)} %get-tuple-element.123), kind=kOutput, calls=%fused_computation.8 | convolution fusion | flops 1604252160 | bytes 40956160 | tf_op jit(solution)/shard_map/cond/branch_1_fun/qhd,khd->hqk/dot_general | solution.py:59
  399.7 6.4 multiply_bitcast_fusion
  406.1 7.5 %multiply_bitcast_fusion.1 = f32[784,10,128]{2,0,1:T(8,128)} fusion(bf16[10,784,784]{2,1,0:T(8,128)(2,1)S(1)} %multiply_convert_fusion, bf16[784,10,128]{0,2,1:T(8,128)(2,1)} %copy-done.1), kind=kOutput, calls=%fused_computation.15 | convolution fusion | flops 1574522880 | bytes 18314240 | tf_op jit(solution)/shard_map/cond/branch_1_fun/hqk,khd->qhd/dot_general | solution.py:61
  421.2 24.0 %multiply_convert_fusion.3 = bf16[10,784,784]{1,2,0:T(8,128)(2,1)} fusion(f32[10,784,784]{1,2,0:T(8,128)} %get-tuple-element.152, f32[10,784,784]{1,2,0:T(8,128)} %get-tuple-element.151, f32[10,784]{1,0:T(8,128)S(1)} %get-tuple-element.148, f32[10,784]{1,0:T(8,128)S(1)} %get-tuple-element.149), kind=kLoop, calls=%fused_computation.29 | loop fusion | flops 30732800 | bytes 61528320 | tf_op jit(solution)/shard_map/convert_element_type | solution.py:60
  445.2 11.4 %fusion.33 = bf16[784,10,128]{2,0,1:T(8,128)(2,1)} fusion(f32[784,10,128]{2,0,1:T(8,128)} %get-tuple-element.84, f32[784,10,128]{2,0,1:T(8,128)} %get-tuple-element.83, bf16[10,784,784]{1,2,0:T(8,128)(2,1)} %multiply_convert_fusion.3, bf16[784,10,128]{0,2,1:T(8,128)(2,1)} %bitcast.114), kind=kOutput, calls=%fused_computation.51 | convolution fusion | flops 1577533440 | bytes 24335360 | tf_op jit(solution)/shard_map/hqk,khd->qhd/dot_general | solution.py:61
  456.7 4.2 copy.58
  464.9 77.7 %collective-permute-done.1 = bf16[2,784,10,128]{3,1,2,0:T(8,128)(2,1)} collective-permute-done((bf16[2,784,10,128]{3,1,2,0:T(8,128)(2,1)}, bf16[2,784,10,128]{3,1,2,0:T(8,128)(2,1)}, u32[]{:S(2)}, u32[]{:S(2)}) %collective-permute-start.1) | collective-permute-done | bytes 4014112 | tf_op jit(solution)/shard_map/ppermute | solution.py:20
  542.6 5.8 convert_element_type.69
  548.4 123.1 %all-reduce.6.cloned.1.call-done = (bf16[784,10,128]{2,0,1:T(8,128)(2,1)}, bf16[784,10,128]{2,0,1:T(8,128)(2,1)}) async-done(((bf16[784,10,128]{2,0,1:T(8,128)(2,1)}, bf16[784,10,128]{2,0,1:T(8,128)(2,1)}), (bf16[784,10,128]{2,0,1:T(8,128)(2,1)}, bf16[784,10,128]{2,0,1:T(8,128)(2,1)})) %all-reduce.6.cloned.1.call-update) | async-done | bytes 4014096 | tf_op jit(solution)/shard_map/psum | solution.py:139
  671.5 15.6 %fusion.28 = bf16[784,10,128]{2,0,1:T(8,128)(2,1)} fusion(f32[2,784,10,128]{3,1,2,0:T(8,128)} %convert_element_type.69, bf16[784,10,128]{2,0,1:T(8,128)(2,1)} %get-tuple-element.137, bf16[784,10,128]{0,2,1:T(8,128)(2,1)} %bitcast.108, f32[10,784,784]{1,2,0:T(8,128)} %get-tuple-element.151, f32[10,784]{1,0:T(8,128)S(1)} %get-tuple-element.149, pred[]{:T(512)S(6)} %eq.10), kind=kOutput, calls=%fused_computation.42 | convolution fusion | flops 1596976640 | bytes 34652800 | tf_op jit(solution)/shard_map/hqk,qhd->khd/dot_general | solution.py:58
  687.1 9.7 %fusion.31 = bf16[784,10,128]{2,0,1:T(8,128)(2,1)} fusion(f32[2,784,10,128]{3,1,2,0:T(8,128)} %convert_element_type.69, bf16[784,10,128]{2,0,1:T(8,128)(2,1)} %get-tuple-element.136, pred[]{:T(512)S(6)} %eq.10, bf16[10,784,784]{1,2,0:T(8,128)(2,1)} %multiply_convert_fusion.3, bf16[784,10,128]{0,2,1:T(8,128)(2,1)S(1)} %bitcast.102), kind=kOutput, calls=%fused_computation.46 | convolution fusion | flops 1579540480 | bytes 22328320 | tf_op jit(solution)/shard_map/hqk,qhd->khd/dot_general | solution.py:64
  (37 shorter events, 50.7 us)
Async XLA Ops:
  8.0 216.2 %all-reduce.4.cloned.1.call-start = ((), (), s32[]{:S(2)}) async-start(), calls=%async_computation | async-start | bytes 8028160 | tf_op jit(solution)/shard_map/psum | solution.py:14
  13.6 7.5 %copy-start.4 = (bf16[784,1280]{1,0:T(8,128)(2,1)S(1)}, bf16[784,1280]{1,0:T(8,128)(2,1)}, u32[]{:S(2)}) copy-start(bf16[784,1280]{1,0:T(8,128)(2,1)} %param.16) | copy-start | bytes 6021124
  13.6 235.9 %all-gather.2.cloned.1.call-start = ((), (), s32[]{:S(2)}) async-start(), calls=%async_computation.1 | async-start | bytes 10035200 | tf_op jit(solution)/shard_map/all_gather | solution.py:78
  14.2 657.3 %all-reduce.6.cloned.1.call-start = ((), (), s32[]{:S(2)}) async-start(), calls=%async_computation.2 | async-start | bytes 8028160 | tf_op jit(solution)/shard_map/psum | solution.py:139
  14.3 222.6 %collective-permute-start = (bf16[2,784,1280]{2,1,0:T(8,128)(2,1)}, bf16[2,784,1280]{2,1,0:T(8,128)(2,1)}, u32[]{:S(2)}, u32[]{:S(2)}) collective-permute-start(bf16[2,784,1280]{2,1,0:T(8,128)(2,1)} %get-tuple-element.145), channel_id=1, source_target_pairs={{0,4},{4,8},{8,12},{12,16},{16,20},{20,24},{24,28},{1,5},{5,9},{9,... | collective-permute-start | bytes 12042248 | tf_op jit(solution)/shard_map/ppermute | solution.py:20
  312.3 25.2 %copy-start.2 = (bf16[1,784,1280]{1,2,0:T(8,128)(2,1)S(1)}, bf16[1,784,1280]{1,2,0:T(8,128)(2,1)}, u32[]{:S(2)}) copy-start(bf16[1,784,1280]{1,2,0:T(8,128)(2,1)} %copy.39) | copy-start | bytes 6021124
  352.5 4.6 copy-start
  357.2 185.4 %collective-permute-start.1 = (bf16[2,784,10,128]{3,1,2,0:T(8,128)(2,1)}, bf16[2,784,10,128]{3,1,2,0:T(8,128)(2,1)}, u32[]{:S(2)}, u32[]{:S(2)}) collective-permute-start(bf16[2,784,10,128]{3,1,2,0:T(8,128)(2,1)} %pad_maximum_fusion.1), channel_id=1, source_target_pairs={{4,0},{8,4},{12,8},{16,12},{20,16},{24,20},{28,24},{5,1},{9,5},{13... | collective-permute-start | bytes 12042248 | tf_op jit(solution)/shard_map/ppermute | solution.py:20
  358.5 1.4 copy-start.1
Sparse Core Ops, SparseCore 0:
  13.8 210.4 all-reduce.3
  421.3 250.1 all-reduce.5
Sparse Core Ops, SparseCore 1:
  15.7 58.8 all-gather.1
where the time goes:
time: 725 us; the launch traced here: 717 us
  waiting for transfers between devices  376 us (52%)
  matrix products  175 us (24%)
  local copies, waits for them, and re-layouts  69.2 us (10%)
  other arithmetic  59.9 us (8%)
  between operations  17.1 us (2%)
  loops' own time  10.4 us (1%)
  starting transfers between devices  8.2 us (1%)
    psum x1, waiting for transfers between devices, from_root(): return lax.psum(jnp.where(mine, shard, jnp.zeros_like(shard)), axis)  175 us
    psum x1, waiting for transfers between devices, local(): lax.psum(first_key.astype(jnp.bfloat16), 'tm').astype(jnp.float32)  123 us
    ppermute x2, waiting for transfers between devices, passed_along(): return lax.ppermute(block, axis, route)  77.7 us
    dot_general x2, matrix products, pair_grads(): jnp.einsum('qhd,khd->hqk', grad_blk, value_blk, preferred_element_type=jn...  38 us
    dot_general x2, matrix products, pair_grads(): jnp.einsum('hqk,qhd->khd', probs_low, grad_blk, preferred_element_type=jn...  30.4 us
    dot_general x2, matrix products, pair_grads(): jnp.einsum('qhd,khd->hqk', query_blk, key_blk, preferred_element_type=jnp...  26.4 us
    convert_element_type x1, other arithmetic, pair_grads(): dscores = (probs * (dprobs - deltas[:, :, None])).astype(jnp.bfloat16)  24 us
    unnamed x12, local copies, waits for them, and re-layouts  20.2 us
  transfers between devices with their start and end apart: 5, of which 3 were waited for; matrix products, arithmetic and copies ran while one was open for 23% of the time, Pallas kernels for 0%

commit v1 on v0

v1 whole, which is shorter than its diff:
```python
import functools
import math

import jax
import jax.numpy as jnp
from jax import lax
from jax.experimental import pallas as pl
from jax.experimental.pallas import tpu as pltpu
from jax.sharding import PartitionSpec as P

D_HEAD = 128
Q_TILE = 256
PAD = 128
NEVER = 1e30


def nt(a, b):
    return lax.dot_general(a, b, (((1,), (1,)), ((), ())), preferred_element_type=jnp.float32)


def nn(a, b):
    return lax.dot_general(a, b, (((1,), (0,)), ((), ())), preferred_element_type=jnp.float32)


def attn_kernel(
    scale, rows, sub, flags_ref, q_ref, g_ref, ko_ref, vo_ref, near_ref, far_ref, prev_ref, *rest
):
    dq_ref, dko_ref, dvo_ref, dfirst_ref, dprev_ref = rest[-12:-7]
    first_ref, kt_ref, s_ref, dp_ref, pds_ref, dk_acc, dv_acc = rest[-7:]
    log2e = scale * math.log2(math.e)
    is_near = pl.program_id(0) == flags_ref[3]

    @pl.when(is_near)
    def _():
        first_ref[...] = near_ref[...]

    @pl.when(jnp.logical_not(is_near))
    def _():
        first_ref[...] = far_ref[...]

    used = [None, flags_ref[0] > 0, flags_ref[1] > 0]
    keys = [ko_ref, first_ref.at[0], prev_ref.at[0, 0]]
    values = [vo_ref, first_ref.at[1], prev_ref.at[0, 1]]
    for p in range(3):
        kt_ref[p] = keys[p][...].T
    dk_acc[...] = jnp.zeros_like(dk_acc)
    dv_acc[...] = jnp.zeros_like(dv_acc)
    cuts = [pl.ds(j * sub, sub) for j in range(rows // sub)]
    halves = [pl.ds(0, rows)]
    if rows % 32 == 0 or rows // 2 % 8 == 0:
        halves = [pl.ds(0, rows // 2), pl.ds(rows // 2, rows // 2)]

    tiles = []
    for start in range(0, rows, Q_TILE):
        left = min(Q_TILE, rows - start)
        width = -(-left // PAD) * PAD
        at = pl.ds(start, left)
        q_t, g_t = q_ref[at, :], g_ref[at, :]
        if width > left:
            pad = jnp.zeros((width - left, D_HEAD), jnp.bfloat16)
            q_t, g_t = jnp.concatenate([q_t, pad], axis=0), jnp.concatenate([g_t, pad], axis=0)
        tiles.append((at, left, width, q_t, g_t))

    def products(t):
        _, _, width, q_t, g_t = tiles[t]
        slot, lanes = t % 2, pl.ds(0, width)
        for p in range(3):
            for part in halves:
                s_ref[slot, p, part, lanes] = nt(keys[p][part, :], q_t)
                yield
        for p in range(3):
            for part in halves:
                dp_ref[slot, p, part, lanes] = nt(values[p][part, :], g_t)
                yield

    def softmax(t):
        _, _, width, _, _ = tiles[t]
        slot, lanes = t % 2, pl.ds(0, width)
        peak = None
        for p in range(3):
            top = None
            for cut in cuts:
                part = jnp.max(s_ref[slot, p, cut, lanes], axis=0, keepdims=True)
                top = part if top is None else jnp.maximum(top, part)
                yield
            if p > 0:
                top = jnp.where(used[p], top, -NEVER)
            peak = top if peak is None else jnp.maximum(peak, top)
        peak = peak * log2e
        total = jnp.zeros((1, width), jnp.float32)
        dots = jnp.zeros((1, width), jnp.float32)
        for p in range(3):
            shift = peak if p == 0 else jnp.where(used[p], peak, NEVER)
            for cut in cuts:
                e = jnp.exp2(s_ref[slot, p, cut, lanes] * log2e - shift)
                s_ref[slot, p, cut, lanes] = e
                total += jnp.sum(e, axis=0, keepdims=True)
                dots += jnp.sum(e * dp_ref[slot, p, cut, lanes], axis=0, keepdims=True)
                yield
        inv = 1.0 / total
        delta = dots * inv
        for p in range(3):
            for cut in cuts:
                prob = s_ref[slot, p, cut, lanes] * inv
                ds = prob * (dp_ref[slot, p, cut, lanes] - delta)
                pds_ref[slot, 0, p, cut, lanes] = prob.astype(jnp.bfloat16)
                pds_ref[slot, 1, p, cut, lanes] = ds.astype(jnp.bfloat16)
                yield

    def gradients(t):
        at, left, width, q_t, g_t = tiles[t]
        slot, lanes = t % 2, pl.ds(0, width)
        dq_t = jnp.zeros((D_HEAD, width), jnp.float32)
        for p in range(3):
            dv_acc[p] += nn(pds_ref[slot, 0, p, :, lanes], g_t)
            yield
            dk_acc[p] += nn(pds_ref[slot, 1, p, :, lanes], q_t)
            yield
            dq_t += nn(kt_ref[p], pds_ref[slot, 1, p, :, lanes])
            yield
        dq_ref[at, :] = (dq_t * scale).T.astype(jnp.bfloat16)[:left]

    count = len(tiles)
    for stage in range(count + 2):
        live = []
        if stage < count:
            live.append([products(stage), 6 * len(halves), 0])
        if 0 < stage <= count:
            live.append([softmax(stage - 1), 9 * len(cuts), 0])
        if stage > 1:
            live.append([gradients(stage - 2), 9, 0])
        while live:
            turn = min(live, key=lambda x: x[2] / x[1])
            turn[2] += 1
            try:
                next(turn[0])
            except StopIteration:
                live.remove(turn)

    dko_ref[...] = (dk_acc[0] * scale).astype(jnp.bfloat16)
    dvo_ref[...] = dv_acc[0].astype(jnp.bfloat16)
    dfirst_ref[0, 0] = (dk_acc[1] * scale).astype(jnp.bfloat16)
    dfirst_ref[0, 1] = dv_acc[1].astype(jnp.bfloat16)
    dprev_ref[0, 0] = (dk_acc[2] * scale).astype(jnp.bfloat16)
    dprev_ref[0, 1] = dv_acc[2].astype(jnp.bfloat16)


def attn_call(flags, q, g, ko, vo, near, far, prev, outs, heads, scale):
    rows, width = q.shape
    count = len(heads)
    stride = heads[1] - heads[0] if count > 1 else 0
    base = heads[0]
    sub = 112 if rows % 112 == 0 else 16
    column = pl.BlockSpec((rows, D_HEAD), lambda h, f: (0, base + stride * h))
    pair = pl.BlockSpec((1, 2, rows, D_HEAD), lambda h, f: (h, 0, 0, 0))
    both = pl.BlockSpec((2, rows, D_HEAD), lambda h, f: (0, 0, 0))
    whole = jax.ShapeDtypeStruct((rows, width), jnp.bfloat16)
    piece = jax.ShapeDtypeStruct((count, 2, rows, D_HEAD), jnp.bfloat16)
    passed = [] if outs is None else list(outs)
    aliases = {8 + i: i for i in range(len(passed))}
    flops = 2 * 5 * 3 * rows * rows * D_HEAD * count
    return pl.pallas_call(
        functools.partial(attn_kernel, scale, rows, sub),
        grid_spec=pltpu.PrefetchScalarGridSpec(
            num_scalar_prefetch=1,
            grid=(count,),
            in_specs=[column, column, column, column, both, both, pair]
            + [pl.BlockSpec(memory_space=pl.ANY)] * len(passed),
            out_specs=[column, column, column, pair, pair],
            scratch_shapes=[
                pltpu.VMEM((2, rows, D_HEAD), jnp.bfloat16),
                pltpu.VMEM((3, D_HEAD, rows), jnp.bfloat16),
                pltpu.VMEM((2, 3, rows, Q_TILE), jnp.float32),
                pltpu.VMEM((2, 3, rows, Q_TILE), jnp.float32),
                pltpu.VMEM((2, 2, 3, rows, Q_TILE), jnp.bfloat16),
                pltpu.VMEM((3, rows, D_HEAD), jnp.float32),
                pltpu.VMEM((3, rows, D_HEAD), jnp.float32),
            ],
        ),
        out_shape=[whole, whole, whole, piece, piece],
        input_output_aliases=aliases,
        compiler_params=pltpu.CompilerParams(
            dimension_semantics=("arbitrary",), vmem_limit_bytes=44 * 1024 * 1024
        ),
        cost_estimate=pl.CostEstimate(
            flops=2 * flops,
            bytes_accessed=15 * rows * D_HEAD * 2 * count,
            transcendentals=3 * rows * rows * count,
        ),
    )(flags, q, g, ko, vo, near, far, prev, *passed)


def join_kernel(flags_ref, dk_ref, dv_ref, back_ref, near_ref, far_ref, dk_out, dv_out):
    owner = flags_ref[2] > 0
    is_near = pl.program_id(0) == flags_ref[3]
    for i, (src, dst) in enumerate(((dk_ref, dk_out), (dv_ref, dv_out))):
        total = jnp.where(is_near, near_ref[i], far_ref[i]).astype(jnp.float32)
        part = src[...].astype(jnp.float32) + back_ref[0, i].astype(jnp.float32)
        dst[...] = (part + jnp.where(owner, total, 0.0)).astype(jnp.bfloat16)


def join_call(flags, dk, dv, back, near, far, heads):
    rows = dk.shape[0]
    count = len(heads)
    stride = heads[1] - heads[0] if count > 1 else 0
    base = heads[0]
    column = pl.BlockSpec((rows, D_HEAD), lambda h, f: (0, base + stride * h))
    pair = pl.BlockSpec((1, 2, rows, D_HEAD), lambda h, f: (h, 0, 0, 0))
    both = pl.BlockSpec((2, rows, D_HEAD), lambda h, f: (0, 0, 0))
    whole = jax.ShapeDtypeStruct(dk.shape, jnp.bfloat16)
    return pl.pallas_call(
        join_kernel,
        grid_spec=pltpu.PrefetchScalarGridSpec(
            num_scalar_prefetch=1,
            grid=(count,),
            in_specs=[column, column, pair, both, both],
            out_specs=[column, column],
        ),
        out_shape=[whole, whole],
        input_output_aliases={1: 0, 2: 1},
        cost_estimate=pl.CostEstimate(
            flops=4 * rows * D_HEAD * count,
            bytes_accessed=8 * rows * D_HEAD * 2 * count,
            transcendentals=0,
        ),
    )(flags, dk, dv, back, near, far)


def pick(index, candidates):
    keys = sorted(candidates)
    out = candidates[keys[0]]
    for k in keys[1:]:
        out = jnp.where(index == k, candidates[k], out)
    return out


def after(value, *others):
    return lax.optimization_barrier((value, *others))[0]


def local(query_in, key_in, value_in, layer_grad, out_weight, group_mask, first_group):
    rows, width = query_in.shape
    heads = width // D_HEAD
    scale = D_HEAD ** (-0.5)
    n = lax.axis_size("tm")
    me = lax.axis_index("tm")
    first = first_group[0]
    owner = first == me
    prev_index = jnp.maximum(me - 1, 0)
    prev_used = (me > 0) & (group_mask[me, prev_index] == 1) & (first != me - 1)
    lines = n // 2
    line, side = me // 2, me % 2
    source = jnp.where(side == first % 2, first, (first + 1) % n) // 2
    hops = jnp.abs(line - source)
    flags = jnp.stack(
        [(~owner).astype(jnp.int32), prev_used.astype(jnp.int32), owner.astype(jnp.int32), side]
    ).astype(jnp.int32)
    count = heads - heads // 2
    chunks = [tuple(range(c, heads, count)) for c in range(count)]
    forward = [(i, (i + 1) % n) for i in range(n)]
    backward = [(b, a) for a, b in forward]
    higher = [(i, i + 2) for i in range(n - 2)]
    lower = [(b, a) for a, b in higher]
    across = [(i, i ^ 1) for i in range(n)]
    blank = jnp.zeros((2, rows, D_HEAD), jnp.bfloat16)

    def unit(h):
        cols = slice(h * D_HEAD, (h + 1) * D_HEAD)
        return jnp.stack([key_in[:, cols], value_in[:, cols]])

    def half_of(chunk, which):
        low, high = chunk[0], chunk[-1]
        return jnp.where(side == which, low, high)

    gathered = lax.all_gather(layer_grad, "head", axis=1, tiled=True)

    prevs, streams, held = [], [], []
    nears, fars, sums = [], [], []
    outs, attn_grad = None, None
    first_parts, backs = [], []
    shares, ends = [], []
    totals, fetched = [], []

    def send_prev(c):
        units = jnp.stack([unit(h) for h in chunks[c]])
        if c > 1:
            units = after(units, prevs[c - 2])
        got = lax.ppermute(units, "tm", forward)
        prevs.append(got)
        streams.append(jnp.where(owner, half_of(units, 0), half_of(got, 0)))

    def spread(s):
        fresh = streams[s] if s < count else blank
        sent = jnp.where(hops == 0, fresh, held[-1]) if held else fresh
        up = lax.ppermute(sent, "tm", higher)
        down = lax.ppermute(sent, "tm", lower)
        held.append(jnp.where(line > source, up, down))

    def exchange(c):
        near = pick(hops, {0: streams[c], **{d: held[c + d - 1] for d in range(1, lines)}})
        if c > 1:
            near = after(near, first_parts[c - 2])
        nears.append(near)
        fars.append(lax.ppermute(near, "tm", across))

    def attend(c):
        nonlocal outs
        arrived = after(prevs[c], backs[c - 2]) if c > 1 else prevs[c]
        done = attn_call(
            flags, query_in, attn_grad, key_in, value_in, nears[c], fars[c], arrived,
            outs, chunks[c], scale,
        )
        outs = done[:3]
        first_parts.append(done[3])
        backs.append(lax.ppermute(done[4], "tm", backward))
        shares.append(lax.ppermute(half_of(done[3], 1), "tm", across))

    def gather_up(s):
        for c in range(len(sums), min(s + 1, count)):
            mine = half_of(first_parts[c], 0).astype(jnp.float32)
            sums.append(mine + shares[c].astype(jnp.float32))
        low = max(0, s - lines + 1)
        total = pick(s - lines + 1 + hops, {c: sums[c] for c in range(low, min(s, count - 1) + 1)})
        if ends:
            up, down = ends[-1]
            total += jnp.where(line > source, down, up).astype(jnp.float32)
        sent = total.astype(jnp.bfloat16)
        if s >= lines:
            sent = after(sent, fetched[s - lines])
        if s >= count:
            sent = after(sent, backs[min(s - 2, count - 1)])
        ends.append((lax.ppermute(sent, "tm", higher), lax.ppermute(sent, "tm", lower)))
        c = s - lines + 2
        if c >= 0:
            up, down = ends[-1]
            whole = sums[c] + up.astype(jnp.float32) + down.astype(jnp.float32)
            totals.append(whole.astype(jnp.bfloat16))
            fetched.append(lax.ppermute(totals[-1], "tm", backward))

    steps = count + lines - 2
    lead = lines + 1
    for k in range(lead + count + steps + 2):
        if k < count:
            send_prev(k)
        if 0 <= k - 1 < steps:
            spread(k - 1)
        if 0 <= k - lines < count:
            exchange(k - lines)
        if k == lead:
            attn_grad = lax.dot_general(
                after(gathered, nears[0]),
                out_weight,
                (((1,), (1,)), ((), ())),
                preferred_element_type=jnp.float32,
            ).astype(jnp.bfloat16)
        if 0 <= k - lead < count:
            attend(k - lead)
        if 0 <= k - lead - 1 < steps:
            gather_up(k - lead - 1)

    dq, dk, dv = outs
    for c, pair in enumerate(chunks):
        dk, dv = join_call(flags, dk, dv, backs[c], totals[c], fetched[c], pair)
    return dq, dk, dv


def solution(mesh):
    placed = (
        P("tm", "head"),
        P("tm", "head"),
        P("tm", "head"),
        P("tm", "head"),
        P("head", None),
        P(),
        P(),
    )
    return jax.shard_map(
        local,
        mesh=mesh,
        in_specs=placed,
        out_specs=(P("tm", "head"), P("tm", "head"), P("tm", "head")),
        check_vma=False,
    )
```

time: 725 us -> 517 us (0.71)
  the two profiles are of different devices: /device:TPU:0 before, /device:TPU:26 now
where the time goes in v1:
time: 517 us; the launch traced here: 509 us
  waiting for transfers between devices  160 us (31%)
  starting transfers between devices  138 us (27%)
  Pallas kernels  126 us (24%)
  other arithmetic  41.2 us (8%)
  between operations  16.7 us (3%)
  matrix products  15.2 us (3%)
  local copies, waits for them, and re-layouts  11.9 us (2%)
    pallas_call x5, Pallas kernels, attn_call(): pl.pallas_call(functools.partial(attn_kernel, scale, rows, sub), grid_spe...  109 us
    ppermute x7, waiting for transfers between devices, spread(): up = lax.ppermute(sent, 'tm', higher)  59.6 us
    ppermute x5, starting transfers between devices, gather_up(): fetched.append(lax.ppermute(totals[-1], 'tm', backward))  45.3 us
    ppermute x7, starting transfers between devices, spread(): down = lax.ppermute(sent, 'tm', lower)  35.5 us
    ppermute x5, waiting for transfers between devices, gather_up(): fetched.append(lax.ppermute(totals[-1], 'tm', backward))  34.2 us
    ppermute x5, waiting for transfers between devices, send_prev(): got = lax.ppermute(units, 'tm', forward)  30.6 us
    ppermute x7, starting transfers between devices, gather_up(): lax.ppermute(sent, 'tm', lower)  19.3 us
    pallas_call x5, Pallas kernels, join_call(): pl.pallas_call(join_kernel, grid_spec=pltpu.PrefetchScalarGridSpec(num_sc...  16.7 us
  transfers between devices with their start and end apart: 54, of which 21 were waited for; matrix products, arithmetic and copies ran while one was open for 12% of the time, Pallas kernels for 24%

profile of v1, /device:TPU:26, one launch (start us, length us, event | category | flops | bytes accessed | tf_op | source)
XLA Modules:
  0.0 509.0 jit_solution(11995721127030686860)
XLA Ops:
  16.6 17.5 %collective-permute-done.prev_ref = bf16[2,2,784,128]{3,2,1,0:T(8,128)(2,1)S(1)} collective-permute-done((bf16[2,2,784,128]{3,2,1,0:T(8,128)(2,1)}, bf16[2,2,784,128]{3,2,1,0:T(8,128)(2,1)S(1)}, u32[]{:S(2)}, u32[]{:S(2)}) %collective-permute-start) | collective-permute-done | bytes 802848 | tf_op jit(solution)/shard_map/ppermute | solution.py:288
  37.4 5.3 %collective-permute-start.4 = (bf16[2,784,128]{2,1,0:T(8,128)(2,1)}, bf16[2,784,128]{2,1,0:T(8,128)(2,1)}, u32[]{:S(2)}, u32[]{:S(2)}) collective-permute-start(bf16[2,784,128]{2,1,0:T(8,128)(2,1)} %fusion.6), channel_id=1, source_target_pairs={{8,0},{12,4},{16,8},{20,12},{24,16},{28,20},{9,1},{13,5},{17,9},{2... | collective-permute-start | bytes 1204232 | tf_op jit(solution)/shard_map/ppermute | solution.py:296
  43.8 7.7 %collective-permute-done.2.prev_ref = bf16[2,2,784,128]{3,2,1,0:T(8,128)(2,1)} collective-permute-done((bf16[2,2,784,128]{3,2,1,0:T(8,128)(2,1)}, bf16[2,2,784,128]{3,2,1,0:T(8,128)(2,1)}, u32[]{:S(2)}, u32[]{:S(2)}) %collective-permute-start.2) | collective-permute-done | bytes 802848 | tf_op jit(solution)/shard_map/ppermute | solution.py:288
  51.4 8.6 %collective-permute-done.3 = bf16[2,784,128]{2,1,0:T(8,128)(2,1)} collective-permute-done((bf16[2,784,128]{2,1,0:T(8,128)(2,1)}, bf16[2,784,128]{2,1,0:T(8,128)(2,1)}, u32[]{:S(2)}, u32[]{:S(2)}) %collective-permute-start.3) | collective-permute-done | bytes 401440 | tf_op jit(solution)/shard_map/ppermute | solution.py:295
  63.6 4.6 collective-permute-start.6
  68.5 17.2 %collective-permute-done.5 = bf16[2,784,128]{2,1,0:T(8,128)(2,1)S(1)} collective-permute-done((bf16[2,784,128]{2,1,0:T(8,128)(2,1)S(1)}, bf16[2,784,128]{2,1,0:T(8,128)(2,1)S(1)}, u32[]{:S(2)}, u32[]{:S(2)}) %collective-permute-start.5) | collective-permute-done | bytes 401440 | tf_op jit(solution)/shard_map/ppermute | solution.py:295
  89.4 4.6 collective-permute-start.8
  95.1 5.4 %collective-permute-done.10.prev_ref = bf16[2,2,784,128]{3,2,1,0:T(8,128)(2,1)S(1)} collective-permute-done((bf16[2,2,784,128]{3,2,1,0:T(8,128)(2,1)S(1)}, bf16[2,2,784,128]{3,2,1,0:T(8,128)(2,1)S(1)}, u32[]{:S(2)}, u32[]{:S(2)}) %collective-permute-start.10) | collective-permute-done | bytes 802848 | tf_op jit(solution)/shard_map/ppermute | solution.py:288
  100.6 11.0 %collective-permute-done.7 = bf16[2,784,128]{2,1,0:T(8,128)(2,1)S(1)} collective-permute-done((bf16[2,784,128]{2,1,0:T(8,128)(2,1)S(1)}, bf16[2,784,128]{2,1,0:T(8,128)(2,1)S(1)}, u32[]{:S(2)}, u32[]{:S(2)}) %collective-permute-start.7) | collective-permute-done | bytes 401440 | tf_op jit(solution)/shard_map/ppermute | solution.py:295
  114.7 5.3 %collective-permute-start.12 = (bf16[2,784,128]{2,1,0:T(8,128)(2,1)}, bf16[2,784,128]{2,1,0:T(8,128)(2,1)}, u32[]{:S(2)}, u32[]{:S(2)}) collective-permute-start(bf16[2,784,128]{2,1,0:T(8,128)(2,1)} %get-tuple-element.121), channel_id=1, source_target_pairs={{8,0},{12,4},{16,8},{20,12},{24,16},{28,20},{9,1},{13,5},{17,9},{2... | collective-permute-start | bytes 1204232 | tf_op jit(solution)/shard_map/ppermute | solution.py:296
  120.1 16.2 %collective-permute-done.11 = bf16[2,784,128]{2,1,0:T(8,128)(2,1)} collective-permute-done((bf16[2,784,128]{2,1,0:T(8,128)(2,1)}, bf16[2,784,128]{2,1,0:T(8,128)(2,1)}, u32[]{:S(2)}, u32[]{:S(2)}) %collective-permute-start.11) | collective-permute-done | bytes 401440 | tf_op jit(solution)/shard_map/ppermute | solution.py:295
  142.6 4.6 collective-permute-start.14
  147.1 6.2 %collective-permute-done.13 = bf16[2,784,128]{2,1,0:T(8,128)(2,1)S(1)} collective-permute-done((bf16[2,784,128]{2,1,0:T(8,128)(2,1)S(1)}, bf16[2,784,128]{2,1,0:T(8,128)(2,1)S(1)}, u32[]{:S(2)}, u32[]{:S(2)}) %collective-permute-start.13) | collective-permute-done | bytes 401440 | tf_op jit(solution)/shard_map/ppermute | solution.py:295
  158.5 5.3 %collective-permute-start.16 = (bf16[2,784,128]{2,1,0:T(8,128)(2,1)}, bf16[2,784,128]{2,1,0:T(8,128)(2,1)}, u32[]{:S(2)}, u32[]{:S(2)}) collective-permute-start(bf16[2,784,128]{2,1,0:T(8,128)(2,1)} %broadcast_select_fusion.6), channel_id=1, source_target_pairs={{8,0},{12,4},{16,8},{20,12},{24,16},{28,20},{9,1},{13,5},{17,9},{2... | collective-permute-start | bytes 1204232 | tf_op jit(solution)/shard_map/ppermute | solution.py:296
  174.4 5.9 %collective-permute-start.18 = (bf16[2,784,128]{2,1,0:T(8,128)(2,1)}, bf16[2,784,128]{2,1,0:T(8,128)(2,1)}, u32[]{:S(2)}, u32[]{:S(2)}) collective-permute-start(bf16[2,784,128]{2,1,0:T(8,128)(2,1)} %broadcast_select_fusion.5), channel_id=1, source_target_pairs={{8,0},{12,4},{16,8},{20,12},{24,16},{28,20},{9,1},{13,5},{17,9},{2... | collective-permute-start | bytes 1204232 | tf_op jit(solution)/shard_map/ppermute | solution.py:296
  180.2 15.2 %convolution_convert_fusion.g_ref = bf16[784,1280]{1,0:T(8,128)(2,1)S(1)} fusion(bf16[784,5120]{1,0:T(8,128)(2,1)} %all-gather.2.cloned.1.call-done, bf16[1280,5120]{1,0:T(8,128)(2,1)} %param.11), kind=kOutput, calls=%fused_computation | convolution fusion | flops 10277048320 | bytes 23142400 | tf_op jit(solution)/shard_map/dot_general | solution.py:350
  195.4 22.0 %shard_map.94 = (bf16[784,1280]{1,0:T(8,128)(2,1)}, bf16[784,1280]{1,0:T(8,128)(2,1)}, bf16[784,1280]{1,0:T(8,128)(2,1)}, bf16[2,2,784,128]{3,2,1,0:T(8,128)(2,1)S(1)}, bf16[2,2,784,128]{3,2,1,0:T(8,128)(2,1)}) custom-call(s32[4]{0:T(128)S(1)} %pad_add_fusion.flags_ref, bf16[784,1280]{1,0:T(8,128)(2,1)S(1)} %copy-done.7, ...), custom_call_target="tpu_custom_call" | custom-call | flops 9441116160 | bytes 6021120 | tf_op jit(solution)/shard_map/pallas_call | solution.py:162
  220.8 22.1 %shard_map.95 = (bf16[784,1280]{1,0:T(8,128)(2,1)}, bf16[784,1280]{1,0:T(8,128)(2,1)}, bf16[784,1280]{1,0:T(8,128)(2,1)}, bf16[2,2,784,128]{3,2,1,0:T(8,128)(2,1)S(1)}, bf16[2,2,784,128]{3,2,1,0:T(8,128)(2,1)S(1)}) custom-call(s32[4]{0:T(128)S(1)} %pad_add_fusion.flags_ref, ...), custom_call_target="tpu_custom_call", output_to_operand_aliasing={{0}: (8, {}), {1}: (9, {}), {2}: (10, {})} | custom-call | flops 9441116160 | bytes 6021120 | tf_op jit(solution)/shard_map/pallas_call | solution.py:162
  257.9 4.9 collective-permute-done.31
  267.2 13.7 %collective-permute-done.20.far_ref = bf16[2,784,128]{2,1,0:T(8,128)(2,1)S(1)} collective-permute-done((bf16[2,784,128]{2,1,0:T(8,128)(2,1)S(1)}, bf16[2,784,128]{2,1,0:T(8,128)(2,1)S(1)}, u32[]{:S(2)}, u32[]{:S(2)}) %collective-permute-start.20) | collective-permute-done | bytes 401440 | tf_op jit(solution)/shard_map/ppermute | solution.py:304
  280.9 21.8 %shard_map.96 = (bf16[784,1280]{1,0:T(8,128)(2,1)}, bf16[784,1280]{1,0:T(8,128)(2,1)}, bf16[784,1280]{1,0:T(8,128)(2,1)}, bf16[2,2,784,128]{3,2,1,0:T(8,128)(2,1)S(1)}, bf16[2,2,784,128]{3,2,1,0:T(8,128)(2,1)S(1)}) custom-call(s32[4]{0:T(128)S(1)} %pad_add_fusion.flags_ref, ...), custom_call_target="tpu_custom_call", output_to_operand_aliasing={{0}: (8, {}), {1}: (9, {}), {2}: (10, {})} | custom-call | flops 9441116160 | bytes 6021120 | tf_op jit(solution)/shard_map/pallas_call | solution.py:162
  307.6 21.7 %shard_map.97 = (bf16[784,1280]{1,0:T(8,128)(2,1)}, bf16[784,1280]{1,0:T(8,128)(2,1)}, bf16[784,1280]{1,0:T(8,128)(2,1)}, bf16[2,2,784,128]{3,2,1,0:T(8,128)(2,1)S(1)}, bf16[2,2,784,128]{3,2,1,0:T(8,128)(2,1)S(1)}) custom-call(s32[4]{0:T(128)S(1)} %pad_add_fusion.flags_ref, ...), custom_call_target="tpu_custom_call", output_to_operand_aliasing={{0}: (8, {}), {1}: (9, {}), {2}: (10, {})} | custom-call | flops 9441116160 | bytes 6021120 | tf_op jit(solution)/shard_map/pallas_call | solution.py:162
  337.3 21.9 %shard_map.98 = (bf16[784,1280]{1,0:T(8,128)(2,1)}, bf16[784,1280]{1,0:T(8,128)(2,1)}, bf16[784,1280]{1,0:T(8,128)(2,1)}, bf16[2,2,784,128]{3,2,1,0:T(8,128)(2,1)S(1)}, bf16[2,2,784,128]{3,2,1,0:T(8,128)(2,1)S(1)}) custom-call(s32[4]{0:T(128)S(1)} %pad_add_fusion.flags_ref, ...), custom_call_target="tpu_custom_call", output_to_operand_aliasing={{0}: (8, {}), {1}: (9, {}), {2}: (10, {})} | custom-call | flops 9441116160 | bytes 6021120 | tf_op jit(solution)/shard_map/pallas_call | solution.py:162
  363.1 5.3 %collective-permute-start.39 = (bf16[2,784,128]{2,1,0:T(8,128)(2,1)S(1)}, bf16[2,784,128]{2,1,0:T(8,128)(2,1)S(1)}, u32[]{:S(2)}, u32[]{:S(2)}) collective-permute-start(bf16[2,784,128]{2,1,0:T(8,128)(2,1)S(1)} %get-tuple-element.105), channel_id=1, source_target_pairs={{8,0},{12,4},{16,8},{20,12},{24,16},{28,20},{9,1},{13,5},{17,9},{2... | collective-permute-start | bytes 1204232 | tf_op jit(solution)/shard_map/ppermute | solution.py:332
  373.9 4.4 collective-permute-done.38
  382.0 9.9 %collective-permute-done.36.far_ref = bf16[2,784,128]{2,1,0:T(8,128)(2,1)} collective-permute-done((bf16[2,784,128]{2,1,0:T(8,128)(2,1)}, bf16[2,784,128]{2,1,0:T(8,128)(2,1)}, u32[]{:S(2)}, u32[]{:S(2)}) %collective-permute-start.36) | collective-permute-done | bytes 401440 | tf_op jit(solution)/shard_map/ppermute | solution.py:338
  394.6 13.6 %collective-permute-start.40 = (bf16[2,784,128]{2,1,0:T(8,128)(2,1)}, bf16[2,784,128]{2,1,0:T(8,128)(2,1)}, u32[]{:S(2)}, u32[]{:S(2)}) collective-permute-start(bf16[2,784,128]{2,1,0:T(8,128)(2,1)} %get-tuple-element.153.near_ref), channel_id=1, source_target_pairs={{4,0},{8,4},{12,8},{16,12},{20,16},{24,20},{28,24},{0,28},{5,1},{9... | collective-permute-start | bytes 1204232 | tf_op jit(solution)/shard_map/ppermute | solution.py:338
  413.5 13.9 %collective-permute-done.40.far_ref = bf16[2,784,128]{2,1,0:T(8,128)(2,1)} collective-permute-done((bf16[2,784,128]{2,1,0:T(8,128)(2,1)}, bf16[2,784,128]{2,1,0:T(8,128)(2,1)}, u32[]{:S(2)}, u32[]{:S(2)}) %collective-permute-start.40) | collective-permute-done | bytes 401440 | tf_op jit(solution)/shard_map/ppermute | solution.py:338
  430.6 13.2 %collective-permute-start.44 = (bf16[2,784,128]{2,1,0:T(8,128)(2,1)}, bf16[2,784,128]{2,1,0:T(8,128)(2,1)S(1)}, u32[]{:S(2)}, u32[]{:S(2)}) collective-permute-start(bf16[2,784,128]{2,1,0:T(8,128)(2,1)} %get-tuple-element.152.near_ref), channel_id=1, source_target_pairs={{4,0},{8,4},{12,8},{16,12},{20,16},{24,20},{28,24},{0,28},{5,1},{9... | collective-permute-start | bytes 1204232 | tf_op jit(solution)/shard_map/ppermute | solution.py:338
  446.4 10.4 %collective-permute-done.44.far_ref = bf16[2,784,128]{2,1,0:T(8,128)(2,1)S(1)} collective-permute-done((bf16[2,784,128]{2,1,0:T(8,128)(2,1)}, bf16[2,784,128]{2,1,0:T(8,128)(2,1)S(1)}, u32[]{:S(2)}, u32[]{:S(2)}) %collective-permute-start.44) | collective-permute-done | bytes 401440 | tf_op jit(solution)/shard_map/ppermute | solution.py:338
  463.6 4.4 collective-permute-done.50
  468.2 15.2 %collective-permute-start.52 = (bf16[2,784,128]{2,1,0:T(8,128)(2,1)S(1)}, bf16[2,784,128]{2,1,0:T(8,128)(2,1)S(1)}, u32[]{:S(2)}, u32[]{:S(2)}) collective-permute-start(bf16[2,784,128]{2,1,0:T(8,128)(2,1)S(1)} %add_convert_fusion.near_ref), channel_id=1, source_target_pairs={{4,0},{8,4},{12,8},{16,12},{20,16},{24,20},{28,24},{0,28},{5,1},{9... | collective-permute-start | bytes 1204232 | tf_op jit(solution)/shard_map/ppermute | solution.py:338
  (252 shorter events, 133.7 us)
Async XLA Ops:
  7.2 173.0 %all-gather.2.cloned.1.call-start = ((), (), s32[]{:S(2)}) async-start(), calls=%async_computation | async-start | bytes 10035200 | tf_op jit(solution)/shard_map/all_gather | solution.py:275
  14.2 37.2 %collective-permute-start.2 = (bf16[2,2,784,128]{3,2,1,0:T(8,128)(2,1)}, bf16[2,2,784,128]{3,2,1,0:T(8,128)(2,1)}, u32[]{:S(2)}, u32[]{:S(2)}) collective-permute-start(bf16[2,2,784,128]{3,2,1,0:T(8,128)(2,1)} %pad_maximum_fusion.2), channel_id=1, source_target_pairs={{0,4},{4,8},{8,12},{12,16},{16,20},{20,24},{24,28},{28,0},{1,5},{5... | collective-permute-start | bytes 2408456 | tf_op jit(solution)/shard_map/ppermute | solution.py:288
  35.9 24.1 %collective-permute-start.3 = (bf16[2,784,128]{2,1,0:T(8,128)(2,1)}, bf16[2,784,128]{2,1,0:T(8,128)(2,1)}, u32[]{:S(2)}, u32[]{:S(2)}) collective-permute-start(bf16[2,784,128]{2,1,0:T(8,128)(2,1)} %fusion.6), channel_id=1, source_target_pairs={{0,8},{4,12},{8,16},{12,20},{16,24},{20,28},{1,9},{5,13},{9,17},{1... | collective-permute-start | bytes 1204232 | tf_op jit(solution)/shard_map/ppermute | solution.py:295
  43.7 42.0 %collective-permute-start.1 = (bf16[2,2,784,128]{3,2,1,0:T(8,128)(2,1)}, bf16[2,2,784,128]{3,2,1,0:T(8,128)(2,1)}, u32[]{:S(2)}, u32[]{:S(2)}) collective-permute-start(bf16[2,2,784,128]{3,2,1,0:T(8,128)(2,1)} %pad_maximum_fusion), channel_id=1, source_target_pairs={{0,4},{4,8},{8,12},{12,16},{16,20},{20,24},{24,28},{28,0},{1,5},{5... | collective-permute-start | bytes 2408456 | tf_op jit(solution)/shard_map/ppermute | solution.py:288
  62.3 23.4 %collective-permute-start.5 = (bf16[2,784,128]{2,1,0:T(8,128)(2,1)S(1)}, bf16[2,784,128]{2,1,0:T(8,128)(2,1)S(1)}, u32[]{:S(2)}, u32[]{:S(2)}) collective-permute-start(bf16[2,784,128]{2,1,0:T(8,128)(2,1)S(1)} %get-tuple-element.127), channel_id=1, source_target_pairs={{0,8},{4,12},{8,16},{12,20},{16,24},{20,28},{1,9},{5,13},{9,17},{1... | collective-permute-start | bytes 1204232 | tf_op jit(solution)/shard_map/ppermute | solution.py:295
  68.4 32.1 %collective-permute-start.10 = (bf16[2,2,784,128]{3,2,1,0:T(8,128)(2,1)S(1)}, bf16[2,2,784,128]{3,2,1,0:T(8,128)(2,1)S(1)}, u32[]{:S(2)}, u32[]{:S(2)}) collective-permute-start(bf16[2,2,784,128]{3,2,1,0:T(8,128)(2,1)S(1)} %pad_maximum_fusion.4), channel_id=1, source_target_pairs={{0,4},{4,8},{8,12},{12,16},{16,20},{20,24},{24,28},{28,0},{1,5},{5... | collective-permute-start | bytes 2408456 | tf_op jit(solution)/shard_map/ppermute | solution.py:288
  88.2 23.4 %collective-permute-start.7 = (bf16[2,784,128]{2,1,0:T(8,128)(2,1)S(1)}, bf16[2,784,128]{2,1,0:T(8,128)(2,1)S(1)}, u32[]{:S(2)}, u32[]{:S(2)}) collective-permute-start(bf16[2,784,128]{2,1,0:T(8,128)(2,1)S(1)} %get-tuple-element.124), channel_id=1, source_target_pairs={{0,8},{4,12},{8,16},{12,20},{16,24},{20,28},{1,9},{5,13},{9,17},{1... | collective-permute-start | bytes 1204232 | tf_op jit(solution)/shard_map/ppermute | solution.py:295
  95.1 43.7 %collective-permute-start.9 = (bf16[2,2,784,128]{3,2,1,0:T(8,128)(2,1)}, bf16[2,2,784,128]{3,2,1,0:T(8,128)(2,1)}, u32[]{:S(2)}, u32[]{:S(2)}) collective-permute-start(bf16[2,2,784,128]{3,2,1,0:T(8,128)(2,1)} %pad_maximum_fusion.3), channel_id=1, source_target_pairs={{0,4},{4,8},{8,12},{12,16},{16,20},{20,24},{24,28},{28,0},{1,5},{5... | collective-permute-start | bytes 2408456 | tf_op jit(solution)/shard_map/ppermute | solution.py:288
  113.5 22.8 %collective-permute-start.11 = (bf16[2,784,128]{2,1,0:T(8,128)(2,1)}, bf16[2,784,128]{2,1,0:T(8,128)(2,1)}, u32[]{:S(2)}, u32[]{:S(2)}) collective-permute-start(bf16[2,784,128]{2,1,0:T(8,128)(2,1)} %get-tuple-element.121), channel_id=1, source_target_pairs={{0,8},{4,12},{8,16},{12,20},{16,24},{20,28},{1,9},{5,13},{9,17},{1... | collective-permute-start | bytes 1204232 | tf_op jit(solution)/shard_map/ppermute | solution.py:295
  165.8 29.6 %collective-permute-start.19 = (bf16[2,784,128]{2,1,0:T(8,128)(2,1)}, bf16[2,784,128]{2,1,0:T(8,128)(2,1)}, u32[]{:S(2)}, u32[]{:S(2)}) collective-permute-start(bf16[2,784,128]{2,1,0:T(8,128)(2,1)} %get-tuple-element.155.near_ref), channel_id=1, source_target_pairs={{0,4},{4,0},{8,12},{12,8},{16,20},{20,16},{24,28},{28,24},{1,5},{5... | collective-permute-start | bytes 1204232 | tf_op jit(solution)/shard_map/ppermute | solution.py:304
  165.9 54.9 %collective-permute-start.22 = (bf16[2,784,128]{2,1,0:T(8,128)(2,1)}, bf16[2,784,128]{2,1,0:T(8,128)(2,1)}, u32[]{:S(2)}, u32[]{:S(2)}) collective-permute-start(bf16[2,784,128]{2,1,0:T(8,128)(2,1)} %get-tuple-element.115.near_ref), channel_id=1, source_target_pairs={{0,4},{4,0},{8,12},{12,8},{16,20},{20,16},{24,28},{28,24},{1,5},{5... | collective-permute-start | bytes 1204232 | tf_op jit(solution)/shard_map/ppermute | solution.py:304
  173.1 77.3 %collective-permute-start.17 = (bf16[2,784,128]{2,1,0:T(8,128)(2,1)}, bf16[2,784,128]{2,1,0:T(8,128)(2,1)}, u32[]{:S(2)}, u32[]{:S(2)}) collective-permute-start(bf16[2,784,128]{2,1,0:T(8,128)(2,1)} %broadcast_select_fusion.5), channel_id=1, source_target_pairs={{0,8},{4,12},{8,16},{12,20},{16,24},{20,28},{1,9},{5,13},{9,17},{1... | collective-permute-start | bytes 1204232 | tf_op jit(solution)/shard_map/ppermute | solution.py:295
  174.4 77.3 %collective-permute-start.18 = (bf16[2,784,128]{2,1,0:T(8,128)(2,1)}, bf16[2,784,128]{2,1,0:T(8,128)(2,1)}, u32[]{:S(2)}, u32[]{:S(2)}) collective-permute-start(bf16[2,784,128]{2,1,0:T(8,128)(2,1)} %broadcast_select_fusion.5), channel_id=1, source_target_pairs={{8,0},{12,4},{16,8},{20,12},{24,16},{28,20},{9,1},{13,5},{17,9},{2... | collective-permute-start | bytes 1204232 | tf_op jit(solution)/shard_map/ppermute | solution.py:296
  217.4 48.5 %collective-permute-start.21 = (bf16[2,2,784,128]{3,2,1,0:T(8,128)(2,1)}, bf16[2,2,784,128]{3,2,1,0:T(8,128)(2,1)}, u32[]{:S(2)}, u32[]{:S(2)}) collective-permute-start(bf16[2,2,784,128]{3,2,1,0:T(8,128)(2,1)} %get-tuple-element.59), channel_id=1, source_target_pairs={{4,0},{8,4},{12,8},{16,12},{20,16},{24,20},{28,24},{0,28},{5,1},{9... | collective-permute-start | bytes 2408456 | tf_op jit(solution)/shard_map/ppermute | solution.py:315
  217.5 27.8 %collective-permute-start.27 = (bf16[2,784,128]{2,1,0:T(8,128)(2,1)S(1)}, bf16[2,784,128]{2,1,0:T(8,128)(2,1)S(1)}, u32[]{:S(2)}, u32[]{:S(2)}) collective-permute-start(bf16[2,784,128]{2,1,0:T(8,128)(2,1)S(1)} %select_bitcast_fusion.4), channel_id=1, source_target_pairs={{0,4},{4,0},{8,12},{12,8},{16,20},{20,16},{24,28},{28,24},{1,5},{5... | collective-permute-start | bytes 1204232 | tf_op jit(solution)/shard_map/ppermute | solution.py:316
  251.7 29.2 %collective-permute-start.20 = (bf16[2,784,128]{2,1,0:T(8,128)(2,1)S(1)}, bf16[2,784,128]{2,1,0:T(8,128)(2,1)S(1)}, u32[]{:S(2)}, u32[]{:S(2)}) collective-permute-start(bf16[2,784,128]{2,1,0:T(8,128)(2,1)S(1)} %get-tuple-element.58.near_ref), channel_id=1, source_target_pairs={{0,4},{4,0},{8,12},{12,8},{16,20},{20,16},{24,28},{28,24},{1,5},{5... | collective-permute-start | bytes 1204232 | tf_op jit(solution)/shard_map/ppermute | solution.py:304
  255.2 49.6 %collective-permute-start.25 = (bf16[2,784,128]{2,1,0:T(8,128)(2,1)S(1)}, bf16[2,784,128]{2,1,0:T(8,128)(2,1)S(1)}, u32[]{:S(2)}, u32[]{:S(2)}) collective-permute-start(bf16[2,784,128]{2,1,0:T(8,128)(2,1)S(1)} %copy-done.3), channel_id=1, source_target_pairs={{0,4},{4,0},{8,12},{12,8},{16,20},{20,16},{24,28},{28,24},{1,5},{5... | collective-permute-start | bytes 1204232 | tf_op jit(solution)/shard_map/ppermute | solution.py:304
  257.9 45.5 %collective-permute-start.26 = (bf16[2,2,784,128]{3,2,1,0:T(8,128)(2,1)S(1)}, bf16[2,2,784,128]{3,2,1,0:T(8,128)(2,1)S(1)}, u32[]{:S(2)}, u32[]{:S(2)}) collective-permute-start(bf16[2,2,784,128]{3,2,1,0:T(8,128)(2,1)S(1)} %copy-done.14), channel_id=1, source_target_pairs={{4,0},{8,4},{12,8},{16,12},{20,16},{24,20},{28,24},{0,28},{5,1},{9... | collective-permute-start | bytes 2408456 | tf_op jit(solution)/shard_map/ppermute | solution.py:315
  264.3 65.1 %collective-permute-start.32 = (bf16[2,784,128]{2,1,0:T(8,128)(2,1)S(1)}, bf16[2,784,128]{2,1,0:T(8,128)(2,1)S(1)}, u32[]{:S(2)}, u32[]{:S(2)}) collective-permute-start(bf16[2,784,128]{2,1,0:T(8,128)(2,1)S(1)} %get-tuple-element.109), channel_id=1, source_target_pairs={{8,0},{12,4},{16,8},{20,12},{24,16},{28,20},{9,1},{13,5},{17,9},{2... | collective-permute-start | bytes 1204232 | tf_op jit(solution)/shard_map/ppermute | solution.py:332
  265.9 63.5 %collective-permute-start.33 = (bf16[2,784,128]{2,1,0:T(8,128)(2,1)S(1)}, bf16[2,784,128]{2,1,0:T(8,128)(2,1)S(1)}, u32[]{:S(2)}, u32[]{:S(2)}) collective-permute-start(bf16[2,784,128]{2,1,0:T(8,128)(2,1)S(1)} %get-tuple-element.109), channel_id=1, source_target_pairs={{0,8},{4,12},{8,16},{12,20},{16,24},{20,28},{1,9},{5,13},{9,17},{1... | collective-permute-start | bytes 1204232 | tf_op jit(solution)/shard_map/ppermute | solution.py:332
  302.7 33.7 %collective-permute-start.23 = (bf16[2,784,128]{2,1,0:T(8,128)(2,1)S(1)}, bf16[2,784,128]{2,1,0:T(8,128)(2,1)S(1)}, u32[]{:S(2)}, u32[]{:S(2)}) collective-permute-start(bf16[2,784,128]{2,1,0:T(8,128)(2,1)S(1)} %select_select_fusion.3.near_ref), channel_id=1, source_target_pairs={{0,4},{4,0},{8,12},{12,8},{16,20},{20,16},{24,28},{28,24},{1,5},{5... | collective-permute-start | bytes 1204232 | tf_op jit(solution)/shard_map/ppermute | solution.py:304
  303.4 33.0 %collective-permute-start.24 = (bf16[2,2,784,128]{3,2,1,0:T(8,128)(2,1)S(1)}, bf16[2,2,784,128]{3,2,1,0:T(8,128)(2,1)S(1)}, u32[]{:S(2)}, u32[]{:S(2)}) collective-permute-start(bf16[2,2,784,128]{3,2,1,0:T(8,128)(2,1)S(1)} %get-tuple-element.69), channel_id=1, source_target_pairs={{4,0},{8,4},{12,8},{16,12},{20,16},{24,20},{28,24},{0,28},{5,1},{9... | collective-permute-start | bytes 2408456 | tf_op jit(solution)/shard_map/ppermute | solution.py:315
  304.8 24.5 %collective-permute-start.28 = (bf16[2,784,128]{2,1,0:T(8,128)(2,1)S(1)}, bf16[2,784,128]{2,1,0:T(8,128)(2,1)S(1)}, u32[]{:S(2)}, u32[]{:S(2)}) collective-permute-start(bf16[2,784,128]{2,1,0:T(8,128)(2,1)S(1)} %select_bitcast_fusion.3), channel_id=1, source_target_pairs={{0,4},{4,0},{8,12},{12,8},{16,20},{20,16},{24,28},{28,24},{1,5},{5... | collective-permute-start | bytes 1204232 | tf_op jit(solution)/shard_map/ppermute | solution.py:316
  329.3 31.0 %collective-permute-start.37 = (bf16[2,784,128]{2,1,0:T(8,128)(2,1)S(1)}, bf16[2,784,128]{2,1,0:T(8,128)(2,1)S(1)}, u32[]{:S(2)}, u32[]{:S(2)}) collective-permute-start(bf16[2,784,128]{2,1,0:T(8,128)(2,1)S(1)} %select_bitcast_fusion.1), channel_id=1, source_target_pairs={{0,4},{4,0},{8,12},{12,8},{16,20},{20,16},{24,28},{28,24},{1,5},{5... | collective-permute-start | bytes 1204232 | tf_op jit(solution)/shard_map/ppermute | solution.py:316
  331.2 29.1 %collective-permute-start.35 = (bf16[2,784,128]{2,1,0:T(8,128)(2,1)S(1)}, bf16[2,784,128]{2,1,0:T(8,128)(2,1)S(1)}, u32[]{:S(2)}, u32[]{:S(2)}) collective-permute-start(bf16[2,784,128]{2,1,0:T(8,128)(2,1)S(1)} %get-tuple-element.107), channel_id=1, source_target_pairs={{8,0},{12,4},{16,8},{20,12},{24,16},{28,20},{9,1},{13,5},{17,9},{2... | collective-permute-start | bytes 1204232 | tf_op jit(solution)/shard_map/ppermute | solution.py:332
  335.1 25.3 %collective-permute-start.34 = (bf16[2,784,128]{2,1,0:T(8,128)(2,1)S(1)}, bf16[2,784,128]{2,1,0:T(8,128)(2,1)S(1)}, u32[]{:S(2)}, u32[]{:S(2)}) collective-permute-start(bf16[2,784,128]{2,1,0:T(8,128)(2,1)S(1)} %get-tuple-element.107), channel_id=1, source_target_pairs={{0,8},{4,12},{8,16},{12,20},{16,24},{20,28},{1,9},{5,13},{9,17},{1... | collective-permute-start | bytes 1204232 | tf_op jit(solution)/shard_map/ppermute | solution.py:332
  370.0 57.3 %collective-permute-start.45 = (bf16[2,2,784,128]{3,2,1,0:T(8,128)(2,1)S(1)}, bf16[2,2,784,128]{3,2,1,0:T(8,128)(2,1)}, u32[]{:S(2)}, u32[]{:S(2)}) collective-permute-start(bf16[2,2,784,128]{3,2,1,0:T(8,128)(2,1)S(1)} %copy-done.10), channel_id=1, source_target_pairs={{4,0},{8,4},{12,8},{16,12},{20,16},{24,20},{28,24},{0,28},{5,1},{9... | collective-permute-start | bytes 2408456 | tf_op jit(solution)/shard_map/ppermute | solution.py:315
  394.6 32.8 %collective-permute-start.40 = (bf16[2,784,128]{2,1,0:T(8,128)(2,1)}, bf16[2,784,128]{2,1,0:T(8,128)(2,1)}, u32[]{:S(2)}, u32[]{:S(2)}) collective-permute-start(bf16[2,784,128]{2,1,0:T(8,128)(2,1)} %get-tuple-element.153.near_ref), channel_id=1, source_target_pairs={{4,0},{8,4},{12,8},{16,12},{20,16},{24,20},{28,24},{0,28},{5,1},{9... | collective-permute-start | bytes 1204232 | tf_op jit(solution)/shard_map/ppermute | solution.py:338
  408.2 48.7 %collective-permute-start.49 = (bf16[2,2,784,128]{3,2,1,0:T(8,128)(2,1)S(1)}, bf16[2,2,784,128]{3,2,1,0:T(8,128)(2,1)}, u32[]{:S(2)}, u32[]{:S(2)}) collective-permute-start(bf16[2,2,784,128]{3,2,1,0:T(8,128)(2,1)S(1)} %copy-done.12), channel_id=1, source_target_pairs={{4,0},{8,4},{12,8},{16,12},{20,16},{24,20},{28,24},{0,28},{5,1},{9... | collective-permute-start | bytes 2408456 | tf_op jit(solution)/shard_map/ppermute | solution.py:315
  430.6 26.3 %collective-permute-start.44 = (bf16[2,784,128]{2,1,0:T(8,128)(2,1)}, bf16[2,784,128]{2,1,0:T(8,128)(2,1)S(1)}, u32[]{:S(2)}, u32[]{:S(2)}) collective-permute-start(bf16[2,784,128]{2,1,0:T(8,128)(2,1)} %get-tuple-element.152.near_ref), channel_id=1, source_target_pairs={{4,0},{8,4},{12,8},{16,12},{20,16},{24,20},{28,24},{0,28},{5,1},{9... | collective-permute-start | bytes 1204232 | tf_op jit(solution)/shard_map/ppermute | solution.py:338
  459.5 33.9 %collective-permute-start.48 = (bf16[2,784,128]{2,1,0:T(8,128)(2,1)S(1)}, bf16[2,784,128]{2,1,0:T(8,128)(2,1)S(1)}, u32[]{:S(2)}, u32[]{:S(2)}) collective-permute-start(bf16[2,784,128]{2,1,0:T(8,128)(2,1)S(1)} %get-tuple-element.150.near_ref), channel_id=1, source_target_pairs={{4,0},{8,4},{12,8},{16,12},{20,16},{24,20},{28,24},{0,28},{5,1},{9... | collective-permute-start | bytes 1204232 | tf_op jit(solution)/shard_map/ppermute | solution.py:338
  468.2 29.3 %collective-permute-start.52 = (bf16[2,784,128]{2,1,0:T(8,128)(2,1)S(1)}, bf16[2,784,128]{2,1,0:T(8,128)(2,1)S(1)}, u32[]{:S(2)}, u32[]{:S(2)}) collective-permute-start(bf16[2,784,128]{2,1,0:T(8,128)(2,1)S(1)} %add_convert_fusion.near_ref), channel_id=1, source_target_pairs={{4,0},{8,4},{12,8},{16,12},{20,16},{24,20},{28,24},{0,28},{5,1},{9... | collective-permute-start | bytes 1204232 | tf_op jit(solution)/shard_map/ppermute | solution.py:338
  (85 other events, 1553.7 us)
Sparse Core Ops, SparseCore 0:
  9.6 57.1 all-gather.1

commit v2 on v1

--- a/solution.py
+++ b/solution.py
@@ -23,24 +23,31 @@
 
 
 def attn_kernel(
-    scale, rows, sub, flags_ref, q_ref, g_ref, ko_ref, vo_ref, near_ref, far_ref, prev_ref, *rest
+    scale, rows, sub, flags_ref, q_ref, g_ref, ko_ref, vo_ref, near_ref, far_ref, *rest
 ):
-    dq_ref, dko_ref, dvo_ref, dfirst_ref, dprev_ref = rest[-12:-7]
-    first_ref, kt_ref, s_ref, dp_ref, pds_ref, dk_acc, dv_acc = rest[-7:]
+    befores = rest[:4]
+    dq_ref, dko_ref, dvo_ref, dfirst_ref, dprev_ref = rest[-13:-8]
+    first_ref, prev_ref, kt_ref, s_ref, dp_ref, pds_ref, dk_acc, dv_acc = rest[-8:]
     log2e = scale * math.log2(math.e)
     is_near = pl.program_id(0) == flags_ref[3]
 
     @pl.when(is_near)
     def _():
-        first_ref[...] = near_ref[...]
+        first_ref[...] = near_ref[0]
 
     @pl.when(jnp.logical_not(is_near))
     def _():
-        first_ref[...] = far_ref[...]
+        first_ref[...] = far_ref[0]
+
+    for which, before_ref in enumerate(befores):
+
+        @pl.when((pl.program_id(0) == which // 2) & (flags_ref[3] == which % 2))
+        def _():
+            prev_ref[...] = before_ref[0]
 
     used = [None, flags_ref[0] > 0, flags_ref[1] > 0]
-    keys = [ko_ref, first_ref.at[0], prev_ref.at[0, 0]]
-    values = [vo_ref, first_ref.at[1], prev_ref.at[0, 1]]
+    keys = [ko_ref, first_ref.at[0], prev_ref.at[0]]
+    values = [vo_ref, first_ref.at[1], prev_ref.at[1]]
     for p in range(3):
         kt_ref[p] = keys[p][...].T
     dk_acc[...] = jnp.zeros_like(dk_acc)
@@ -145,7 +152,12 @@
     dprev_ref[0, 1] = dv_acc[2].astype(jnp.bfloat16)
 
 
-def attn_call(flags, q, g, ko, vo, near, far, prev, outs, heads, scale):
+def piece_spec(given):
+    stack, at = given
+    return pl.BlockSpec((1, *stack.shape[1:]), lambda h, f: (at, 0, 0, 0))
+
+
+def attn_call(flags, q, g, ko, vo, near, far, befores, outs, heads, scale):
     rows, width = q.shape
     count = len(heads)
     stride = heads[1] - heads[0] if count > 1 else 0
@@ -153,21 +165,22 @@
     sub = 112 if rows % 112 == 0 else 16
     column = pl.BlockSpec((rows, D_HEAD), lambda h, f: (0, base + stride * h))
     pair = pl.BlockSpec((1, 2, rows, D_HEAD), lambda h, f: (h, 0, 0, 0))
-    both = pl.BlockSpec((2, rows, D_HEAD), lambda h, f: (0, 0, 0))
+    given = [near, far, *befores]
     whole = jax.ShapeDtypeStruct((rows, width), jnp.bfloat16)
     piece = jax.ShapeDtypeStruct((count, 2, rows, D_HEAD), jnp.bfloat16)
     passed = [] if outs is None else list(outs)
-    aliases = {8 + i: i for i in range(len(passed))}
+    aliases = {11 + i: i for i in range(len(passed))}
     flops = 2 * 5 * 3 * rows * rows * D_HEAD * count
     return pl.pallas_call(
         functools.partial(attn_kernel, scale, rows, sub),
         grid_spec=pltpu.PrefetchScalarGridSpec(
             num_scalar_prefetch=1,
             grid=(count,),
-            in_specs=[column, column, column, column, both, both, pair]
+            in_specs=[column] * 4 + [piece_spec(x) for x in given]
             + [pl.BlockSpec(memory_space=pl.ANY)] * len(passed),
             out_specs=[column, column, column, pair, pair],
             scratch_shapes=[
+                pltpu.VMEM((2, rows, D_HEAD), jnp.bfloat16),
                 pltpu.VMEM((2, rows, D_HEAD), jnp.bfloat16),
                 pltpu.VMEM((3, D_HEAD, rows), jnp.bfloat16),
                 pltpu.VMEM((2, 3, rows, Q_TILE), jnp.float32),
@@ -187,33 +200,33 @@
             bytes_accessed=15 * rows * D_HEAD * 2 * count,
             transcendentals=3 * rows * rows * count,
         ),
-    )(flags, q, g, ko, vo, near, far, prev, *passed)
-
-
-def join_kernel(flags_ref, dk_ref, dv_ref, back_ref, near_ref, far_ref, dk_out, dv_out):
-    owner = flags_ref[2] > 0
-    is_near = pl.program_id(0) == flags_ref[3]
+    )(flags, q, g, ko, vo, *[x[0] for x in given], *passed)
+
+
+def join_kernel(flags_ref, dk_ref, dv_ref, *rest):
+    backs, total_ref, dk_out, dv_out = rest[:3], rest[3], rest[4], rest[5]
+    owner, side, head = flags_ref[2] > 0, flags_ref[3], pl.program_id(0)
     for i, (src, dst) in enumerate(((dk_ref, dk_out), (dv_ref, dv_out))):
-        total = jnp.where(is_near, near_ref[i], far_ref[i]).astype(jnp.float32)
-        part = src[...].astype(jnp.float32) + back_ref[0, i].astype(jnp.float32)
-        dst[...] = (part + jnp.where(owner, total, 0.0)).astype(jnp.bfloat16)
-
-
-def join_call(flags, dk, dv, back, near, far, heads):
+        back = jnp.where(side == 0, backs[1][0, i], backs[2][0, i])
+        back = jnp.where(head == 0, backs[0][0, i], back).astype(jnp.float32)
+        total = jnp.where(owner & (head == side), total_ref[0, i].astype(jnp.float32), 0.0)
+        dst[...] = (src[...].astype(jnp.float32) + back + total).astype(jnp.bfloat16)
+
+
+def join_call(flags, dk, dv, backs, total, heads):
     rows = dk.shape[0]
     count = len(heads)
     stride = heads[1] - heads[0] if count > 1 else 0
     base = heads[0]
     column = pl.BlockSpec((rows, D_HEAD), lambda h, f: (0, base + stride * h))
-    pair = pl.BlockSpec((1, 2, rows, D_HEAD), lambda h, f: (h, 0, 0, 0))
-    both = pl.BlockSpec((2, rows, D_HEAD), lambda h, f: (0, 0, 0))
+    given = [*backs, total]
     whole = jax.ShapeDtypeStruct(dk.shape, jnp.bfloat16)
     return pl.pallas_call(
         join_kernel,
         grid_spec=pltpu.PrefetchScalarGridSpec(
             num_scalar_prefetch=1,
             grid=(count,),
-            in_specs=[column, column, pair, both, both],
+            in_specs=[column, column] + [piece_spec(x) for x in given],
             out_specs=[column, column],
         ),
         out_shape=[whole, whole],
@@ -223,7 +236,7 @@
             bytes_accessed=8 * rows * D_HEAD * 2 * count,
             transcendentals=0,
         ),
-    )(flags, dk, dv, back, near, far)
+    )(flags, dk, dv, *[x[0] for x in given])
 
 
 def pick(index, candidates):
@@ -250,118 +263,165 @@
     prev_used = (me > 0) & (group_mask[me, prev_index] == 1) & (first != me - 1)
     lines = n // 2
     line, side = me // 2, me % 2
-    source = jnp.where(side == first % 2, first, (first + 1) % n) // 2
-    hops = jnp.abs(line - source)
+    low_side = side == 0
+    hops = (line - first // 2) % lines
+    beside = first == (me ^ 1)
     flags = jnp.stack(
         [(~owner).astype(jnp.int32), prev_used.astype(jnp.int32), owner.astype(jnp.int32), side]
     ).astype(jnp.int32)
     count = heads - heads // 2
     chunks = [tuple(range(c, heads, count)) for c in range(count)]
-    forward = [(i, (i + 1) % n) for i in range(n)]
-    backward = [(b, a) for a, b in forward]
-    higher = [(i, i + 2) for i in range(n - 2)]
-    lower = [(b, a) for a, b in higher]
-    across = [(i, i ^ 1) for i in range(n)]
-    blank = jnp.zeros((2, rows, D_HEAD), jnp.bfloat16)
+    routes = {
+        "swap": [(i, i ^ 1) for i in range(n)],
+        "up": [(i, (i + 2) % n) for i in range(n)],
+        "down": [((i + 2) % n, i) for i in range(n)],
+    }
+    lead = lines + 1
+    steps = count + lines - 2
+    f32, bf16 = jnp.float32, jnp.bfloat16
 
     def unit(h):
         cols = slice(h * D_HEAD, (h + 1) * D_HEAD)
         return jnp.stack([key_in[:, cols], value_in[:, cols]])
 
-    def half_of(chunk, which):
-        low, high = chunk[0], chunk[-1]
-        return jnp.where(side == which, low, high)
-
     gathered = lax.all_gather(layer_grad, "head", axis=1, tiled=True)
 
-    prevs, streams, held = [], [], []
-    nears, fars, sums = [], [], []
-    outs, attn_grad = None, None
-    first_parts, backs = [], []
-    shares, ends = [], []
-    totals, fetched = [], []
-
-    def send_prev(c):
-        units = jnp.stack([unit(h) for h in chunks[c]])
-        if c > 1:
-            units = after(units, prevs[c - 2])
-        got = lax.ppermute(units, "tm", forward)
-        prevs.append(got)
-        streams.append(jnp.where(owner, half_of(units, 0), half_of(got, 0)))
-
-    def spread(s):
-        fresh = streams[s] if s < count else blank
-        sent = jnp.where(hops == 0, fresh, held[-1]) if held else fresh
-        up = lax.ppermute(sent, "tm", higher)
-        down = lax.ppermute(sent, "tm", lower)
-        held.append(jnp.where(line > source, up, down))
-
-    def exchange(c):
-        near = pick(hops, {0: streams[c], **{d: held[c + d - 1] for d in range(1, lines)}})
-        if c > 1:
-            near = after(near, first_parts[c - 2])
-        nears.append(near)
-        fars.append(lax.ppermute(near, "tm", across))
-
-    def attend(c):
-        nonlocal outs
-        arrived = after(prevs[c], backs[c - 2]) if c > 1 else prevs[c]
-        done = attn_call(
-            flags, query_in, attn_grad, key_in, value_in, nears[c], fars[c], arrived,
-            outs, chunks[c], scale,
-        )
-        outs = done[:3]
-        first_parts.append(done[3])
-        backs.append(lax.ppermute(done[4], "tm", backward))
-        shares.append(lax.ppermute(half_of(done[3], 1), "tm", across))
-
-    def gather_up(s):
-        for c in range(len(sums), min(s + 1, count)):
-            mine = half_of(first_parts[c], 0).astype(jnp.float32)
-            sums.append(mine + shares[c].astype(jnp.float32))
-        low = max(0, s - lines + 1)
-        total = pick(s - lines + 1 + hops, {c: sums[c] for c in range(low, min(s, count - 1) + 1)})
-        if ends:
-            up, down = ends[-1]
-            total += jnp.where(line > source, down, up).astype(jnp.float32)
-        sent = total.astype(jnp.bfloat16)
-        if s >= lines:
-            sent = after(sent, fetched[s - lines])
-        if s >= count:
-            sent = after(sent, backs[min(s - 2, count - 1)])
-        ends.append((lax.ppermute(sent, "tm", higher), lax.ppermute(sent, "tm", lower)))
-        c = s - lines + 2
-        if c >= 0:
-            up, down = ends[-1]
-            whole = sums[c] + up.astype(jnp.float32) + down.astype(jnp.float32)
-            totals.append(whole.astype(jnp.bfloat16))
-            fetched.append(lax.ppermute(totals[-1], "tm", backward))
-
-    steps = count + lines - 2
-    lead = lines + 1
-    for k in range(lead + count + steps + 2):
-        if k < count:
-            send_prev(k)
-        if 0 <= k - 1 < steps:
-            spread(k - 1)
-        if 0 <= k - lines < count:
-            exchange(k - lines)
-        if k == lead:
+    sent, came, place = {}, {}, {}
+
+    def out(kind, name, k):
+        return sent[kind, k], place[name, k]
+
+    def into(kind, name, k):
+        return came[kind, k], place[name, k]
+
+    def read(piece):
+        return piece[0][piece[1]]
+
+    def has(c):
+        return 0 <= c < count
+
+    own = [(unit(pair[0]), unit(pair[-1])) for pair in chunks]
+    firsts, prevs, sums, totals = {}, {}, {}, {}
+    outs, attn_grad, done = None, None, []
+
+    def swap_parts(k):
+        parts = {}
+        if has(k):
+            parts["a"] = own[k][0]
+        if has(k) and has(k - 2):
+            parts["b"] = jnp.where(low_side, own[k][1], read(into("up", "next", k - 1)))
+        elif has(k):
+            parts["b"] = own[k][1]
+        elif has(k - 2):
+            parts["b"] = read(into("up", "next", k - 1))
+        c = k - lines
+        if has(c):
+            choice = {0: read(out("up", "stream", c + 1))}
+            choice.update({d: read(into("up", "stream", c + d)) for d in range(1, lines)})
+            parts["first"] = pick(hops, choice)
+        c, e = k - lead - 1, k - lead - lines - 1
+        if has(c):
+            parts["share"] = jnp.where(low_side, firsts[c][-1], firsts[c][0])
+        if has(e):
+            carried = read(into("down", "sum", k - 1)).astype(f32)
+            total = sums[e].astype(f32) + carried
+            totals[e] = total.astype(bf16)
+            extra = jnp.where(beside, total, 0.0)
+            relay = (read(into("down", "back", lead + 2 + e)).astype(f32) + extra).astype(bf16)
+            parts["back_a"] = jnp.where(low_side, relay, prevs[e][0])
+            high_b = (prevs[e][-1].astype(f32) + extra).astype(bf16)
+            parts["back_b"] = jnp.where(low_side, prevs[c][-1], high_b) if has(c) else high_b
+        elif has(c):
+            parts["back_b"] = prevs[c][-1]
+        return parts
+
+    def up_parts(k):
+        parts = {}
+        c = k - 1
+        if has(c):
+            parts["next"] = jnp.where(low_side, read(into("swap", "a", c)), own[c][1])
+            fresh = jnp.where(
+                low_side,
+                jnp.where(owner, own[c][0], read(into("swap", "a", c))),
+                jnp.where(owner, own[c][1], read(into("swap", "b", c))),
+            )
+            parts["stream"] = fresh
+        if 0 < c < steps:
+            passed = read(into("up", "stream", k - 1))
+            parts["stream"] = jnp.where(hops == 0, fresh, passed) if has(c) else passed
+        return parts
+
+    def down_parts(k):
+        parts = {}
+        s = k - lead - 2
+        if has(s):
+            mine = jnp.where(low_side, firsts[s][0], firsts[s][-1]).astype(f32)
+            share = read(into("swap", "share", k - 1)).astype(f32)
+            sums[s] = after((mine + share).astype(bf16))
+            parts["back"] = jnp.where(
+                low_side, prevs[s][0], read(into("swap", "back_b", k - 1))
+            )
+        if 0 <= s < steps:
+            low = max(0, s - lines + 1)
+            at = s - lines + 1 + hops
+            total = pick(at, {c: sums[c] for c in range(low, min(s, count - 1) + 1)})
+            if s > 0:
+                carried = read(into("down", "sum", k - 1)).astype(f32)
+                carried = jnp.where(hops == lines - 1, 0.0, carried)
+                total = (total.astype(f32) + carried).astype(bf16)
+            parts["sum"] = total
+        return parts
+
+    for k in range(lead + count + lines + 2):
+        stacks = {}
+        for kind, parts in (
+            ("swap", swap_parts(k)), ("up", up_parts(k)), ("down", down_parts(k))
+        ):
+            for i, name in enumerate(parts):
+                place[name, k] = i
+            if parts:
+                stacks[kind] = jnp.stack(list(parts.values()))
+        kinds = list(stacks)
+        if kinds:
+            held = lax.optimization_barrier((*[stacks[x] for x in kinds], *done))
+            for kind, stack in zip(kinds, held):
+                sent[kind, k] = stack
+                came[kind, k] = lax.ppermute(stack, "tm", routes[kind])
+        done = []
+        ready = [sent[x, k] for x in kinds]
+        if k == lines - 1:
             attn_grad = lax.dot_general(
-                after(gathered, nears[0]),
-                out_weight,
-                (((1,), (1,)), ((), ())),
-                preferred_element_type=jnp.float32,
-            ).astype(jnp.bfloat16)
-        if 0 <= k - lead < count:
-            attend(k - lead)
-        if 0 <= k - lead - 1 < steps:
-            gather_up(k - lead - 1)
-
-    dq, dk, dv = outs
-    for c, pair in enumerate(chunks):
-        dk, dv = join_call(flags, dk, dv, backs[c], totals[c], fetched[c], pair)
-    return dq, dk, dv
+                after(gathered, *ready), out_weight, (((1,), (1,)), ((), ())),
+                preferred_element_type=f32,
+            ).astype(bf16)
+            done.append(attn_grad)
+        c = k - lead
+        if has(c):
+            befores = (
+                into("up", "next", c + 1), into("swap", "a", c),
+                into("swap", "b", c + 2), into("swap", "b", c),
+            )
+            results = attn_call(
+                after(flags, *ready), query_in, attn_grad, key_in, value_in,
+                out("swap", "first", c + lines), into("swap", "first", c + lines),
+                befores, outs, chunks[c], scale,
+            )
+            outs, firsts[c], prevs[c] = results[:3], results[3], results[4]
+            done.append(results[3])
+        c = k - lead - lines - 2
+        if has(c):
+            returned = (
+                into("swap", "back_a", k - 1), into("swap", "back_b", k - 1),
+                into("down", "back", lead + 2 + c),
+            )
+            dq, dk, dv = outs
+            dk, dv = join_call(
+                after(flags, *ready) if ready else flags, dk, dv, returned,
+                (totals[c][None], 0), chunks[c],
+            )
+            outs = (dq, dk, dv)
+            done.append(dk)
+    return tuple(outs)
 
 
 def solution(mesh):

time: 517 us -> 419 us (0.81)
  the two profiles are of different devices: /device:TPU:26 before, /device:TPU:0 now
where the time goes in v2:
time: 419 us; the launch traced here: 412 us
  waiting for transfers between devices  154 us (37%)
  Pallas kernels  127 us (30%)
  other arithmetic  47 us (11%)
  starting transfers between devices  30.2 us (7%)
  local copies, waits for them, and re-layouts  21.5 us (5%)
  matrix products  16.3 us (4%)
  between operations  16.3 us (4%)
    ppermute x29, waiting for transfers between devices, local(): came[kind, k] = lax.ppermute(stack, 'tm', routes[kind])  153 us
    pallas_call x5, Pallas kernels, attn_call(): pl.pallas_call(functools.partial(attn_kernel, scale, rows, sub), grid_spe...  109 us
    ppermute x29, starting transfers between devices, local(): came[kind, k] = lax.ppermute(stack, 'tm', routes[kind])  30.1 us
    another operation x37, other arithmetic, local(): stacks[kind] = jnp.stack(list(parts.values()))  24 us
    pallas_call x5, Pallas kernels, join_call(): pl.pallas_call(join_kernel, grid_spec=pltpu.PrefetchScalarGridSpec(num_sc...  17.5 us
    unnamed x126, local copies, waits for them, and re-layouts  17.2 us
    dot_general x1, matrix products, local(): lax.dot_general(after(gathered, *ready), out_weight, (((1,), (1,)), ((),...  16.3 us
  transfers between devices with their start and end apart: 30, of which 16 were waited for; matrix products, arithmetic and copies ran while one was open for 8% of the time, Pallas kernels for 30%

profile of v2, /device:TPU:0, one launch (start us, length us, event | category | flops | bytes accessed | tf_op | source)
XLA Modules:
  0.0 411.8 jit_solution(1734783678561636069)
XLA Ops:
  12.6 3.0 collective-permute-start
  18.4 15.1 %collective-permute-done.rest_1_.rest_3_ = bf16[2,2,784,128]{3,2,1,0:T(8,128)(2,1)S(1)} collective-permute-done((bf16[2,2,784,128]{3,2,1,0:T(8,128)(2,1)S(1)}, bf16[2,2,784,128]{3,2,1,0:T(8,128)(2,1)S(1)}, u32[]{:S(2)}, u32[]{:S(2)}) %collective-permute-start) | collective-permute-done | bytes 802848 | tf_op jit(solution)/shard_map/ppermute | solution.py:389
  38.9 15.0 %collective-permute-done.2.rest_1_.rest_3_ = bf16[2,2,784,128]{3,2,1,0:T(8,128)(2,1)S(1)} collective-permute-done((bf16[2,2,784,128]{3,2,1,0:T(8,128)(2,1)}, bf16[2,2,784,128]{3,2,1,0:T(8,128)(2,1)S(1)}, u32[]{:S(2)}, u32[]{:S(2)}) %collective-permute-start.2) | collective-permute-done | bytes 802848 | tf_op jit(solution)/shard_map/ppermute | solution.py:389
  53.9 2.8 collective-permute-done.1.rest_0_
  59.5 18.7 %collective-permute-done.3.rest_0_ = bf16[2,2,784,128]{3,2,1,0:T(8,128)(2,1)S(1)} collective-permute-done((bf16[2,2,784,128]{3,2,1,0:T(8,128)(2,1)S(1)}, bf16[2,2,784,128]{3,2,1,0:T(8,128)(2,1)S(1)}, u32[]{:S(2)}, u32[]{:S(2)}) %collective-permute-start.3) | collective-permute-done | bytes 802848 | tf_op jit(solution)/shard_map/ppermute | solution.py:389
  83.0 17.0 %collective-permute-done.5.rest_0_ = bf16[2,2,784,128]{3,2,1,0:T(8,128)(2,1)S(1)} collective-permute-done((bf16[2,2,784,128]{3,2,1,0:T(8,128)(2,1)}, bf16[2,2,784,128]{3,2,1,0:T(8,128)(2,1)S(1)}, u32[]{:S(2)}, u32[]{:S(2)}) %collective-permute-start.5) | collective-permute-done | bytes 802848 | tf_op jit(solution)/shard_map/ppermute | solution.py:389
  104.4 16.3 %convolution_convert_fusion.g_ref = bf16[784,1280]{1,0:T(8,128)(2,1)} fusion(bf16[784,5120]{1,0:T(8,128)(2,1)} %all-gather.2.cloned.1.call-done, bf16[1280,5120]{1,0:T(8,128)(2,1)} %param.11), kind=kOutput, calls=%fused_computation | convolution fusion | flops 10277048320 | bytes 23142400 | tf_op jit(solution)/shard_map/dot_general | solution.py:393
  123.8 15.8 %collective-permute-done.7.rest_0_ = bf16[2,2,784,128]{3,2,1,0:T(8,128)(2,1)S(1)} collective-permute-done((bf16[2,2,784,128]{3,2,1,0:T(8,128)(2,1)}, bf16[2,2,784,128]{3,2,1,0:T(8,128)(2,1)S(1)}, u32[]{:S(2)}, u32[]{:S(2)}) %collective-permute-start.7) | collective-permute-done | bytes 802848 | tf_op jit(solution)/shard_map/ppermute | solution.py:389
  140.7 4.8 %collective-permute-done.8.far_ref.rest_2_.rest_1_.rest_3_ = bf16[3,2,784,128]{3,2,1,0:T(8,128)(2,1)} collective-permute-done((bf16[3,2,784,128]{3,2,1,0:T(8,128)(2,1)}, bf16[3,2,784,128]{3,2,1,0:T(8,128)(2,1)}, u32[]{:S(2)}, u32[]{:S(2)}) %collective-permute-start.8) | collective-permute-done | bytes 1204256 | tf_op jit(solution)/shard_map/ppermute | solution.py:389
  149.8 21.9 %shard_map.94 = (bf16[784,1280]{1,0:T(8,128)(2,1)}, bf16[784,1280]{1,0:T(8,128)(2,1)}, bf16[784,1280]{1,0:T(8,128)(2,1)}, bf16[2,2,784,128]{3,2,1,0:T(8,128)(2,1)S(1)}, bf16[2,2,784,128]{3,2,1,0:T(8,128)(2,1)S(1)}) custom-call(s32[4]{0:T(128)S(1)} %pad_add_fusion.flags_ref, bf16[784,1280]{1,0:T(8,128)(2,1)S(1)} %copy-done.25, ...), custom_call_target="tpu_custom_call" | custom-call | flops 9441116160 | bytes 6021120 | tf_op jit(solution)/shard_map/pallas_call | solution.py:174
  171.9 2.2 fusion.70
  183.3 21.8 %shard_map.95 = (bf16[784,1280]{1,0:T(8,128)(2,1)}, bf16[784,1280]{1,0:T(8,128)(2,1)}, bf16[784,1280]{1,0:T(8,128)(2,1)}, bf16[2,2,784,128]{3,2,1,0:T(8,128)(2,1)S(1)}, bf16[2,2,784,128]{3,2,1,0:T(8,128)(2,1)S(1)}) custom-call(s32[4]{0:T(128)S(1)} %pad_add_fusion.flags_ref, ...), custom_call_target="tpu_custom_call", output_to_operand_aliasing={{0}: (11, {}), {1}: (12, {}), {2}: (13, {})} | custom-call | flops 9441116160 | bytes 6021120 | tf_op jit(solution)/shard_map/pallas_call | solution.py:174
  210.8 2.5 collective-permute-start.13
  216.2 22.0 %shard_map.96 = (bf16[784,1280]{1,0:T(8,128)(2,1)}, bf16[784,1280]{1,0:T(8,128)(2,1)}, bf16[784,1280]{1,0:T(8,128)(2,1)}, bf16[2,2,784,128]{3,2,1,0:T(8,128)(2,1)S(1)}, bf16[2,2,784,128]{3,2,1,0:T(8,128)(2,1)S(1)}) custom-call(s32[4]{0:T(128)S(1)} %pad_add_fusion.flags_ref, ...), custom_call_target="tpu_custom_call", output_to_operand_aliasing={{0}: (11, {}), {1}: (12, {}), {2}: (13, {})} | custom-call | flops 9441116160 | bytes 6021120 | tf_op jit(solution)/shard_map/pallas_call | solution.py:174
  240.4 2.2 collective-permute-start.17
  243.4 21.8 %shard_map.97 = (bf16[784,1280]{1,0:T(8,128)(2,1)}, bf16[784,1280]{1,0:T(8,128)(2,1)}, bf16[784,1280]{1,0:T(8,128)(2,1)}, bf16[2,2,784,128]{3,2,1,0:T(8,128)(2,1)S(1)}, bf16[2,2,784,128]{3,2,1,0:T(8,128)(2,1)S(1)}) custom-call(s32[4]{0:T(128)S(1)} %pad_add_fusion.flags_ref, ...), custom_call_target="tpu_custom_call", output_to_operand_aliasing={{0}: (11, {}), {1}: (12, {}), {2}: (13, {})} | custom-call | flops 9441116160 | bytes 6021120 | tf_op jit(solution)/shard_map/pallas_call | solution.py:174
  266.6 2.4 collective-permute-start.18
  270.2 22.0 %shard_map.98 = (bf16[784,1280]{1,0:T(8,128)(2,1)}, bf16[784,1280]{1,0:T(8,128)(2,1)}, bf16[784,1280]{1,0:T(8,128)(2,1)}, bf16[2,2,784,128]{3,2,1,0:T(8,128)(2,1)S(1)}, bf16[2,2,784,128]{3,2,1,0:T(8,128)(2,1)S(1)}) custom-call(s32[4]{0:T(128)S(1)} %pad_add_fusion.flags_ref, ...), custom_call_target="tpu_custom_call", output_to_operand_aliasing={{0}: (11, {}), {1}: (12, {}), {2}: (13, {})} | custom-call | flops 9441116160 | bytes 6021120 | tf_op jit(solution)/shard_map/pallas_call | solution.py:174
  297.9 12.4 %collective-permute-done.20.rest_2_ = bf16[2,2,784,128]{3,2,1,0:T(8,128)(2,1)} collective-permute-done((bf16[2,2,784,128]{3,2,1,0:T(8,128)(2,1)}, bf16[2,2,784,128]{3,2,1,0:T(8,128)(2,1)}, u32[]{:S(2)}, u32[]{:S(2)}) %collective-permute-start.20) | collective-permute-done | bytes 802848 | tf_op jit(solution)/shard_map/ppermute | solution.py:389
  311.8 6.1 %collective-permute-done.21.rest_0_.rest_1_ = bf16[3,2,784,128]{3,2,1,0:T(8,128)(2,1)} collective-permute-done((bf16[3,2,784,128]{3,2,1,0:T(8,128)(2,1)}, bf16[3,2,784,128]{3,2,1,0:T(8,128)(2,1)}, u32[]{:S(2)}, u32[]{:S(2)}) %collective-permute-start.21) | collective-permute-done | bytes 1204256 | tf_op jit(solution)/shard_map/ppermute | solution.py:389
  319.1 2.4 fusion.31
  326.0 3.6 shard_map.99
  329.6 10.8 %collective-permute-done.22.rest_2_ = bf16[2,2,784,128]{3,2,1,0:T(8,128)(2,1)} collective-permute-done((bf16[2,2,784,128]{3,2,1,0:T(8,128)(2,1)}, bf16[2,2,784,128]{3,2,1,0:T(8,128)(2,1)}, u32[]{:S(2)}, u32[]{:S(2)}) %collective-permute-start.22) | collective-permute-done | bytes 802848 | tf_op jit(solution)/shard_map/ppermute | solution.py:389
  344.3 3.4 shard_map.100
  347.7 7.9 %collective-permute-done.23 = bf16[1,2,784,128]{3,2,1,0:T(8,128)(2,1)S(1)} collective-permute-done((bf16[1,2,784,128]{3,2,1,0:T(8,128)(2,1)S(1)}, bf16[1,2,784,128]{3,2,1,0:T(8,128)(2,1)S(1)}, u32[]{:S(2)}, u32[]{:S(2)}) %collective-permute-start.23) | collective-permute-done | bytes 401440 | tf_op jit(solution)/shard_map/ppermute | solution.py:389
  362.3 4.5 %collective-permute-done.25 = bf16[1,2,784,128]{3,2,1,0:T(8,128)(2,1)S(1)} collective-permute-done((bf16[1,2,784,128]{3,2,1,0:T(8,128)(2,1)S(1)}, bf16[1,2,784,128]{3,2,1,0:T(8,128)(2,1)S(1)}, u32[]{:S(2)}, u32[]{:S(2)}) %collective-permute-start.25) | collective-permute-done | bytes 401440 | tf_op jit(solution)/shard_map/ppermute | solution.py:389
  370.0 11.1 %collective-permute-done.26.rest_0_.rest_1_ = bf16[2,2,784,128]{3,2,1,0:T(8,128)(2,1)S(1)} collective-permute-done((bf16[2,2,784,128]{3,2,1,0:T(8,128)(2,1)S(1)}, bf16[2,2,784,128]{3,2,1,0:T(8,128)(2,1)S(1)}, u32[]{:S(2)}, u32[]{:S(2)}) %collective-permute-start.26) | collective-permute-done | bytes 802848 | tf_op jit(solution)/shard_map/ppermute | solution.py:389
  382.0 3.6 shard_map.101
  385.7 6.1 %collective-permute-done.27.rest_0_.rest_1_ = bf16[2,2,784,128]{3,2,1,0:T(8,128)(2,1)S(1)} collective-permute-done((bf16[2,2,784,128]{3,2,1,0:T(8,128)(2,1)}, bf16[2,2,784,128]{3,2,1,0:T(8,128)(2,1)S(1)}, u32[]{:S(2)}, u32[]{:S(2)}) %collective-permute-start.27) | collective-permute-done | bytes 802848 | tf_op jit(solution)/shard_map/ppermute | solution.py:389
  392.7 3.4 shard_map.102
  396.2 4.3 %collective-permute-done.28.rest_0_.rest_1_ = bf16[2,2,784,128]{3,2,1,0:T(8,128)(2,1)S(1)} collective-permute-done((bf16[2,2,784,128]{3,2,1,0:T(8,128)(2,1)S(1)}, bf16[2,2,784,128]{3,2,1,0:T(8,128)(2,1)S(1)}, u32[]{:S(2)}, u32[]{:S(2)}) %collective-permute-start.28) | collective-permute-done | bytes 802848 | tf_op jit(solution)/shard_map/ppermute | solution.py:389
  401.4 3.4 shard_map.103
  (241 shorter events, 85.2 us)
Async XLA Ops:
  7.2 97.2 %all-gather.2.cloned.1.call-start = ((), (), s32[]{:S(2)}) async-start(), calls=%async_computation | async-start | bytes 10035200 | tf_op jit(solution)/shard_map/all_gather | solution.py:287
  12.5 65.8 %copy-start.47 = (bf16[1,1,784,128]{3,2,1,0:T(8,128)(2,1)}, bf16[1,1,784,128]{3,2,1,0:T(8,128)(2,1)S(1)}, u32[]{:S(2)}) copy-start(bf16[1,1,784,128]{3,2,1,0:T(8,128)(2,1)S(1)} %get-tuple-element.164) | copy-start | bytes 602116
  12.6 20.9 %collective-permute-start = (bf16[2,2,784,128]{3,2,1,0:T(8,128)(2,1)S(1)}, bf16[2,2,784,128]{3,2,1,0:T(8,128)(2,1)S(1)}, u32[]{:S(2)}, u32[]{:S(2)}) collective-permute-start(bf16[2,2,784,128]{3,2,1,0:T(8,128)(2,1)S(1)} %pad_maximum_fusion.6), channel_id=1, source_target_pairs={{0,4},{4,0},{8,12},{12,8},{16,20},{20,16},{24,28},{28,24},{1,5},{5... | collective-permute-start | bytes 2408456 | tf_op jit(solution)/shard_map/ppermute | solution.py:389
  34.5 19.4 %collective-permute-start.2 = (bf16[2,2,784,128]{3,2,1,0:T(8,128)(2,1)}, bf16[2,2,784,128]{3,2,1,0:T(8,128)(2,1)S(1)}, u32[]{:S(2)}, u32[]{:S(2)}) collective-permute-start(bf16[2,2,784,128]{3,2,1,0:T(8,128)(2,1)} %pad_maximum_fusion.5), channel_id=1, source_target_pairs={{0,4},{4,0},{8,12},{12,8},{16,20},{20,16},{24,28},{28,24},{1,5},{5... | collective-permute-start | bytes 2408456 | tf_op jit(solution)/shard_map/ppermute | solution.py:389
  36.2 20.4 %collective-permute-start.1 = (bf16[2,2,784,128]{3,2,1,0:T(8,128)(2,1)S(1)}, bf16[2,2,784,128]{3,2,1,0:T(8,128)(2,1)S(1)}, u32[]{:S(2)}, u32[]{:S(2)}) collective-permute-start(bf16[2,2,784,128]{3,2,1,0:T(8,128)(2,1)S(1)} %pad_maximum_fusion.7), channel_id=1, source_target_pairs={{0,8},{4,12},{8,16},{12,20},{16,24},{20,28},{24,0},{28,4},{1,9},{5... | collective-permute-start | bytes 2408456 | tf_op jit(solution)/shard_map/ppermute | solution.py:389
  58.7 19.6 %collective-permute-start.3 = (bf16[2,2,784,128]{3,2,1,0:T(8,128)(2,1)S(1)}, bf16[2,2,784,128]{3,2,1,0:T(8,128)(2,1)S(1)}, u32[]{:S(2)}, u32[]{:S(2)}) collective-permute-start(bf16[2,2,784,128]{3,2,1,0:T(8,128)(2,1)S(1)} %pad_maximum_fusion.9), channel_id=1, source_target_pairs={{0,8},{4,12},{8,16},{12,20},{16,24},{20,28},{24,0},{28,4},{1,9},{5... | collective-permute-start | bytes 2408456 | tf_op jit(solution)/shard_map/ppermute | solution.py:389
  58.7 19.5 %collective-permute-start.4 = (bf16[2,2,784,128]{3,2,1,0:T(8,128)(2,1)S(1)}, bf16[2,2,784,128]{3,2,1,0:T(8,128)(2,1)S(1)}, u32[]{:S(2)}, u32[]{:S(2)}) collective-permute-start(bf16[2,2,784,128]{3,2,1,0:T(8,128)(2,1)S(1)} %pad_maximum_fusion.8), channel_id=1, source_target_pairs={{0,4},{4,0},{8,12},{12,8},{16,20},{20,16},{24,28},{28,24},{1,5},{5... | collective-permute-start | bytes 2408456 | tf_op jit(solution)/shard_map/ppermute | solution.py:389
  81.1 18.8 %collective-permute-start.5 = (bf16[2,2,784,128]{3,2,1,0:T(8,128)(2,1)}, bf16[2,2,784,128]{3,2,1,0:T(8,128)(2,1)S(1)}, u32[]{:S(2)}, u32[]{:S(2)}) collective-permute-start(bf16[2,2,784,128]{3,2,1,0:T(8,128)(2,1)} %pad_maximum_fusion.11), channel_id=1, source_target_pairs={{0,8},{4,12},{8,16},{12,20},{16,24},{20,28},{24,0},{28,4},{1,9},{5... | collective-permute-start | bytes 2408456 | tf_op jit(solution)/shard_map/ppermute | solution.py:389
  81.1 18.8 %collective-permute-start.6 = (bf16[2,2,784,128]{3,2,1,0:T(8,128)(2,1)}, bf16[2,2,784,128]{3,2,1,0:T(8,128)(2,1)S(1)}, u32[]{:S(2)}, u32[]{:S(2)}) collective-permute-start(bf16[2,2,784,128]{3,2,1,0:T(8,128)(2,1)} %pad_maximum_fusion.10), channel_id=1, source_target_pairs={{0,4},{4,0},{8,12},{12,8},{16,20},{20,16},{24,28},{28,24},{1,5},{5... | collective-permute-start | bytes 2408456 | tf_op jit(solution)/shard_map/ppermute | solution.py:389
  120.7 24.8 %collective-permute-start.8 = (bf16[3,2,784,128]{3,2,1,0:T(8,128)(2,1)}, bf16[3,2,784,128]{3,2,1,0:T(8,128)(2,1)}, u32[]{:S(2)}, u32[]{:S(2)}) collective-permute-start(bf16[3,2,784,128]{3,2,1,0:T(8,128)(2,1)} %pad_maximum_fusion.1.near_ref), channel_id=1, source_target_pairs={{0,4},{4,0},{8,12},{12,8},{16,20},{20,16},{24,28},{28,24},{1,5},{5... | collective-permute-start | bytes 3612680 | tf_op jit(solution)/shard_map/ppermute | solution.py:389
  121.8 17.8 %collective-permute-start.7 = (bf16[2,2,784,128]{3,2,1,0:T(8,128)(2,1)}, bf16[2,2,784,128]{3,2,1,0:T(8,128)(2,1)S(1)}, u32[]{:S(2)}, u32[]{:S(2)}) collective-permute-start(bf16[2,2,784,128]{3,2,1,0:T(8,128)(2,1)} %pad_maximum_fusion.12), channel_id=1, source_target_pairs={{0,8},{4,12},{8,16},{12,20},{16,24},{20,28},{24,0},{28,4},{1,9},{5... | collective-permute-start | bytes 2408456 | tf_op jit(solution)/shard_map/ppermute | solution.py:389
  123.8 146.3 %copy-start.24 = (s32[4]{0:T(128)}, s32[4]{0:T(128)S(1)}, u32[]{:S(2)}) copy-start(s32[4]{0:T(128)S(1)} %pad_add_fusion.flags_ref) | copy-start | bytes 52
  148.1 23.7 %collective-permute-start.9 = (bf16[2,2,784,128]{3,2,1,0:T(8,128)(2,1)S(1)}, bf16[2,2,784,128]{3,2,1,0:T(8,128)(2,1)S(1)}, u32[]{:S(2)}, u32[]{:S(2)}) collective-permute-start(bf16[2,2,784,128]{3,2,1,0:T(8,128)(2,1)S(1)} %pad_maximum_fusion.14), channel_id=1, source_target_pairs={{0,8},{4,12},{8,16},{12,20},{16,24},{20,28},{24,0},{28,4},{1,9},{5... | collective-permute-start | bytes 2408456 | tf_op jit(solution)/shard_map/ppermute | solution.py:389
  148.5 28.2 %collective-permute-start.11 = (bf16[2,2,784,128]{3,2,1,0:T(8,128)(2,1)}, bf16[2,2,784,128]{3,2,1,0:T(8,128)(2,1)}, u32[]{:S(2)}, u32[]{:S(2)}) collective-permute-start(bf16[2,2,784,128]{3,2,1,0:T(8,128)(2,1)} %pad_maximum_fusion.13.near_ref), channel_id=1, source_target_pairs={{0,4},{4,0},{8,12},{12,8},{16,20},{20,16},{24,28},{28,24},{1,5},{5... | collective-permute-start | bytes 2408456 | tf_op jit(solution)/shard_map/ppermute | solution.py:389
  175.4 32.4 %collective-permute-start.12 = (bf16[4,2,784,128]{3,2,1,0:T(8,128)(2,1)}, bf16[4,2,784,128]{3,2,1,0:T(8,128)(2,1)}, u32[]{:S(2)}, u32[]{:S(2)}) collective-permute-start(bf16[4,2,784,128]{3,2,1,0:T(8,128)(2,1)} %pad_maximum_fusion.near_ref), channel_id=1, source_target_pairs={{0,4},{4,0},{8,12},{12,8},{16,20},{20,16},{24,28},{28,24},{1,5},{5... | collective-permute-start | bytes 4816904 | tf_op jit(solution)/shard_map/ppermute | solution.py:389
  176.2 29.0 %collective-permute-start.10 = (bf16[1,2,784,128]{3,2,1,0:T(8,128)(2,1)}, bf16[1,2,784,128]{3,2,1,0:T(8,128)(2,1)S(1)}, u32[]{:S(2)}, u32[]{:S(2)}) collective-permute-start(bf16[1,2,784,128]{3,2,1,0:T(8,128)(2,1)} %get-tuple-element.90), channel_id=1, source_target_pairs={{0,8},{4,12},{8,16},{12,20},{16,24},{20,28},{24,0},{28,4},{1,9},{5... | collective-permute-start | bytes 1204232 | tf_op jit(solution)/shard_map/ppermute | solution.py:389
  210.8 27.5 %collective-permute-start.13 = (bf16[1,2,784,128]{3,2,1,0:T(8,128)(2,1)S(1)}, bf16[1,2,784,128]{3,2,1,0:T(8,128)(2,1)S(1)}, u32[]{:S(2)}, u32[]{:S(2)}) collective-permute-start(bf16[1,2,784,128]{3,2,1,0:T(8,128)(2,1)S(1)} %collective-permute-done.10), channel_id=1, source_target_pairs={{0,8},{4,12},{8,16},{12,20},{16,24},{20,28},{24,0},{28,4},{1,9},{5... | collective-permute-start | bytes 1204232 | tf_op jit(solution)/shard_map/ppermute | solution.py:389
  213.3 26.8 %collective-permute-start.15 = (bf16[2,2,784,128]{3,2,1,0:T(8,128)(2,1)S(1)}, bf16[2,2,784,128]{3,2,1,0:T(8,128)(2,1)S(1)}, u32[]{:S(2)}, u32[]{:S(2)}) collective-permute-start(bf16[2,2,784,128]{3,2,1,0:T(8,128)(2,1)S(1)} %pad_maximum_fusion.15), channel_id=1, source_target_pairs={{8,0},{12,4},{16,8},{20,12},{24,16},{28,20},{0,24},{4,28},{9,1},{1... | collective-permute-start | bytes 2408456 | tf_op jit(solution)/shard_map/ppermute | solution.py:389
  214.9 25.0 %collective-permute-start.14 = (bf16[3,2,784,128]{3,2,1,0:T(8,128)(2,1)S(1)}, bf16[3,2,784,128]{3,2,1,0:T(8,128)(2,1)S(1)}, u32[]{:S(2)}, u32[]{:S(2)}) collective-permute-start(bf16[3,2,784,128]{3,2,1,0:T(8,128)(2,1)S(1)} %pad_maximum_fusion.2.near_ref), channel_id=1, source_target_pairs={{0,4},{4,0},{8,12},{12,8},{16,20},{20,16},{24,28},{28,24},{1,5},{5... | collective-permute-start | bytes 3612680 | tf_op jit(solution)/shard_map/ppermute | solution.py:389
  240.4 25.2 %collective-permute-start.17 = (bf16[2,2,784,128]{3,2,1,0:T(8,128)(2,1)S(1)}, bf16[2,2,784,128]{3,2,1,0:T(8,128)(2,1)S(1)}, u32[]{:S(2)}, u32[]{:S(2)}) collective-permute-start(bf16[2,2,784,128]{3,2,1,0:T(8,128)(2,1)S(1)} %pad_maximum_fusion.16), channel_id=1, source_target_pairs={{8,0},{12,4},{16,8},{20,12},{24,16},{28,20},{0,24},{4,28},{9,1},{1... | collective-permute-start | bytes 2408456 | tf_op jit(solution)/shard_map/ppermute | solution.py:389
  242.7 22.7 %collective-permute-start.16 = (bf16[3,2,784,128]{3,2,1,0:T(8,128)(2,1)S(1)}, bf16[3,2,784,128]{3,2,1,0:T(8,128)(2,1)S(1)}, u32[]{:S(2)}, u32[]{:S(2)}) collective-permute-start(bf16[3,2,784,128]{3,2,1,0:T(8,128)(2,1)S(1)} %pad_maximum_fusion.3.near_ref), channel_id=1, source_target_pairs={{0,4},{4,0},{8,12},{12,8},{16,20},{20,16},{24,28},{28,24},{1,5},{5... | collective-permute-start | bytes 3612680 | tf_op jit(solution)/shard_map/ppermute | solution.py:389
  266.6 26.6 %collective-permute-start.18 = (bf16[2,2,784,128]{3,2,1,0:T(8,128)(2,1)S(1)}, bf16[2,2,784,128]{3,2,1,0:T(8,128)(2,1)S(1)}, u32[]{:S(2)}, u32[]{:S(2)}) collective-permute-start(bf16[2,2,784,128]{3,2,1,0:T(8,128)(2,1)S(1)} %pad_maximum_fusion.18), channel_id=1, source_target_pairs={{8,0},{12,4},{16,8},{20,12},{24,16},{28,20},{0,24},{4,28},{9,1},{1... | collective-permute-start | bytes 2408456 | tf_op jit(solution)/shard_map/ppermute | solution.py:389
  269.0 23.2 %collective-permute-start.19 = (bf16[2,2,784,128]{3,2,1,0:T(8,128)(2,1)S(1)}, bf16[2,2,784,128]{3,2,1,0:T(8,128)(2,1)S(1)}, u32[]{:S(2)}, u32[]{:S(2)}) collective-permute-start(bf16[2,2,784,128]{3,2,1,0:T(8,128)(2,1)S(1)} %pad_maximum_fusion.17), channel_id=1, source_target_pairs={{0,4},{4,0},{8,12},{12,8},{16,20},{20,16},{24,28},{28,24},{1,5},{5... | collective-permute-start | bytes 2408456 | tf_op jit(solution)/shard_map/ppermute | solution.py:389
  296.8 21.1 %collective-permute-start.21 = (bf16[3,2,784,128]{3,2,1,0:T(8,128)(2,1)}, bf16[3,2,784,128]{3,2,1,0:T(8,128)(2,1)}, u32[]{:S(2)}, u32[]{:S(2)}) collective-permute-start(bf16[3,2,784,128]{3,2,1,0:T(8,128)(2,1)} %pad_maximum_fusion.4), channel_id=1, source_target_pairs={{0,4},{4,0},{8,12},{12,8},{16,20},{20,16},{24,28},{28,24},{1,5},{5... | collective-permute-start | bytes 3612680 | tf_op jit(solution)/shard_map/ppermute | solution.py:389
  297.7 12.6 %collective-permute-start.20 = (bf16[2,2,784,128]{3,2,1,0:T(8,128)(2,1)}, bf16[2,2,784,128]{3,2,1,0:T(8,128)(2,1)}, u32[]{:S(2)}, u32[]{:S(2)}) collective-permute-start(bf16[2,2,784,128]{3,2,1,0:T(8,128)(2,1)} %pad_maximum_fusion.19), channel_id=1, source_target_pairs={{8,0},{12,4},{16,8},{20,12},{24,16},{28,20},{0,24},{4,28},{9,1},{1... | collective-permute-start | bytes 2408456 | tf_op jit(solution)/shard_map/ppermute | solution.py:389
  324.5 15.9 %collective-permute-start.22 = (bf16[2,2,784,128]{3,2,1,0:T(8,128)(2,1)}, bf16[2,2,784,128]{3,2,1,0:T(8,128)(2,1)}, u32[]{:S(2)}, u32[]{:S(2)}) collective-permute-start(bf16[2,2,784,128]{3,2,1,0:T(8,128)(2,1)} %pad_maximum_fusion.21), channel_id=1, source_target_pairs={{8,0},{12,4},{16,8},{20,12},{24,16},{28,20},{0,24},{4,28},{9,1},{1... | collective-permute-start | bytes 2408456 | tf_op jit(solution)/shard_map/ppermute | solution.py:389
  324.9 19.4 %collective-permute-start.24 = (bf16[2,2,784,128]{3,2,1,0:T(8,128)(2,1)}, bf16[2,2,784,128]{3,2,1,0:T(8,128)(2,1)}, u32[]{:S(2)}, u32[]{:S(2)}) collective-permute-start(bf16[2,2,784,128]{3,2,1,0:T(8,128)(2,1)} %pad_maximum_fusion.20), channel_id=1, source_target_pairs={{0,4},{4,0},{8,12},{12,8},{16,20},{20,16},{24,28},{28,24},{1,5},{5... | collective-permute-start | bytes 2408456 | tf_op jit(solution)/shard_map/ppermute | solution.py:389
  343.9 11.7 %collective-permute-start.23 = (bf16[1,2,784,128]{3,2,1,0:T(8,128)(2,1)S(1)}, bf16[1,2,784,128]{3,2,1,0:T(8,128)(2,1)S(1)}, u32[]{:S(2)}, u32[]{:S(2)}) collective-permute-start(bf16[1,2,784,128]{3,2,1,0:T(8,128)(2,1)S(1)} %get-tuple-element.132), channel_id=1, source_target_pairs={{8,0},{12,4},{16,8},{20,12},{24,16},{28,20},{0,24},{4,28},{9,1},{1... | collective-permute-start | bytes 1204232 | tf_op jit(solution)/shard_map/ppermute | solution.py:389
  358.9 7.9 %collective-permute-start.25 = (bf16[1,2,784,128]{3,2,1,0:T(8,128)(2,1)S(1)}, bf16[1,2,784,128]{3,2,1,0:T(8,128)(2,1)S(1)}, u32[]{:S(2)}, u32[]{:S(2)}) collective-permute-start(bf16[1,2,784,128]{3,2,1,0:T(8,128)(2,1)S(1)} %get-tuple-element.137), channel_id=1, source_target_pairs={{8,0},{12,4},{16,8},{20,12},{24,16},{28,20},{0,24},{4,28},{9,1},{1... | collective-permute-start | bytes 1204232 | tf_op jit(solution)/shard_map/ppermute | solution.py:389
  360.3 20.8 %collective-permute-start.26 = (bf16[2,2,784,128]{3,2,1,0:T(8,128)(2,1)S(1)}, bf16[2,2,784,128]{3,2,1,0:T(8,128)(2,1)S(1)}, u32[]{:S(2)}, u32[]{:S(2)}) collective-permute-start(bf16[2,2,784,128]{3,2,1,0:T(8,128)(2,1)S(1)} %pad_maximum_fusion.22), channel_id=1, source_target_pairs={{0,4},{4,0},{8,12},{12,8},{16,20},{20,16},{24,28},{28,24},{1,5},{5... | collective-permute-start | bytes 2408456 | tf_op jit(solution)/shard_map/ppermute | solution.py:389
  360.4 31.5 %collective-permute-start.27 = (bf16[2,2,784,128]{3,2,1,0:T(8,128)(2,1)}, bf16[2,2,784,128]{3,2,1,0:T(8,128)(2,1)S(1)}, u32[]{:S(2)}, u32[]{:S(2)}) collective-permute-start(bf16[2,2,784,128]{3,2,1,0:T(8,128)(2,1)} %pad_maximum_fusion.23), channel_id=1, source_target_pairs={{0,4},{4,0},{8,12},{12,8},{16,20},{20,16},{24,28},{28,24},{1,5},{5... | collective-permute-start | bytes 2408456 | tf_op jit(solution)/shard_map/ppermute | solution.py:389
  385.6 14.9 %collective-permute-start.28 = (bf16[2,2,784,128]{3,2,1,0:T(8,128)(2,1)S(1)}, bf16[2,2,784,128]{3,2,1,0:T(8,128)(2,1)S(1)}, u32[]{:S(2)}, u32[]{:S(2)}) collective-permute-start(bf16[2,2,784,128]{3,2,1,0:T(8,128)(2,1)S(1)} %copy-done.57), channel_id=1, source_target_pairs={{0,4},{4,0},{8,12},{12,8},{16,20},{20,16},{24,28},{28,24},{1,5},{5... | collective-permute-start | bytes 2408456 | tf_op jit(solution)/shard_map/ppermute | solution.py:389
  (61 other events, 756.3 us)
Sparse Core Ops, SparseCore 0:
  9.6 58.9 all-gather.1

commit v3 on v2

--- a/solution.py
+++ b/solution.py
@@ -193,7 +193,7 @@
         out_shape=[whole, whole, whole, piece, piece],
         input_output_aliases=aliases,
         compiler_params=pltpu.CompilerParams(
-            dimension_semantics=("arbitrary",), vmem_limit_bytes=44 * 1024 * 1024
+            dimension_semantics=("arbitrary",), vmem_limit_bytes=58 * 1024 * 1024
         ),
         cost_estimate=pl.CostEstimate(
             flops=2 * flops,
@@ -306,40 +306,41 @@
 
     def swap_parts(k):
         parts = {}
+        c, e = k - lead - 1, k - lead - lines - 1
+        extra = 0.0
+        if has(e):
+            total = sums[e].astype(f32) + read(into("down", "sum", k - 1)).astype(f32)
+            totals[e] = total.astype(bf16)
+            extra = jnp.where(beside, total, 0.0)
+        low_b = own[k][1] if has(k) else prevs[c][-1] if has(c) else None
+        high_b = None
+        if has(k - lines):
+            high_b = read(into("up", "next", k - 1))
+        elif has(e):
+            high_b = (prevs[e][-1].astype(f32) + extra).astype(bf16)
         if has(k):
             parts["a"] = own[k][0]
-        if has(k) and has(k - 2):
-            parts["b"] = jnp.where(low_side, own[k][1], read(into("up", "next", k - 1)))
-        elif has(k):
-            parts["b"] = own[k][1]
-        elif has(k - 2):
-            parts["b"] = read(into("up", "next", k - 1))
+        if low_b is not None and high_b is not None:
+            parts["b"] = jnp.where(low_side, low_b, high_b)
+        elif low_b is not None or high_b is not None:
+            parts["b"] = high_b if low_b is None else low_b
+        if has(e):
+            relay = (read(into("down", "back", lead + 2 + e)).astype(f32) + extra).astype(bf16)
+            parts["back_a"] = jnp.where(low_side, relay, prevs[e][0])
         c = k - lines
         if has(c):
             choice = {0: read(out("up", "stream", c + 1))}
             choice.update({d: read(into("up", "stream", c + d)) for d in range(1, lines)})
             parts["first"] = pick(hops, choice)
-        c, e = k - lead - 1, k - lead - lines - 1
+        c = k - lead - 1
         if has(c):
             parts["share"] = jnp.where(low_side, firsts[c][-1], firsts[c][0])
-        if has(e):
-            carried = read(into("down", "sum", k - 1)).astype(f32)
-            total = sums[e].astype(f32) + carried
-            totals[e] = total.astype(bf16)
-            extra = jnp.where(beside, total, 0.0)
-            relay = (read(into("down", "back", lead + 2 + e)).astype(f32) + extra).astype(bf16)
-            parts["back_a"] = jnp.where(low_side, relay, prevs[e][0])
-            high_b = (prevs[e][-1].astype(f32) + extra).astype(bf16)
-            parts["back_b"] = jnp.where(low_side, prevs[c][-1], high_b) if has(c) else high_b
-        elif has(c):
-            parts["back_b"] = prevs[c][-1]
         return parts
 
     def up_parts(k):
         parts = {}
         c = k - 1
         if has(c):
-            parts["next"] = jnp.where(low_side, read(into("swap", "a", c)), own[c][1])
             fresh = jnp.where(
                 low_side,
                 jnp.where(owner, own[c][0], read(into("swap", "a", c))),
@@ -349,6 +350,9 @@
         if 0 < c < steps:
             passed = read(into("up", "stream", k - 1))
             parts["stream"] = jnp.where(hops == 0, fresh, passed) if has(c) else passed
+        c = k - lines + 1
+        if has(c):
+            parts["next"] = jnp.where(low_side, read(into("swap", "a", c)), own[c][1])
         return parts
 
     def down_parts(k):
@@ -359,7 +363,7 @@
             share = read(into("swap", "share", k - 1)).astype(f32)
             sums[s] = after((mine + share).astype(bf16))
             parts["back"] = jnp.where(
-                low_side, prevs[s][0], read(into("swap", "back_b", k - 1))
+                low_side, prevs[s][0], read(into("swap", "b", k - 1))
             )
         if 0 <= s < steps:
             low = max(0, s - lines + 1)
@@ -382,24 +386,26 @@
             if parts:
                 stacks[kind] = jnp.stack(list(parts.values()))
         kinds = list(stacks)
-        if kinds:
+        if k >= lines and kinds:
             held = lax.optimization_barrier((*[stacks[x] for x in kinds], *done))
-            for kind, stack in zip(kinds, held):
-                sent[kind, k] = stack
-                came[kind, k] = lax.ppermute(stack, "tm", routes[kind])
+            stacks = dict(zip(kinds, held))
+        for kind, stack in stacks.items():
+            sent[kind, k] = stack
+            came[kind, k] = lax.ppermute(stack, "tm", routes[kind])
         done = []
         ready = [sent[x, k] for x in kinds]
-        if k == lines - 1:
+        if k == lines:
             attn_grad = lax.dot_general(
                 after(gathered, *ready), out_weight, (((1,), (1,)), ((), ())),
                 preferred_element_type=f32,
             ).astype(bf16)
-            done.append(attn_grad)
+            for kind in kinds:
+                came[kind, k] = after(came[kind, k], attn_grad)
         c = k - lead
         if has(c):
             befores = (
-                into("up", "next", c + 1), into("swap", "a", c),
-                into("swap", "b", c + 2), into("swap", "b", c),
+                into("up", "next", c + lines - 1), into("swap", "a", c),
+                into("swap", "b", c + lines), into("swap", "b", c),
             )
             results = attn_call(
                 after(flags, *ready), query_in, attn_grad, key_in, value_in,
@@ -411,7 +417,7 @@
         c = k - lead - lines - 2
         if has(c):
             returned = (
-                into("swap", "back_a", k - 1), into("swap", "back_b", k - 1),
+                into("swap", "back_a", k - 1), into("swap", "b", k - 1),
                 into("down", "back", lead + 2 + c),
             )
             dq, dk, dv = outs

time: 419 us -> 428 us (1.021)
  waiting for transfers between devices: 154 us -> 131 us
  other arithmetic: 47 us -> 65.1 us
  starting transfers between devices: 30.2 us -> 46.9 us
  local copies, waits for them, and re-layouts: 21.5 us -> 14.5 us
  Pallas kernels: 127 us -> 132 us
    ppermute x29, waiting for transfers between devices: 153 us -> 130 us  [local(): came[kind, k] = lax.ppermute(stack, 'tm', routes[kind])]
    ppermute x29, starting transfers between devices: 30.1 us -> 46.9 us  [local(): came[kind, k] = lax.ppermute(stack, 'tm', routes[kind])]
    unnamed x126 -> x120, local copies, waits for them, and re-layouts: 17.2 us -> 9.03 us
    select_n x5, other arithmetic: 0.21 us -> 4.99 us  [swap_parts(): parts['share'] = jnp.where(low_side, firsts[c][-1], firsts[c][0])]
    pallas_call x5, Pallas kernels: 109 us -> 114 us  [attn_call(): pl.pallas_call(functools.partial(attn_kernel, scale, rows, sub), grid_spe...]
    select_n x5, other arithmetic: 5.25 us -> 9.63 us  [up_parts(): parts['next'] = jnp.where(low_side, read(into('swap', 'a', c)), own[c][1])]
  transfers between devices with their start and end apart: 30 -> 30, of which waited for: 16 -> 15; matrix products, arithmetic and copies ran while one was open for 8% -> 15% of each run, Pallas kernels for 30% -> 30%
where the time goes in v3:
time: 428 us; the launch traced here: 421 us
  Pallas kernels  132 us (31%)
  waiting for transfers between devices  131 us (31%)
  other arithmetic  65.1 us (15%)
  starting transfers between devices  46.9 us (11%)
  matrix products  16.3 us (4%)
  between operations  16.2 us (4%)
  local copies, waits for them, and re-layouts  14.5 us (3%)
    ppermute x29, waiting for transfers between devices, local(): came[kind, k] = lax.ppermute(stack, 'tm', routes[kind])  130 us
    pallas_call x5, Pallas kernels, attn_call(): pl.pallas_call(functools.partial(attn_kernel, scale, rows, sub), grid_spe...  114 us
    ppermute x29, starting transfers between devices, local(): came[kind, k] = lax.ppermute(stack, 'tm', routes[kind])  46.9 us
    another operation x37, other arithmetic, local(): stacks[kind] = jnp.stack(list(parts.values()))  28 us
    pallas_call x5, Pallas kernels, join_call(): pl.pallas_call(join_kernel, grid_spec=pltpu.PrefetchScalarGridSpec(num_sc...  17.6 us
    dot_general x1, matrix products, local(): lax.dot_general(after(gathered, *ready), out_weight, (((1,), (1,)), ((),...  16.3 us
    select_n x5, other arithmetic, up_parts(): parts['next'] = jnp.where(low_side, read(into('swap', 'a', c)), own[c][1])  9.63 us
    unnamed x120, local copies, waits for them, and re-layouts  9.03 us
  transfers between devices with their start and end apart: 30, of which 15 were waited for; matrix products, arithmetic and copies ran while one was open for 15% of the time, Pallas kernels for 30%

profile of v3, /device:TPU:0, one launch (start us, length us, event | category | flops | bytes accessed | tf_op | source)
XLA Modules:
  0.0 421.3 jit_solution(9322271671881130930)
XLA Ops:
  13.7 2.9 collective-permute-start.2
  18.4 17.2 %collective-permute-done.2.rest_1_.rest_3_ = bf16[2,2,784,128]{3,2,1,0:T(8,128)(2,1)S(1)} collective-permute-done((bf16[2,2,784,128]{3,2,1,0:T(8,128)(2,1)}, bf16[2,2,784,128]{3,2,1,0:T(8,128)(2,1)S(1)}, u32[]{:S(2)}, u32[]{:S(2)}) %collective-permute-start.2) | collective-permute-done | bytes 802848 | tf_op jit(solution)/shard_map/ppermute | solution.py:394
  42.7 10.2 %collective-permute-done.1.rest_1_.rest_3_ = bf16[2,2,784,128]{3,2,1,0:T(8,128)(2,1)} collective-permute-done((bf16[2,2,784,128]{3,2,1,0:T(8,128)(2,1)}, bf16[2,2,784,128]{3,2,1,0:T(8,128)(2,1)}, u32[]{:S(2)}, u32[]{:S(2)}) %collective-permute-start.1) | collective-permute-done | bytes 802848 | tf_op jit(solution)/shard_map/ppermute | solution.py:394
  52.9 2.4 broadcast_select_fusion.8
  60.1 10.0 %collective-permute-done.rest_1_.rest_3_ = bf16[2,2,784,128]{3,2,1,0:T(8,128)(2,1)} collective-permute-done((bf16[2,2,784,128]{3,2,1,0:T(8,128)(2,1)}, bf16[2,2,784,128]{3,2,1,0:T(8,128)(2,1)}, u32[]{:S(2)}, u32[]{:S(2)}) %collective-permute-start) | collective-permute-done | bytes 802848 | tf_op jit(solution)/shard_map/ppermute | solution.py:394
  78.9 7.6 %collective-permute-done.6.rest_1_.rest_3_ = bf16[2,2,784,128]{3,2,1,0:T(8,128)(2,1)} collective-permute-done((bf16[2,2,784,128]{3,2,1,0:T(8,128)(2,1)}, bf16[2,2,784,128]{3,2,1,0:T(8,128)(2,1)}, u32[]{:S(2)}, u32[]{:S(2)}) %collective-permute-start.6) | collective-permute-done | bytes 802848 | tf_op jit(solution)/shard_map/ppermute | solution.py:394
  86.4 6.9 %collective-permute-done.5.rest_0_ = bf16[2,2,784,128]{3,2,1,0:T(8,128)(2,1)S(1)} collective-permute-done((bf16[2,2,784,128]{3,2,1,0:T(8,128)(2,1)}, bf16[2,2,784,128]{3,2,1,0:T(8,128)(2,1)S(1)}, u32[]{:S(2)}, u32[]{:S(2)}) %collective-permute-start.5) | collective-permute-done | bytes 802848 | tf_op jit(solution)/shard_map/ppermute | solution.py:394
  99.2 16.3 %convolution_convert_fusion.g_ref = bf16[784,1280]{1,0:T(8,128)(2,1)} fusion(bf16[784,5120]{1,0:T(8,128)(2,1)} %all-gather.2.cloned.1.call-done, bf16[1280,5120]{1,0:T(8,128)(2,1)} %param.11), kind=kOutput, calls=%fused_computation | convolution fusion | flops 10277048320 | bytes 23142400 | tf_op jit(solution)/shard_map/dot_general | solution.py:398
  116.7 6.9 %collective-permute-done.8.far_ref.rest_2_.rest_1_.rest_3_ = bf16[3,2,784,128]{3,2,1,0:T(8,128)(2,1)} collective-permute-done((bf16[3,2,784,128]{3,2,1,0:T(8,128)(2,1)}, bf16[3,2,784,128]{3,2,1,0:T(8,128)(2,1)}, u32[]{:S(2)}, u32[]{:S(2)}) %collective-permute-start.8) | collective-permute-done | bytes 1204256 | tf_op jit(solution)/shard_map/ppermute | solution.py:394
  129.5 22.8 %shard_map.94 = (bf16[784,1280]{1,0:T(8,128)(2,1)}, bf16[784,1280]{1,0:T(8,128)(2,1)}, bf16[784,1280]{1,0:T(8,128)(2,1)}, bf16[2,2,784,128]{3,2,1,0:T(8,128)(2,1)}, bf16[2,2,784,128]{3,2,1,0:T(8,128)(2,1)}) custom-call(s32[4]{0:T(128)} %pad_add_fusion.flags_ref, bf16[784,1280]{1,0:T(8,128)(2,1)} %q_ref.9, bf16[784,1280]{1,0:T(8,128)(2,1)} %convolution_convert_fusion.g_ref, ...), custom_call_target="tpu_custom_call" | custom-call | flops 9441116160 | bytes 6021120 | tf_op jit(solution)/shard_map/pallas_call | solution.py:174
  158.8 22.8 %shard_map.95 = (bf16[784,1280]{1,0:T(8,128)(2,1)}, bf16[784,1280]{1,0:T(8,128)(2,1)}, bf16[784,1280]{1,0:T(8,128)(2,1)}, bf16[2,2,784,128]{3,2,1,0:T(8,128)(2,1)}, bf16[2,2,784,128]{3,2,1,0:T(8,128)(2,1)}) custom-call(s32[4]{0:T(128)} %pad_add_fusion.flags_ref, ...), custom_call_target="tpu_custom_call", output_to_operand_aliasing={{0}: (11, {}), {1}: (12, {}), {2}: (13, {})} | custom-call | flops 9441116160 | bytes 6021120 | tf_op jit(solution)/shard_map/pallas_call | solution.py:174
  190.1 2.4 collective-permute-start.13
  195.6 22.8 %shard_map.96 = (bf16[784,1280]{1,0:T(8,128)(2,1)}, bf16[784,1280]{1,0:T(8,128)(2,1)}, bf16[784,1280]{1,0:T(8,128)(2,1)}, bf16[2,2,784,128]{3,2,1,0:T(8,128)(2,1)}, bf16[2,2,784,128]{3,2,1,0:T(8,128)(2,1)}) custom-call(s32[4]{0:T(128)} %pad_add_fusion.flags_ref, ...), custom_call_target="tpu_custom_call", output_to_operand_aliasing={{0}: (11, {}), {1}: (12, {}), {2}: (13, {})} | custom-call | flops 9441116160 | bytes 6021120 | tf_op jit(solution)/shard_map/pallas_call | solution.py:174
  228.0 22.8 %shard_map.97 = (bf16[784,1280]{1,0:T(8,128)(2,1)}, bf16[784,1280]{1,0:T(8,128)(2,1)}, bf16[784,1280]{1,0:T(8,128)(2,1)}, bf16[2,2,784,128]{3,2,1,0:T(8,128)(2,1)}, bf16[2,2,784,128]{3,2,1,0:T(8,128)(2,1)}) custom-call(s32[4]{0:T(128)} %pad_add_fusion.flags_ref, ...), custom_call_target="tpu_custom_call", output_to_operand_aliasing={{0}: (11, {}), {1}: (12, {}), {2}: (13, {})} | custom-call | flops 9441116160 | bytes 6021120 | tf_op jit(solution)/shard_map/pallas_call | solution.py:174
  260.2 22.8 %shard_map.98 = (bf16[784,1280]{1,0:T(8,128)(2,1)}, bf16[784,1280]{1,0:T(8,128)(2,1)}, bf16[784,1280]{1,0:T(8,128)(2,1)}, bf16[2,2,784,128]{3,2,1,0:T(8,128)(2,1)}, bf16[2,2,784,128]{3,2,1,0:T(8,128)(2,1)}) custom-call(s32[4]{0:T(128)} %pad_add_fusion.flags_ref, ...), custom_call_target="tpu_custom_call", output_to_operand_aliasing={{0}: (11, {}), {1}: (12, {}), {2}: (13, {})} | custom-call | flops 9441116160 | bytes 6021120 | tf_op jit(solution)/shard_map/pallas_call | solution.py:174
  291.1 2.5 collective-permute-start.21
  293.6 15.2 %collective-permute-done.21.rest_2_ = bf16[2,2,784,128]{3,2,1,0:T(8,128)(2,1)} collective-permute-done((bf16[2,2,784,128]{3,2,1,0:T(8,128)(2,1)}, bf16[2,2,784,128]{3,2,1,0:T(8,128)(2,1)}, u32[]{:S(2)}, u32[]{:S(2)}) %collective-permute-start.21) | collective-permute-done | bytes 802848 | tf_op jit(solution)/shard_map/ppermute | solution.py:394
  310.3 5.9 %collective-permute-done.20.rest_0_.rest_1_ = bf16[3,2,784,128]{3,2,1,0:T(8,128)(2,1)S(1)} collective-permute-done((bf16[3,2,784,128]{3,2,1,0:T(8,128)(2,1)}, bf16[3,2,784,128]{3,2,1,0:T(8,128)(2,1)S(1)}, u32[]{:S(2)}, u32[]{:S(2)}) %collective-permute-start.20) | collective-permute-done | bytes 1204256 | tf_op jit(solution)/shard_map/ppermute | solution.py:394
  318.0 2.2 fusion.31
  322.6 3.4 collective-permute-start.22
  326.3 3.6 shard_map.99
  329.9 11.0 %collective-permute-done.22.rest_2_ = bf16[2,2,784,128]{3,2,1,0:T(8,128)(2,1)S(1)} collective-permute-done((bf16[2,2,784,128]{3,2,1,0:T(8,128)(2,1)}, bf16[2,2,784,128]{3,2,1,0:T(8,128)(2,1)S(1)}, u32[]{:S(2)}, u32[]{:S(2)}) %collective-permute-start.22) | collective-permute-done | bytes 802848 | tf_op jit(solution)/shard_map/ppermute | solution.py:394
  343.4 4.2 collective-permute-start.23
  347.6 3.6 shard_map.100
  356.7 4.2 collective-permute-start.25
  362.9 3.4 collective-permute-done.25
  368.4 13.2 %collective-permute-done.26.rest_0_.rest_1_ = bf16[2,2,784,128]{3,2,1,0:T(8,128)(2,1)S(1)} collective-permute-done((bf16[2,2,784,128]{3,2,1,0:T(8,128)(2,1)S(1)}, bf16[2,2,784,128]{3,2,1,0:T(8,128)(2,1)S(1)}, u32[]{:S(2)}, u32[]{:S(2)}) %collective-permute-start.26) | collective-permute-done | bytes 802848 | tf_op jit(solution)/shard_map/ppermute | solution.py:394
  382.6 3.6 shard_map.101
  386.2 12.6 %collective-permute-done.27.rest_0_.rest_1_ = bf16[2,2,784,128]{3,2,1,0:T(8,128)(2,1)S(1)} collective-permute-done((bf16[2,2,784,128]{3,2,1,0:T(8,128)(2,1)}, bf16[2,2,784,128]{3,2,1,0:T(8,128)(2,1)S(1)}, u32[]{:S(2)}, u32[]{:S(2)}) %collective-permute-start.27) | collective-permute-done | bytes 802848 | tf_op jit(solution)/shard_map/ppermute | solution.py:394
  399.8 3.4 shard_map.102
  403.2 6.7 %collective-permute-done.28.rest_0_.rest_1_ = bf16[2,2,784,128]{3,2,1,0:T(8,128)(2,1)S(1)} collective-permute-done((bf16[2,2,784,128]{3,2,1,0:T(8,128)(2,1)S(1)}, bf16[2,2,784,128]{3,2,1,0:T(8,128)(2,1)S(1)}, u32[]{:S(2)}, u32[]{:S(2)}) %collective-permute-start.28) | collective-permute-done | bytes 802848 | tf_op jit(solution)/shard_map/ppermute | solution.py:394
  410.8 3.4 shard_map.103
  (232 shorter events, 106.3 us)
Async XLA Ops:
  7.2 92.0 %all-gather.2.cloned.1.call-start = ((), (), s32[]{:S(2)}) async-start(), calls=%async_computation | async-start | bytes 10035200 | tf_op jit(solution)/shard_map/all_gather | solution.py:287
  13.7 21.9 %collective-permute-start.2 = (bf16[2,2,784,128]{3,2,1,0:T(8,128)(2,1)}, bf16[2,2,784,128]{3,2,1,0:T(8,128)(2,1)S(1)}, u32[]{:S(2)}, u32[]{:S(2)}) collective-permute-start(bf16[2,2,784,128]{3,2,1,0:T(8,128)(2,1)} %pad_maximum_fusion.7), channel_id=1, source_target_pairs={{0,4},{4,0},{8,12},{12,8},{16,20},{20,16},{24,28},{28,24},{1,5},{5... | collective-permute-start | bytes 2408456 | tf_op jit(solution)/shard_map/ppermute | solution.py:394
  17.7 35.2 %collective-permute-start.1 = (bf16[2,2,784,128]{3,2,1,0:T(8,128)(2,1)}, bf16[2,2,784,128]{3,2,1,0:T(8,128)(2,1)}, u32[]{:S(2)}, u32[]{:S(2)}) collective-permute-start(bf16[2,2,784,128]{3,2,1,0:T(8,128)(2,1)} %pad_maximum_fusion.6), channel_id=1, source_target_pairs={{0,4},{4,0},{8,12},{12,8},{16,20},{20,16},{24,28},{28,24},{1,5},{5... | collective-permute-start | bytes 2408456 | tf_op jit(solution)/shard_map/ppermute | solution.py:394
  37.9 14.9 %collective-permute-start.3 = (bf16[1,2,784,128]{3,2,1,0:T(8,128)(2,1)S(1)}, bf16[1,2,784,128]{3,2,1,0:T(8,128)(2,1)S(1)}, u32[]{:S(2)}, u32[]{:S(2)}) collective-permute-start(bf16[1,2,784,128]{3,2,1,0:T(8,128)(2,1)S(1)} %get-tuple-element.198), channel_id=1, source_target_pairs={{0,8},{4,12},{8,16},{12,20},{16,24},{20,28},{24,0},{28,4},{1,9},{5... | collective-permute-start | bytes 1204232 | tf_op jit(solution)/shard_map/ppermute | solution.py:394
  41.2 28.9 %collective-permute-start = (bf16[2,2,784,128]{3,2,1,0:T(8,128)(2,1)}, bf16[2,2,784,128]{3,2,1,0:T(8,128)(2,1)}, u32[]{:S(2)}, u32[]{:S(2)}) collective-permute-start(bf16[2,2,784,128]{3,2,1,0:T(8,128)(2,1)} %pad_maximum_fusion.5), channel_id=1, source_target_pairs={{0,4},{4,0},{8,12},{12,8},{16,20},{20,16},{24,28},{28,24},{1,5},{5... | collective-permute-start | bytes 2408456 | tf_op jit(solution)/shard_map/ppermute | solution.py:394
  55.4 14.7 %collective-permute-start.4 = (bf16[1,2,784,128]{3,2,1,0:T(8,128)(2,1)S(1)}, bf16[1,2,784,128]{3,2,1,0:T(8,128)(2,1)S(1)}, u32[]{:S(2)}, u32[]{:S(2)}) collective-permute-start(bf16[1,2,784,128]{3,2,1,0:T(8,128)(2,1)S(1)} %get-tuple-element.196), channel_id=1, source_target_pairs={{0,8},{4,12},{8,16},{12,20},{16,24},{20,28},{24,0},{28,4},{1,9},{5... | collective-permute-start | bytes 1204232 | tf_op jit(solution)/shard_map/ppermute | solution.py:394
  58.6 27.9 %collective-permute-start.6 = (bf16[2,2,784,128]{3,2,1,0:T(8,128)(2,1)}, bf16[2,2,784,128]{3,2,1,0:T(8,128)(2,1)}, u32[]{:S(2)}, u32[]{:S(2)}) collective-permute-start(bf16[2,2,784,128]{3,2,1,0:T(8,128)(2,1)} %pad_maximum_fusion.9), channel_id=1, source_target_pairs={{0,4},{4,0},{8,12},{12,8},{16,20},{20,16},{24,28},{28,24},{1,5},{5... | collective-permute-start | bytes 2408456 | tf_op jit(solution)/shard_map/ppermute | solution.py:394
  73.1 20.3 %collective-permute-start.5 = (bf16[2,2,784,128]{3,2,1,0:T(8,128)(2,1)}, bf16[2,2,784,128]{3,2,1,0:T(8,128)(2,1)S(1)}, u32[]{:S(2)}, u32[]{:S(2)}) collective-permute-start(bf16[2,2,784,128]{3,2,1,0:T(8,128)(2,1)} %pad_maximum_fusion.8), channel_id=1, source_target_pairs={{0,8},{4,12},{8,16},{12,20},{16,24},{20,28},{24,0},{28,4},{1,9},{5... | collective-permute-start | bytes 2408456 | tf_op jit(solution)/shard_map/ppermute | solution.py:394
  97.7 19.0 %collective-permute-start.7 = (bf16[2,2,784,128]{3,2,1,0:T(8,128)(2,1)}, bf16[2,2,784,128]{3,2,1,0:T(8,128)(2,1)S(1)}, u32[]{:S(2)}, u32[]{:S(2)}) collective-permute-start(bf16[2,2,784,128]{3,2,1,0:T(8,128)(2,1)} %pad_maximum_fusion.10), channel_id=1, source_target_pairs={{0,8},{4,12},{8,16},{12,20},{16,24},{20,28},{24,0},{28,4},{1,9},{5... | collective-permute-start | bytes 2408456 | tf_op jit(solution)/shard_map/ppermute | solution.py:394
  97.7 25.9 %collective-permute-start.8 = (bf16[3,2,784,128]{3,2,1,0:T(8,128)(2,1)}, bf16[3,2,784,128]{3,2,1,0:T(8,128)(2,1)}, u32[]{:S(2)}, u32[]{:S(2)}) collective-permute-start(bf16[3,2,784,128]{3,2,1,0:T(8,128)(2,1)} %pad_maximum_fusion.near_ref), channel_id=1, source_target_pairs={{0,4},{4,0},{8,12},{12,8},{16,20},{20,16},{24,28},{28,24},{1,5},{5... | collective-permute-start | bytes 3612680 | tf_op jit(solution)/shard_map/ppermute | solution.py:394
  116.7 36.9 %copy-start.1 = (bf16[2,2,784,128]{3,2,1,0:T(8,128)(2,1)}, bf16[2,2,784,128]{3,2,1,0:T(8,128)(2,1)S(1)}, u32[]{:S(2)}) copy-start(bf16[2,2,784,128]{3,2,1,0:T(8,128)(2,1)S(1)} %collective-permute-done.7.rest_0_) | copy-start | bytes 2408452
  126.9 26.6 %collective-permute-start.9 = (bf16[2,2,784,128]{3,2,1,0:T(8,128)(2,1)S(1)}, bf16[2,2,784,128]{3,2,1,0:T(8,128)(2,1)S(1)}, u32[]{:S(2)}, u32[]{:S(2)}) collective-permute-start(bf16[2,2,784,128]{3,2,1,0:T(8,128)(2,1)S(1)} %pad_maximum_fusion.12), channel_id=1, source_target_pairs={{0,8},{4,12},{8,16},{12,20},{16,24},{20,28},{24,0},{28,4},{1,9},{5... | collective-permute-start | bytes 2408456 | tf_op jit(solution)/shard_map/ppermute | solution.py:394
  128.0 30.9 %collective-permute-start.10 = (bf16[2,2,784,128]{3,2,1,0:T(8,128)(2,1)}, bf16[2,2,784,128]{3,2,1,0:T(8,128)(2,1)}, u32[]{:S(2)}, u32[]{:S(2)}) collective-permute-start(bf16[2,2,784,128]{3,2,1,0:T(8,128)(2,1)} %pad_maximum_fusion.11.near_ref), channel_id=1, source_target_pairs={{0,4},{4,0},{8,12},{12,8},{16,20},{20,16},{24,28},{28,24},{1,5},{5... | collective-permute-start | bytes 2408456 | tf_op jit(solution)/shard_map/ppermute | solution.py:394
  156.2 26.7 %collective-permute-start.11 = (bf16[2,2,784,128]{3,2,1,0:T(8,128)(2,1)S(1)}, bf16[2,2,784,128]{3,2,1,0:T(8,128)(2,1)S(1)}, u32[]{:S(2)}, u32[]{:S(2)}) collective-permute-start(bf16[2,2,784,128]{3,2,1,0:T(8,128)(2,1)S(1)} %pad_maximum_fusion.13), channel_id=1, source_target_pairs={{0,8},{4,12},{8,16},{12,20},{16,24},{20,28},{24,0},{28,4},{1,9},{5... | collective-permute-start | bytes 2408456 | tf_op jit(solution)/shard_map/ppermute | solution.py:394
  158.3 27.4 %collective-permute-start.12 = (bf16[3,2,784,128]{3,2,1,0:T(8,128)(2,1)}, bf16[3,2,784,128]{3,2,1,0:T(8,128)(2,1)}, u32[]{:S(2)}, u32[]{:S(2)}) collective-permute-start(bf16[3,2,784,128]{3,2,1,0:T(8,128)(2,1)} %pad_maximum_fusion.1.near_ref), channel_id=1, source_target_pairs={{0,4},{4,0},{8,12},{12,8},{16,20},{20,16},{24,28},{28,24},{1,5},{5... | collective-permute-start | bytes 3612680 | tf_op jit(solution)/shard_map/ppermute | solution.py:394
  190.1 29.5 %collective-permute-start.13 = (bf16[2,2,784,128]{3,2,1,0:T(8,128)(2,1)}, bf16[2,2,784,128]{3,2,1,0:T(8,128)(2,1)S(1)}, u32[]{:S(2)}, u32[]{:S(2)}) collective-permute-start(bf16[2,2,784,128]{3,2,1,0:T(8,128)(2,1)} %pad_maximum_fusion.14), channel_id=1, source_target_pairs={{0,8},{4,12},{8,16},{12,20},{16,24},{20,28},{24,0},{28,4},{1,9},{5... | collective-permute-start | bytes 2408456 | tf_op jit(solution)/shard_map/ppermute | solution.py:394
  192.5 32.3 %collective-permute-start.15 = (bf16[2,2,784,128]{3,2,1,0:T(8,128)(2,1)}, bf16[2,2,784,128]{3,2,1,0:T(8,128)(2,1)S(1)}, u32[]{:S(2)}, u32[]{:S(2)}) collective-permute-start(bf16[2,2,784,128]{3,2,1,0:T(8,128)(2,1)} %pad_maximum_fusion.15), channel_id=1, source_target_pairs={{8,0},{12,4},{16,8},{20,12},{24,16},{28,20},{0,24},{4,28},{9,1},{1... | collective-permute-start | bytes 2408456 | tf_op jit(solution)/shard_map/ppermute | solution.py:394
  194.1 28.2 %collective-permute-start.14 = (bf16[3,2,784,128]{3,2,1,0:T(8,128)(2,1)S(1)}, bf16[3,2,784,128]{3,2,1,0:T(8,128)(2,1)}, u32[]{:S(2)}, u32[]{:S(2)}) collective-permute-start(bf16[3,2,784,128]{3,2,1,0:T(8,128)(2,1)S(1)} %pad_maximum_fusion.2.near_ref), channel_id=1, source_target_pairs={{0,4},{4,0},{8,12},{12,8},{16,20},{20,16},{24,28},{28,24},{1,5},{5... | collective-permute-start | bytes 3612680 | tf_op jit(solution)/shard_map/ppermute | solution.py:394
  224.8 63.8 %copy-start.11 = (bf16[2,2,784,128]{3,2,1,0:T(8,128)(2,1)}, bf16[2,2,784,128]{3,2,1,0:T(8,128)(2,1)S(1)}, u32[]{:S(2)}) copy-start(bf16[2,2,784,128]{3,2,1,0:T(8,128)(2,1)S(1)} %collective-permute-done.15.rest_2_) | copy-start | bytes 2408452
  225.1 30.6 %collective-permute-start.17 = (bf16[2,2,784,128]{3,2,1,0:T(8,128)(2,1)S(1)}, bf16[2,2,784,128]{3,2,1,0:T(8,128)(2,1)}, u32[]{:S(2)}, u32[]{:S(2)}) collective-permute-start(bf16[2,2,784,128]{3,2,1,0:T(8,128)(2,1)S(1)} %pad_maximum_fusion.16), channel_id=1, source_target_pairs={{8,0},{12,4},{16,8},{20,12},{24,16},{28,20},{0,24},{4,28},{9,1},{1... | collective-permute-start | bytes 2408456 | tf_op jit(solution)/shard_map/ppermute | solution.py:394
  226.9 26.1 %collective-permute-start.16 = (bf16[3,2,784,128]{3,2,1,0:T(8,128)(2,1)}, bf16[3,2,784,128]{3,2,1,0:T(8,128)(2,1)}, u32[]{:S(2)}, u32[]{:S(2)}) collective-permute-start(bf16[3,2,784,128]{3,2,1,0:T(8,128)(2,1)} %pad_maximum_fusion.3.near_ref), channel_id=1, source_target_pairs={{0,4},{4,0},{8,12},{12,8},{16,20},{20,16},{24,28},{28,24},{1,5},{5... | collective-permute-start | bytes 3612680 | tf_op jit(solution)/shard_map/ppermute | solution.py:394
  257.9 28.5 %collective-permute-start.18 = (bf16[2,2,784,128]{3,2,1,0:T(8,128)(2,1)}, bf16[2,2,784,128]{3,2,1,0:T(8,128)(2,1)S(1)}, u32[]{:S(2)}, u32[]{:S(2)}) collective-permute-start(bf16[2,2,784,128]{3,2,1,0:T(8,128)(2,1)} %pad_maximum_fusion.18), channel_id=1, source_target_pairs={{8,0},{12,4},{16,8},{20,12},{24,16},{28,20},{0,24},{4,28},{9,1},{1... | collective-permute-start | bytes 2408456 | tf_op jit(solution)/shard_map/ppermute | solution.py:394
  258.7 25.5 %collective-permute-start.19 = (bf16[2,2,784,128]{3,2,1,0:T(8,128)(2,1)}, bf16[2,2,784,128]{3,2,1,0:T(8,128)(2,1)}, u32[]{:S(2)}, u32[]{:S(2)}) collective-permute-start(bf16[2,2,784,128]{3,2,1,0:T(8,128)(2,1)} %pad_maximum_fusion.17), channel_id=1, source_target_pairs={{0,4},{4,0},{8,12},{12,8},{16,20},{20,16},{24,28},{28,24},{1,5},{5... | collective-permute-start | bytes 2408456 | tf_op jit(solution)/shard_map/ppermute | solution.py:394
  290.6 25.7 %collective-permute-start.20 = (bf16[3,2,784,128]{3,2,1,0:T(8,128)(2,1)}, bf16[3,2,784,128]{3,2,1,0:T(8,128)(2,1)S(1)}, u32[]{:S(2)}, u32[]{:S(2)}) collective-permute-start(bf16[3,2,784,128]{3,2,1,0:T(8,128)(2,1)} %pad_maximum_fusion.4), channel_id=1, source_target_pairs={{0,4},{4,0},{8,12},{12,8},{16,20},{20,16},{24,28},{28,24},{1,5},{5... | collective-permute-start | bytes 3612680 | tf_op jit(solution)/shard_map/ppermute | solution.py:394
  291.1 17.8 %collective-permute-start.21 = (bf16[2,2,784,128]{3,2,1,0:T(8,128)(2,1)}, bf16[2,2,784,128]{3,2,1,0:T(8,128)(2,1)}, u32[]{:S(2)}, u32[]{:S(2)}) collective-permute-start(bf16[2,2,784,128]{3,2,1,0:T(8,128)(2,1)} %pad_maximum_fusion.19), channel_id=1, source_target_pairs={{8,0},{12,4},{16,8},{20,12},{24,16},{28,20},{0,24},{4,28},{9,1},{1... | collective-permute-start | bytes 2408456 | tf_op jit(solution)/shard_map/ppermute | solution.py:394
  322.6 18.3 %collective-permute-start.22 = (bf16[2,2,784,128]{3,2,1,0:T(8,128)(2,1)}, bf16[2,2,784,128]{3,2,1,0:T(8,128)(2,1)S(1)}, u32[]{:S(2)}, u32[]{:S(2)}) collective-permute-start(bf16[2,2,784,128]{3,2,1,0:T(8,128)(2,1)} %pad_maximum_fusion.21), channel_id=1, source_target_pairs={{8,0},{12,4},{16,8},{20,12},{24,16},{28,20},{0,24},{4,28},{9,1},{1... | collective-permute-start | bytes 2408456 | tf_op jit(solution)/shard_map/ppermute | solution.py:394
  326.0 21.6 %collective-permute-start.24 = (bf16[2,2,784,128]{3,2,1,0:T(8,128)(2,1)}, bf16[2,2,784,128]{3,2,1,0:T(8,128)(2,1)}, u32[]{:S(2)}, u32[]{:S(2)}) collective-permute-start(bf16[2,2,784,128]{3,2,1,0:T(8,128)(2,1)} %pad_maximum_fusion.20), channel_id=1, source_target_pairs={{0,4},{4,0},{8,12},{12,8},{16,20},{20,16},{24,28},{28,24},{1,5},{5... | collective-permute-start | bytes 2408456 | tf_op jit(solution)/shard_map/ppermute | solution.py:394
  343.4 9.9 %collective-permute-start.23 = (bf16[1,2,784,128]{3,2,1,0:T(8,128)(2,1)}, bf16[1,2,784,128]{3,2,1,0:T(8,128)(2,1)S(1)}, u32[]{:S(2)}, u32[]{:S(2)}) collective-permute-start(bf16[1,2,784,128]{3,2,1,0:T(8,128)(2,1)} %get-tuple-element.124), channel_id=1, source_target_pairs={{8,0},{12,4},{16,8},{20,12},{24,16},{28,20},{0,24},{4,28},{9,1},{1... | collective-permute-start | bytes 1204232 | tf_op jit(solution)/shard_map/ppermute | solution.py:394
  356.7 9.6 %collective-permute-start.25 = (bf16[1,2,784,128]{3,2,1,0:T(8,128)(2,1)S(1)}, bf16[1,2,784,128]{3,2,1,0:T(8,128)(2,1)S(1)}, u32[]{:S(2)}, u32[]{:S(2)}) collective-permute-start(bf16[1,2,784,128]{3,2,1,0:T(8,128)(2,1)S(1)} %get-tuple-element.129), channel_id=1, source_target_pairs={{8,0},{12,4},{16,8},{20,12},{24,16},{28,20},{0,24},{4,28},{9,1},{1... | collective-permute-start | bytes 1204232 | tf_op jit(solution)/shard_map/ppermute | solution.py:394
  360.8 20.8 %collective-permute-start.26 = (bf16[2,2,784,128]{3,2,1,0:T(8,128)(2,1)S(1)}, bf16[2,2,784,128]{3,2,1,0:T(8,128)(2,1)S(1)}, u32[]{:S(2)}, u32[]{:S(2)}) collective-permute-start(bf16[2,2,784,128]{3,2,1,0:T(8,128)(2,1)S(1)} %copy-done.58), channel_id=1, source_target_pairs={{0,4},{4,0},{8,12},{12,8},{16,20},{20,16},{24,28},{28,24},{1,5},{5... | collective-permute-start | bytes 2408456 | tf_op jit(solution)/shard_map/ppermute | solution.py:394
  360.9 38.0 %collective-permute-start.27 = (bf16[2,2,784,128]{3,2,1,0:T(8,128)(2,1)}, bf16[2,2,784,128]{3,2,1,0:T(8,128)(2,1)S(1)}, u32[]{:S(2)}, u32[]{:S(2)}) collective-permute-start(bf16[2,2,784,128]{3,2,1,0:T(8,128)(2,1)} %pad_maximum_fusion.23), channel_id=1, source_target_pairs={{0,4},{4,0},{8,12},{12,8},{16,20},{20,16},{24,28},{28,24},{1,5},{5... | collective-permute-start | bytes 2408456 | tf_op jit(solution)/shard_map/ppermute | solution.py:394
  386.1 23.7 %collective-permute-start.28 = (bf16[2,2,784,128]{3,2,1,0:T(8,128)(2,1)S(1)}, bf16[2,2,784,128]{3,2,1,0:T(8,128)(2,1)S(1)}, u32[]{:S(2)}, u32[]{:S(2)}) collective-permute-start(bf16[2,2,784,128]{3,2,1,0:T(8,128)(2,1)S(1)} %copy-done.59), channel_id=1, source_target_pairs={{0,4},{4,0},{8,12},{12,8},{16,20},{20,16},{24,28},{28,24},{1,5},{5... | collective-permute-start | bytes 2408456 | tf_op jit(solution)/shard_map/ppermute | solution.py:394
  (58 other events, 399.5 us)
Sparse Core Ops, SparseCore 0:
  9.6 58.9 all-gather.1

commit v4 on v3

--- a/solution.py
+++ b/solution.py
@@ -193,7 +193,7 @@
         out_shape=[whole, whole, whole, piece, piece],
         input_output_aliases=aliases,
         compiler_params=pltpu.CompilerParams(
-            dimension_semantics=("arbitrary",), vmem_limit_bytes=58 * 1024 * 1024
+            dimension_semantics=("arbitrary",), vmem_limit_bytes=44 * 1024 * 1024
         ),
         cost_estimate=pl.CostEstimate(
             flops=2 * flops,
@@ -273,6 +273,7 @@
     chunks = [tuple(range(c, heads, count)) for c in range(count)]
     routes = {
         "swap": [(i, i ^ 1) for i in range(n)],
+        "early": [(i, i ^ 1) for i in range(n)],
         "up": [(i, (i + 2) % n) for i in range(n)],
         "down": [((i + 2) % n, i) for i in range(n)],
     }
@@ -312,13 +313,13 @@
             total = sums[e].astype(f32) + read(into("down", "sum", k - 1)).astype(f32)
             totals[e] = total.astype(bf16)
             extra = jnp.where(beside, total, 0.0)
-        low_b = own[k][1] if has(k) else prevs[c][-1] if has(c) else None
+        low_b = own[k][1] if has(k) and k < lines else prevs[c][-1] if has(c) else None
         high_b = None
         if has(k - lines):
             high_b = read(into("up", "next", k - 1))
         elif has(e):
             high_b = (prevs[e][-1].astype(f32) + extra).astype(bf16)
-        if has(k):
+        if has(k) and k < lines:
             parts["a"] = own[k][0]
         if low_b is not None and high_b is not None:
             parts["b"] = jnp.where(low_side, low_b, high_b)
@@ -337,14 +338,23 @@
             parts["share"] = jnp.where(low_side, firsts[c][-1], firsts[c][0])
         return parts
 
+    def early_parts(k):
+        return {"a": own[k][0], "own_b": own[k][1]} if has(k) and k >= lines else {}
+
+    def other_a(c):
+        return into("swap" if c < lines else "early", "a", c)
+
+    def other_b(c):
+        return into("swap", "b", c) if c < lines else into("early", "own_b", c)
+
     def up_parts(k):
         parts = {}
         c = k - 1
         if has(c):
             fresh = jnp.where(
                 low_side,
-                jnp.where(owner, own[c][0], read(into("swap", "a", c))),
-                jnp.where(owner, own[c][1], read(into("swap", "b", c))),
+                jnp.where(owner, own[c][0], read(other_a(c))),
+                jnp.where(owner, own[c][1], read(other_b(c))),
             )
             parts["stream"] = fresh
         if 0 < c < steps:
@@ -352,7 +362,7 @@
             parts["stream"] = jnp.where(hops == 0, fresh, passed) if has(c) else passed
         c = k - lines + 1
         if has(c):
-            parts["next"] = jnp.where(low_side, read(into("swap", "a", c)), own[c][1])
+            parts["next"] = jnp.where(low_side, read(other_a(c)), own[c][1])
         return parts
 
     def down_parts(k):
@@ -379,19 +389,23 @@
     for k in range(lead + count + lines + 2):
         stacks = {}
         for kind, parts in (
-            ("swap", swap_parts(k)), ("up", up_parts(k)), ("down", down_parts(k))
+            ("early", early_parts(k)), ("swap", swap_parts(k)), ("up", up_parts(k)), ("down", down_parts(k))
         ):
             for i, name in enumerate(parts):
                 place[name, k] = i
             if parts:
                 stacks[kind] = jnp.stack(list(parts.values()))
+        if "early" in stacks:
+            came["early", k] = lax.ppermute(stacks.pop("early"), "tm", routes["early"])
         kinds = list(stacks)
-        if k >= lines and kinds:
+        if lines <= k <= lead + count and kinds:
             held = lax.optimization_barrier((*[stacks[x] for x in kinds], *done))
             stacks = dict(zip(kinds, held))
         for kind, stack in stacks.items():
             sent[kind, k] = stack
             came[kind, k] = lax.ppermute(stack, "tm", routes[kind])
+        if k > lead + count and "down" in kinds and "swap" in kinds:
+            came["down", k] = after(came["down", k], sent["swap", k])
         done = []
         ready = [sent[x, k] for x in kinds]
         if k == lines:
@@ -404,8 +418,8 @@
         c = k - lead
         if has(c):
             befores = (
-                into("up", "next", c + lines - 1), into("swap", "a", c),
-                into("swap", "b", c + lines), into("swap", "b", c),
+                into("up", "next", c + lines - 1), other_a(c),
+                into("swap", "b", c + lines), other_b(c),
             )
             results = attn_call(
                 after(flags, *ready), query_in, attn_grad, key_in, value_in,
@@ -422,11 +436,10 @@
             )
             dq, dk, dv = outs
             dk, dv = join_call(
-                after(flags, *ready) if ready else flags, dk, dv, returned,
+                flags, dk, dv, returned,
                 (totals[c][None], 0), chunks[c],
             )
             outs = (dq, dk, dv)
-            done.append(dk)
     return tuple(outs)
 
 

time: 428 us -> 397 us (0.928)
  other arithmetic: 65.1 us -> 44.7 us
  Pallas kernels: 132 us -> 125 us
    pallas_call x5, Pallas kernels: 114 us -> 108 us  [attn_call(): pl.pallas_call(functools.partial(attn_kernel, scale, rows, sub), grid_spe...]
    select_n x5, other arithmetic: 4.99 us -> 0.21 us  [swap_parts(): parts['share'] = jnp.where(low_side, firsts[c][-1], firsts[c][0])]
    broadcast_in_dim x5 -> x2, other arithmetic: 6.72 us -> 2.06 us  [local(): dk, dv = join_call(flags, dk, dv, returned, (totals[c][None], 0), chunks[c])]
    convert_element_type x5, other arithmetic: 6.45 us -> 1.8 us  [down_parts(): sums[s] = after((mine + share).astype(bf16))]
    another operation x37 -> x41, other arithmetic: 28 us -> 29.6 us  [local(): stacks[kind] = jnp.stack(list(parts.values()))]
    unnamed x120 -> x126, local copies, waits for them, and re-layouts: 9.03 us -> 8.17 us
  transfers between devices with their start and end apart: 30 -> 31, of which waited for: 15 -> 16; matrix products, arithmetic and copies ran while one was open for 15% -> 15% of each run, Pallas kernels for 30% -> 31%
where the time goes in v4:
time: 397 us; the launch traced here: 390 us
  waiting for transfers between devices  128 us (32%)
  Pallas kernels  125 us (31%)
  starting transfers between devices  47.3 us (12%)
  other arithmetic  44.7 us (11%)
  between operations  16.3 us (4%)
  matrix products  15.1 us (4%)
  local copies, waits for them, and re-layouts  13.9 us (4%)
    ppermute x29, waiting for transfers between devices, local(): came[kind, k] = lax.ppermute(stack, 'tm', routes[kind])  127 us
    pallas_call x5, Pallas kernels, attn_call(): pl.pallas_call(functools.partial(attn_kernel, scale, rows, sub), grid_spe...  108 us
    ppermute x29, starting transfers between devices, local(): came[kind, k] = lax.ppermute(stack, 'tm', routes[kind])  46.8 us
    another operation x41, other arithmetic, local(): stacks[kind] = jnp.stack(list(parts.values()))  29.6 us
    pallas_call x5, Pallas kernels, join_call(): pl.pallas_call(join_kernel, grid_spec=pltpu.PrefetchScalarGridSpec(num_sc...  17.2 us
    dot_general x1, matrix products, local(): lax.dot_general(after(gathered, *ready), out_weight, (((1,), (1,)), ((),...  15.1 us
    unnamed x126, local copies, waits for them, and re-layouts  8.17 us
  transfers between devices with their start and end apart: 31, of which 16 were waited for; matrix products, arithmetic and copies ran while one was open for 15% of the time, Pallas kernels for 31%

profile of v4, /device:TPU:0, one launch (start us, length us, event | category | flops | bytes accessed | tf_op | source)
XLA Modules:
  0.0 390.2 jit_solution(16097439299662990305)
XLA Ops:
  13.9 2.9 collective-permute-start.2
  18.6 17.2 %collective-permute-done.2.rest_1_.rest_3_ = bf16[2,2,784,128]{3,2,1,0:T(8,128)(2,1)S(1)} collective-permute-done((bf16[2,2,784,128]{3,2,1,0:T(8,128)(2,1)}, bf16[2,2,784,128]{3,2,1,0:T(8,128)(2,1)S(1)}, u32[]{:S(2)}, u32[]{:S(2)}) %collective-permute-start.2) | collective-permute-done | bytes 802848 | tf_op jit(solution)/shard_map/ppermute | solution.py:406
  43.2 9.8 %collective-permute-done.1.rest_1_.rest_3_ = bf16[2,2,784,128]{3,2,1,0:T(8,128)(2,1)S(1)} collective-permute-done((bf16[2,2,784,128]{3,2,1,0:T(8,128)(2,1)}, bf16[2,2,784,128]{3,2,1,0:T(8,128)(2,1)S(1)}, u32[]{:S(2)}, u32[]{:S(2)}) %collective-permute-start.1) | collective-permute-done | bytes 802848 | tf_op jit(solution)/shard_map/ppermute | solution.py:406
  53.0 2.2 broadcast_select_fusion.8
  58.4 10.9 %collective-permute-done.rest_1_.rest_3_ = bf16[2,2,784,128]{3,2,1,0:T(8,128)(2,1)S(1)} collective-permute-done((bf16[2,2,784,128]{3,2,1,0:T(8,128)(2,1)}, bf16[2,2,784,128]{3,2,1,0:T(8,128)(2,1)S(1)}, u32[]{:S(2)}, u32[]{:S(2)}) %collective-permute-start) | collective-permute-done | bytes 802848 | tf_op jit(solution)/shard_map/ppermute | solution.py:406
  79.5 13.0 %collective-permute-done.5.rest_0_ = bf16[2,2,784,128]{3,2,1,0:T(8,128)(2,1)S(1)} collective-permute-done((bf16[2,2,784,128]{3,2,1,0:T(8,128)(2,1)}, bf16[2,2,784,128]{3,2,1,0:T(8,128)(2,1)S(1)}, u32[]{:S(2)}, u32[]{:S(2)}) %collective-permute-start.5) | collective-permute-done | bytes 802848 | tf_op jit(solution)/shard_map/ppermute | solution.py:406
  101.4 15.1 %convolution_convert_fusion.g_ref = bf16[784,1280]{1,0:T(8,128)(2,1)S(1)} fusion(bf16[784,5120]{1,0:T(8,128)(2,1)} %all-gather.2.cloned.1.call-done, bf16[1280,5120]{1,0:T(8,128)(2,1)} %param.11), kind=kOutput, calls=%fused_computation | convolution fusion | flops 10277048320 | bytes 23142400 | tf_op jit(solution)/shard_map/dot_general | solution.py:412
  122.4 7.5 %collective-permute-done.9.far_ref.rest_2_ = bf16[2,2,784,128]{3,2,1,0:T(8,128)(2,1)} collective-permute-done((bf16[2,2,784,128]{3,2,1,0:T(8,128)(2,1)}, bf16[2,2,784,128]{3,2,1,0:T(8,128)(2,1)}, u32[]{:S(2)}, u32[]{:S(2)}) %collective-permute-start.9) | collective-permute-done | bytes 802848 | tf_op jit(solution)/shard_map/ppermute | solution.py:406
  129.9 21.9 %shard_map.94 = (bf16[784,1280]{1,0:T(8,128)(2,1)}, bf16[784,1280]{1,0:T(8,128)(2,1)}, bf16[784,1280]{1,0:T(8,128)(2,1)}, bf16[2,2,784,128]{3,2,1,0:T(8,128)(2,1)S(1)}, bf16[2,2,784,128]{3,2,1,0:T(8,128)(2,1)S(1)}) custom-call(s32[4]{0:T(128)S(1)} %pad_add_fusion.flags_ref, bf16[784,1280]{1,0:T(8,128)(2,1)S(1)} %copy-done.9, ...), custom_call_target="tpu_custom_call" | custom-call | flops 9441116160 | bytes 6021120 | tf_op jit(solution)/shard_map/pallas_call | solution.py:174
  156.8 21.5 %shard_map.95 = (bf16[784,1280]{1,0:T(8,128)(2,1)}, bf16[784,1280]{1,0:T(8,128)(2,1)}, bf16[784,1280]{1,0:T(8,128)(2,1)}, bf16[2,2,784,128]{3,2,1,0:T(8,128)(2,1)S(1)}, bf16[2,2,784,128]{3,2,1,0:T(8,128)(2,1)S(1)}) custom-call(s32[4]{0:T(128)S(1)} %pad_add_fusion.flags_ref, ...), custom_call_target="tpu_custom_call", output_to_operand_aliasing={{0}: (11, {}), {1}: (12, {}), {2}: (13, {})} | custom-call | flops 9441116160 | bytes 6021120 | tf_op jit(solution)/shard_map/pallas_call | solution.py:174
  181.6 2.4 collective-permute-start.16
  184.6 21.5 %shard_map.96 = (bf16[784,1280]{1,0:T(8,128)(2,1)}, bf16[784,1280]{1,0:T(8,128)(2,1)}, bf16[784,1280]{1,0:T(8,128)(2,1)}, bf16[2,2,784,128]{3,2,1,0:T(8,128)(2,1)S(1)}, bf16[2,2,784,128]{3,2,1,0:T(8,128)(2,1)S(1)}) custom-call(s32[4]{0:T(128)S(1)} %pad_add_fusion.flags_ref, ...), custom_call_target="tpu_custom_call", output_to_operand_aliasing={{0}: (11, {}), {1}: (12, {}), {2}: (13, {})} | custom-call | flops 9441116160 | bytes 6021120 | tf_op jit(solution)/shard_map/pallas_call | solution.py:174
  207.0 6.4 %collective-permute-done.16.rest_2_ = bf16[2,2,784,128]{3,2,1,0:T(8,128)(2,1)S(1)} collective-permute-done((bf16[2,2,784,128]{3,2,1,0:T(8,128)(2,1)S(1)}, bf16[2,2,784,128]{3,2,1,0:T(8,128)(2,1)S(1)}, u32[]{:S(2)}, u32[]{:S(2)}) %collective-permute-start.16) | collective-permute-done | bytes 802848 | tf_op jit(solution)/shard_map/ppermute | solution.py:406
  217.7 21.5 %shard_map.97 = (bf16[784,1280]{1,0:T(8,128)(2,1)}, bf16[784,1280]{1,0:T(8,128)(2,1)}, bf16[784,1280]{1,0:T(8,128)(2,1)}, bf16[2,2,784,128]{3,2,1,0:T(8,128)(2,1)S(1)}, bf16[2,2,784,128]{3,2,1,0:T(8,128)(2,1)S(1)}) custom-call(s32[4]{0:T(128)S(1)} %pad_add_fusion.flags_ref, ...), custom_call_target="tpu_custom_call", output_to_operand_aliasing={{0}: (11, {}), {1}: (12, {}), {2}: (13, {})} | custom-call | flops 9441116160 | bytes 6021120 | tf_op jit(solution)/shard_map/pallas_call | solution.py:174
  239.3 2.6 collective-permute-done.17.far_ref.rest_2_
  244.8 21.8 %shard_map.98 = (bf16[784,1280]{1,0:T(8,128)(2,1)}, bf16[784,1280]{1,0:T(8,128)(2,1)}, bf16[784,1280]{1,0:T(8,128)(2,1)}, bf16[2,2,784,128]{3,2,1,0:T(8,128)(2,1)S(1)}, bf16[2,2,784,128]{3,2,1,0:T(8,128)(2,1)S(1)}) custom-call(s32[4]{0:T(128)S(1)} %pad_add_fusion.flags_ref, ...), custom_call_target="tpu_custom_call", output_to_operand_aliasing={{0}: (11, {}), {1}: (12, {}), {2}: (13, {})} | custom-call | flops 9441116160 | bytes 6021120 | tf_op jit(solution)/shard_map/pallas_call | solution.py:174
  271.2 2.5 collective-permute-start.22
  273.7 22.5 %collective-permute-done.21.rest_0_.rest_1_ = bf16[3,2,784,128]{3,2,1,0:T(8,128)(2,1)} collective-permute-done((bf16[3,2,784,128]{3,2,1,0:T(8,128)(2,1)}, bf16[3,2,784,128]{3,2,1,0:T(8,128)(2,1)}, u32[]{:S(2)}, u32[]{:S(2)}) %collective-permute-start.21) | collective-permute-done | bytes 1204256 | tf_op jit(solution)/shard_map/ppermute | solution.py:406
  298.6 2.4 fusion.59
  302.0 3.9 collective-permute-start.24
  309.8 11.0 %collective-permute-done.24.rest_2_ = bf16[2,2,784,128]{3,2,1,0:T(8,128)(2,1)} collective-permute-done((bf16[2,2,784,128]{3,2,1,0:T(8,128)(2,1)}, bf16[2,2,784,128]{3,2,1,0:T(8,128)(2,1)}, u32[]{:S(2)}, u32[]{:S(2)}) %collective-permute-start.24) | collective-permute-done | bytes 802848 | tf_op jit(solution)/shard_map/ppermute | solution.py:406
  322.9 4.3 %collective-permute-start.26 = (bf16[1,2,784,128]{3,2,1,0:T(8,128)(2,1)S(1)}, bf16[1,2,784,128]{3,2,1,0:T(8,128)(2,1)S(1)}, u32[]{:S(2)}, u32[]{:S(2)}) collective-permute-start(bf16[1,2,784,128]{3,2,1,0:T(8,128)(2,1)S(1)} %get-tuple-element.165), channel_id=1, source_target_pairs={{8,0},{12,4},{16,8},{20,12},{24,16},{28,20},{0,24},{4,28},{9,1},{1... | collective-permute-start | bytes 1204232 | tf_op jit(solution)/shard_map/ppermute | solution.py:406
  328.6 4.0 %collective-permute-done.26 = bf16[1,2,784,128]{3,2,1,0:T(8,128)(2,1)S(1)} collective-permute-done((bf16[1,2,784,128]{3,2,1,0:T(8,128)(2,1)S(1)}, bf16[1,2,784,128]{3,2,1,0:T(8,128)(2,1)S(1)}, u32[]{:S(2)}, u32[]{:S(2)}) %collective-permute-start.26) | collective-permute-done | bytes 401440 | tf_op jit(solution)/shard_map/ppermute | solution.py:406
  333.7 4.3 %collective-permute-start.28 = (bf16[1,2,784,128]{3,2,1,0:T(8,128)(2,1)S(1)}, bf16[1,2,784,128]{3,2,1,0:T(8,128)(2,1)S(1)}, u32[]{:S(2)}, u32[]{:S(2)}) collective-permute-start(bf16[1,2,784,128]{3,2,1,0:T(8,128)(2,1)S(1)} %get-tuple-element.187), channel_id=1, source_target_pairs={{8,0},{12,4},{16,8},{20,12},{24,16},{28,20},{0,24},{4,28},{9,1},{1... | collective-permute-start | bytes 1204232 | tf_op jit(solution)/shard_map/ppermute | solution.py:406
  340.2 3.2 collective-permute-done.28
  346.6 3.4 shard_map.99
  350.0 3.4 shard_map.100
  354.4 3.4 shard_map.101
  357.8 8.8 %collective-permute-done.27.rest_0_.rest_1_ = bf16[2,2,784,128]{3,2,1,0:T(8,128)(2,1)S(1)} collective-permute-done((bf16[2,2,784,128]{3,2,1,0:T(8,128)(2,1)}, bf16[2,2,784,128]{3,2,1,0:T(8,128)(2,1)S(1)}, u32[]{:S(2)}, u32[]{:S(2)}) %collective-permute-start.27) | collective-permute-done | bytes 802848 | tf_op jit(solution)/shard_map/ppermute | solution.py:406
  367.6 3.4 shard_map.102
  371.0 7.8 %collective-permute-done.29.rest_0_.rest_1_ = bf16[2,2,784,128]{3,2,1,0:T(8,128)(2,1)S(1)} collective-permute-done((bf16[2,2,784,128]{3,2,1,0:T(8,128)(2,1)}, bf16[2,2,784,128]{3,2,1,0:T(8,128)(2,1)S(1)}, u32[]{:S(2)}, u32[]{:S(2)}) %collective-permute-start.29) | collective-permute-done | bytes 802848 | tf_op jit(solution)/shard_map/ppermute | solution.py:406
  379.8 3.4 shard_map.103
  (242 shorter events, 83.9 us)
Async XLA Ops:
  7.2 94.2 %all-gather.2.cloned.1.call-start = ((), (), s32[]{:S(2)}) async-start(), calls=%async_computation | async-start | bytes 10035200 | tf_op jit(solution)/shard_map/all_gather | solution.py:288
  13.9 21.9 %collective-permute-start.2 = (bf16[2,2,784,128]{3,2,1,0:T(8,128)(2,1)}, bf16[2,2,784,128]{3,2,1,0:T(8,128)(2,1)S(1)}, u32[]{:S(2)}, u32[]{:S(2)}) collective-permute-start(bf16[2,2,784,128]{3,2,1,0:T(8,128)(2,1)} %pad_maximum_fusion.6), channel_id=1, source_target_pairs={{0,4},{4,0},{8,12},{12,8},{16,20},{20,16},{24,28},{28,24},{1,5},{5... | collective-permute-start | bytes 2408456 | tf_op jit(solution)/shard_map/ppermute | solution.py:406
  17.9 35.1 %collective-permute-start.1 = (bf16[2,2,784,128]{3,2,1,0:T(8,128)(2,1)}, bf16[2,2,784,128]{3,2,1,0:T(8,128)(2,1)S(1)}, u32[]{:S(2)}, u32[]{:S(2)}) collective-permute-start(bf16[2,2,784,128]{3,2,1,0:T(8,128)(2,1)} %pad_maximum_fusion.5), channel_id=1, source_target_pairs={{0,4},{4,0},{8,12},{12,8},{16,20},{20,16},{24,28},{28,24},{1,5},{5... | collective-permute-start | bytes 2408456 | tf_op jit(solution)/shard_map/ppermute | solution.py:406
  37.2 15.8 %collective-permute-start.3 = (bf16[1,2,784,128]{3,2,1,0:T(8,128)(2,1)S(1)}, bf16[1,2,784,128]{3,2,1,0:T(8,128)(2,1)S(1)}, u32[]{:S(2)}, u32[]{:S(2)}) collective-permute-start(bf16[1,2,784,128]{3,2,1,0:T(8,128)(2,1)S(1)} %get-tuple-element.182), channel_id=1, source_target_pairs={{0,8},{4,12},{8,16},{12,20},{16,24},{20,28},{24,0},{28,4},{1,9},{5... | collective-permute-start | bytes 1204232 | tf_op jit(solution)/shard_map/ppermute | solution.py:406
  41.7 27.7 %collective-permute-start = (bf16[2,2,784,128]{3,2,1,0:T(8,128)(2,1)}, bf16[2,2,784,128]{3,2,1,0:T(8,128)(2,1)S(1)}, u32[]{:S(2)}, u32[]{:S(2)}) collective-permute-start(bf16[2,2,784,128]{3,2,1,0:T(8,128)(2,1)} %pad_maximum_fusion.4), channel_id=1, source_target_pairs={{0,4},{4,0},{8,12},{12,8},{16,20},{20,16},{24,28},{28,24},{1,5},{5... | collective-permute-start | bytes 2408456 | tf_op jit(solution)/shard_map/ppermute | solution.py:406
  55.2 14.1 %collective-permute-start.4 = (bf16[1,2,784,128]{3,2,1,0:T(8,128)(2,1)S(1)}, bf16[1,2,784,128]{3,2,1,0:T(8,128)(2,1)S(1)}, u32[]{:S(2)}, u32[]{:S(2)}) collective-permute-start(bf16[1,2,784,128]{3,2,1,0:T(8,128)(2,1)S(1)} %get-tuple-element.180), channel_id=1, source_target_pairs={{0,8},{4,12},{8,16},{12,20},{16,24},{20,28},{24,0},{28,4},{1,9},{5... | collective-permute-start | bytes 1204232 | tf_op jit(solution)/shard_map/ppermute | solution.py:406
  71.4 21.1 %collective-permute-start.5 = (bf16[2,2,784,128]{3,2,1,0:T(8,128)(2,1)}, bf16[2,2,784,128]{3,2,1,0:T(8,128)(2,1)S(1)}, u32[]{:S(2)}, u32[]{:S(2)}) collective-permute-start(bf16[2,2,784,128]{3,2,1,0:T(8,128)(2,1)} %pad_maximum_fusion.7), channel_id=1, source_target_pairs={{0,8},{4,12},{8,16},{12,20},{16,24},{20,28},{24,0},{28,4},{1,9},{5... | collective-permute-start | bytes 2408456 | tf_op jit(solution)/shard_map/ppermute | solution.py:406
  74.3 21.0 %collective-permute-start.6 = (bf16[2,2,784,128]{3,2,1,0:T(8,128)(2,1)}, bf16[2,2,784,128]{3,2,1,0:T(8,128)(2,1)S(1)}, u32[]{:S(2)}, u32[]{:S(2)}) collective-permute-start(bf16[2,2,784,128]{3,2,1,0:T(8,128)(2,1)} %pad_maximum_fusion.9), channel_id=1, source_target_pairs={{0,4},{4,0},{8,12},{12,8},{16,20},{20,16},{24,28},{28,24},{1,5},{5... | collective-permute-start | bytes 2408456 | tf_op jit(solution)/shard_map/ppermute | solution.py:406
  76.9 39.9 %collective-permute-start.8 = (bf16[2,2,784,128]{3,2,1,0:T(8,128)(2,1)}, bf16[2,2,784,128]{3,2,1,0:T(8,128)(2,1)}, u32[]{:S(2)}, u32[]{:S(2)}) collective-permute-start(bf16[2,2,784,128]{3,2,1,0:T(8,128)(2,1)} %pad_maximum_fusion.12), channel_id=1, source_target_pairs={{0,4},{4,0},{8,12},{12,8},{16,20},{20,16},{24,28},{28,24},{1,5},{5... | collective-permute-start | bytes 2408456 | tf_op jit(solution)/shard_map/ppermute | solution.py:399
  79.5 165.3 %copy-start.8 = (s32[4]{0:T(128)}, s32[4]{0:T(128)S(1)}, u32[]{:S(2)}) copy-start(s32[4]{0:T(128)S(1)} %pad_add_fusion.flags_ref) | copy-start | bytes 52
  98.3 18.4 %collective-permute-start.7 = (bf16[2,2,784,128]{3,2,1,0:T(8,128)(2,1)}, bf16[2,2,784,128]{3,2,1,0:T(8,128)(2,1)S(1)}, u32[]{:S(2)}, u32[]{:S(2)}) collective-permute-start(bf16[2,2,784,128]{3,2,1,0:T(8,128)(2,1)} %pad_maximum_fusion.10), channel_id=1, source_target_pairs={{0,8},{4,12},{8,16},{12,20},{16,24},{20,28},{24,0},{28,4},{1,9},{5... | collective-permute-start | bytes 2408456 | tf_op jit(solution)/shard_map/ppermute | solution.py:406
  99.9 30.0 %collective-permute-start.9 = (bf16[2,2,784,128]{3,2,1,0:T(8,128)(2,1)}, bf16[2,2,784,128]{3,2,1,0:T(8,128)(2,1)}, u32[]{:S(2)}, u32[]{:S(2)}) collective-permute-start(bf16[2,2,784,128]{3,2,1,0:T(8,128)(2,1)} %pad_maximum_fusion.8.near_ref), channel_id=1, source_target_pairs={{0,4},{4,0},{8,12},{12,8},{16,20},{20,16},{24,28},{28,24},{1,5},{5... | collective-permute-start | bytes 2408456 | tf_op jit(solution)/shard_map/ppermute | solution.py:406
  119.9 32.0 %collective-permute-start.10 = (bf16[2,2,784,128]{3,2,1,0:T(8,128)(2,1)S(1)}, bf16[2,2,784,128]{3,2,1,0:T(8,128)(2,1)S(1)}, u32[]{:S(2)}, u32[]{:S(2)}) collective-permute-start(bf16[2,2,784,128]{3,2,1,0:T(8,128)(2,1)S(1)} %pad_maximum_fusion.13), channel_id=1, source_target_pairs={{0,8},{4,12},{8,16},{12,20},{16,24},{20,28},{24,0},{28,4},{1,9},{5... | collective-permute-start | bytes 2408456 | tf_op jit(solution)/shard_map/ppermute | solution.py:406
  121.9 34.9 %collective-permute-start.11 = (bf16[2,2,784,128]{3,2,1,0:T(8,128)(2,1)S(1)}, bf16[2,2,784,128]{3,2,1,0:T(8,128)(2,1)S(1)}, u32[]{:S(2)}, u32[]{:S(2)}) collective-permute-start(bf16[2,2,784,128]{3,2,1,0:T(8,128)(2,1)S(1)} %pad_maximum_fusion.11.near_ref), channel_id=1, source_target_pairs={{0,4},{4,0},{8,12},{12,8},{16,20},{20,16},{24,28},{28,24},{1,5},{5... | collective-permute-start | bytes 2408456 | tf_op jit(solution)/shard_map/ppermute | solution.py:406
  153.1 25.2 %collective-permute-start.12 = (bf16[2,2,784,128]{3,2,1,0:T(8,128)(2,1)S(1)}, bf16[2,2,784,128]{3,2,1,0:T(8,128)(2,1)S(1)}, u32[]{:S(2)}, u32[]{:S(2)}) collective-permute-start(bf16[2,2,784,128]{3,2,1,0:T(8,128)(2,1)S(1)} %pad_maximum_fusion.14), channel_id=1, source_target_pairs={{0,8},{4,12},{8,16},{12,20},{16,24},{20,28},{24,0},{28,4},{1,9},{5... | collective-permute-start | bytes 2408456 | tf_op jit(solution)/shard_map/ppermute | solution.py:406
  155.3 24.4 %collective-permute-start.13 = (bf16[3,2,784,128]{3,2,1,0:T(8,128)(2,1)S(1)}, bf16[3,2,784,128]{3,2,1,0:T(8,128)(2,1)S(1)}, u32[]{:S(2)}, u32[]{:S(2)}) collective-permute-start(bf16[3,2,784,128]{3,2,1,0:T(8,128)(2,1)S(1)} %pad_maximum_fusion.near_ref), channel_id=1, source_target_pairs={{0,4},{4,0},{8,12},{12,8},{16,20},{20,16},{24,28},{28,24},{1,5},{5... | collective-permute-start | bytes 3612680 | tf_op jit(solution)/shard_map/ppermute | solution.py:406
  180.0 26.1 %collective-permute-start.14 = (bf16[2,2,784,128]{3,2,1,0:T(8,128)(2,1)S(1)}, bf16[2,2,784,128]{3,2,1,0:T(8,128)(2,1)S(1)}, u32[]{:S(2)}, u32[]{:S(2)}) collective-permute-start(bf16[2,2,784,128]{3,2,1,0:T(8,128)(2,1)S(1)} %pad_maximum_fusion.15), channel_id=1, source_target_pairs={{0,8},{4,12},{8,16},{12,20},{16,24},{20,28},{24,0},{28,4},{1,9},{5... | collective-permute-start | bytes 2408456 | tf_op jit(solution)/shard_map/ppermute | solution.py:406
  181.6 31.7 %collective-permute-start.16 = (bf16[2,2,784,128]{3,2,1,0:T(8,128)(2,1)S(1)}, bf16[2,2,784,128]{3,2,1,0:T(8,128)(2,1)S(1)}, u32[]{:S(2)}, u32[]{:S(2)}) collective-permute-start(bf16[2,2,784,128]{3,2,1,0:T(8,128)(2,1)S(1)} %pad_maximum_fusion.16), channel_id=1, source_target_pairs={{8,0},{12,4},{16,8},{20,12},{24,16},{28,20},{0,24},{4,28},{9,1},{1... | collective-permute-start | bytes 2408456 | tf_op jit(solution)/shard_map/ppermute | solution.py:406
  184.1 22.7 %collective-permute-start.15 = (bf16[3,2,784,128]{3,2,1,0:T(8,128)(2,1)S(1)}, bf16[3,2,784,128]{3,2,1,0:T(8,128)(2,1)S(1)}, u32[]{:S(2)}, u32[]{:S(2)}) collective-permute-start(bf16[3,2,784,128]{3,2,1,0:T(8,128)(2,1)S(1)} %pad_maximum_fusion.1.near_ref), channel_id=1, source_target_pairs={{0,4},{4,0},{8,12},{12,8},{16,20},{20,16},{24,28},{28,24},{1,5},{5... | collective-permute-start | bytes 3612680 | tf_op jit(solution)/shard_map/ppermute | solution.py:406
  213.7 28.5 %collective-permute-start.18 = (bf16[2,2,784,128]{3,2,1,0:T(8,128)(2,1)S(1)}, bf16[2,2,784,128]{3,2,1,0:T(8,128)(2,1)S(1)}, u32[]{:S(2)}, u32[]{:S(2)}) collective-permute-start(bf16[2,2,784,128]{3,2,1,0:T(8,128)(2,1)S(1)} %pad_maximum_fusion.17), channel_id=1, source_target_pairs={{8,0},{12,4},{16,8},{20,12},{24,16},{28,20},{0,24},{4,28},{9,1},{1... | collective-permute-start | bytes 2408456 | tf_op jit(solution)/shard_map/ppermute | solution.py:406
  215.9 26.1 %collective-permute-start.17 = (bf16[3,2,784,128]{3,2,1,0:T(8,128)(2,1)S(1)}, bf16[3,2,784,128]{3,2,1,0:T(8,128)(2,1)S(1)}, u32[]{:S(2)}, u32[]{:S(2)}) collective-permute-start(bf16[3,2,784,128]{3,2,1,0:T(8,128)(2,1)S(1)} %pad_maximum_fusion.2.near_ref), channel_id=1, source_target_pairs={{0,4},{4,0},{8,12},{12,8},{16,20},{20,16},{24,28},{28,24},{1,5},{5... | collective-permute-start | bytes 3612680 | tf_op jit(solution)/shard_map/ppermute | solution.py:406
  242.6 24.3 %collective-permute-start.19 = (bf16[2,2,784,128]{3,2,1,0:T(8,128)(2,1)S(1)}, bf16[2,2,784,128]{3,2,1,0:T(8,128)(2,1)S(1)}, u32[]{:S(2)}, u32[]{:S(2)}) collective-permute-start(bf16[2,2,784,128]{3,2,1,0:T(8,128)(2,1)S(1)} %pad_maximum_fusion.19), channel_id=1, source_target_pairs={{8,0},{12,4},{16,8},{20,12},{24,16},{28,20},{0,24},{4,28},{9,1},{1... | collective-permute-start | bytes 2408456 | tf_op jit(solution)/shard_map/ppermute | solution.py:406
  243.4 23.2 %collective-permute-start.20 = (bf16[2,2,784,128]{3,2,1,0:T(8,128)(2,1)S(1)}, bf16[2,2,784,128]{3,2,1,0:T(8,128)(2,1)S(1)}, u32[]{:S(2)}, u32[]{:S(2)}) collective-permute-start(bf16[2,2,784,128]{3,2,1,0:T(8,128)(2,1)S(1)} %pad_maximum_fusion.18), channel_id=1, source_target_pairs={{0,4},{4,0},{8,12},{12,8},{16,20},{20,16},{24,28},{28,24},{1,5},{5... | collective-permute-start | bytes 2408456 | tf_op jit(solution)/shard_map/ppermute | solution.py:406
  270.6 25.6 %collective-permute-start.21 = (bf16[3,2,784,128]{3,2,1,0:T(8,128)(2,1)}, bf16[3,2,784,128]{3,2,1,0:T(8,128)(2,1)}, u32[]{:S(2)}, u32[]{:S(2)}) collective-permute-start(bf16[3,2,784,128]{3,2,1,0:T(8,128)(2,1)} %pad_maximum_fusion.3), channel_id=1, source_target_pairs={{0,4},{4,0},{8,12},{12,8},{16,20},{20,16},{24,28},{28,24},{1,5},{5... | collective-permute-start | bytes 3612680 | tf_op jit(solution)/shard_map/ppermute | solution.py:406
  271.2 27.3 %collective-permute-start.22 = (bf16[2,2,784,128]{3,2,1,0:T(8,128)(2,1)}, bf16[2,2,784,128]{3,2,1,0:T(8,128)(2,1)}, u32[]{:S(2)}, u32[]{:S(2)}) collective-permute-start(bf16[2,2,784,128]{3,2,1,0:T(8,128)(2,1)} %pad_maximum_fusion.20), channel_id=1, source_target_pairs={{8,0},{12,4},{16,8},{20,12},{24,16},{28,20},{0,24},{4,28},{9,1},{1... | collective-permute-start | bytes 2408456 | tf_op jit(solution)/shard_map/ppermute | solution.py:406
  302.0 18.7 %collective-permute-start.24 = (bf16[2,2,784,128]{3,2,1,0:T(8,128)(2,1)}, bf16[2,2,784,128]{3,2,1,0:T(8,128)(2,1)}, u32[]{:S(2)}, u32[]{:S(2)}) collective-permute-start(bf16[2,2,784,128]{3,2,1,0:T(8,128)(2,1)} %pad_maximum_fusion.22), channel_id=1, source_target_pairs={{8,0},{12,4},{16,8},{20,12},{24,16},{28,20},{0,24},{4,28},{9,1},{1... | collective-permute-start | bytes 2408456 | tf_op jit(solution)/shard_map/ppermute | solution.py:406
  309.5 40.6 %collective-permute-start.23 = (bf16[2,2,784,128]{3,2,1,0:T(8,128)(2,1)}, bf16[2,2,784,128]{3,2,1,0:T(8,128)(2,1)}, u32[]{:S(2)}, u32[]{:S(2)}) collective-permute-start(bf16[2,2,784,128]{3,2,1,0:T(8,128)(2,1)} %pad_maximum_fusion.21), channel_id=1, source_target_pairs={{0,4},{4,0},{8,12},{12,8},{16,20},{20,16},{24,28},{28,24},{1,5},{5... | collective-permute-start | bytes 2408456 | tf_op jit(solution)/shard_map/ppermute | solution.py:406
  322.9 9.7 %collective-permute-start.26 = (bf16[1,2,784,128]{3,2,1,0:T(8,128)(2,1)S(1)}, bf16[1,2,784,128]{3,2,1,0:T(8,128)(2,1)S(1)}, u32[]{:S(2)}, u32[]{:S(2)}) collective-permute-start(bf16[1,2,784,128]{3,2,1,0:T(8,128)(2,1)S(1)} %get-tuple-element.165), channel_id=1, source_target_pairs={{8,0},{12,4},{16,8},{20,12},{24,16},{28,20},{0,24},{4,28},{9,1},{1... | collective-permute-start | bytes 1204232 | tf_op jit(solution)/shard_map/ppermute | solution.py:406
  328.6 24.9 %collective-permute-start.25 = (bf16[2,2,784,128]{3,2,1,0:T(8,128)(2,1)S(1)}, bf16[2,2,784,128]{3,2,1,0:T(8,128)(2,1)S(1)}, u32[]{:S(2)}, u32[]{:S(2)}) collective-permute-start(bf16[2,2,784,128]{3,2,1,0:T(8,128)(2,1)S(1)} %pad_maximum_fusion.23), channel_id=1, source_target_pairs={{0,4},{4,0},{8,12},{12,8},{16,20},{20,16},{24,28},{28,24},{1,5},{5... | collective-permute-start | bytes 2408456 | tf_op jit(solution)/shard_map/ppermute | solution.py:406
  333.7 9.7 %collective-permute-start.28 = (bf16[1,2,784,128]{3,2,1,0:T(8,128)(2,1)S(1)}, bf16[1,2,784,128]{3,2,1,0:T(8,128)(2,1)S(1)}, u32[]{:S(2)}, u32[]{:S(2)}) collective-permute-start(bf16[1,2,784,128]{3,2,1,0:T(8,128)(2,1)S(1)} %get-tuple-element.187), channel_id=1, source_target_pairs={{8,0},{12,4},{16,8},{20,12},{24,16},{28,20},{0,24},{4,28},{9,1},{1... | collective-permute-start | bytes 1204232 | tf_op jit(solution)/shard_map/ppermute | solution.py:406
  340.2 26.5 %collective-permute-start.27 = (bf16[2,2,784,128]{3,2,1,0:T(8,128)(2,1)}, bf16[2,2,784,128]{3,2,1,0:T(8,128)(2,1)S(1)}, u32[]{:S(2)}, u32[]{:S(2)}) collective-permute-start(bf16[2,2,784,128]{3,2,1,0:T(8,128)(2,1)} %pad_maximum_fusion.24), channel_id=1, source_target_pairs={{0,4},{4,0},{8,12},{12,8},{16,20},{20,16},{24,28},{28,24},{1,5},{5... | collective-permute-start | bytes 2408456 | tf_op jit(solution)/shard_map/ppermute | solution.py:406
  346.6 32.2 %collective-permute-start.29 = (bf16[2,2,784,128]{3,2,1,0:T(8,128)(2,1)}, bf16[2,2,784,128]{3,2,1,0:T(8,128)(2,1)S(1)}, u32[]{:S(2)}, u32[]{:S(2)}) collective-permute-start(bf16[2,2,784,128]{3,2,1,0:T(8,128)(2,1)} %pad_maximum_fusion.25), channel_id=1, source_target_pairs={{0,4},{4,0},{8,12},{12,8},{16,20},{20,16},{24,28},{28,24},{1,5},{5... | collective-permute-start | bytes 2408456 | tf_op jit(solution)/shard_map/ppermute | solution.py:406
  (62 other events, 808.2 us)
Sparse Core Ops, SparseCore 0:
  9.6 58.9 all-gather.1
